TPU v7x, 32 devices: a whole 2x2x4 slice. The times are simulated.
32 devices in a mesh: dp: 2 (over core), seq: 16 (over z, y, x).
Axes of the slice: x: 2, y: 2, z: 4, core: 2. Of those that a mesh axis runs over, the one named last changes fastest.
Arguments:
- tokens: bfloat16 [2, 2, 2048, 768], P(None, 'dp', 'seq'), may hold values from -6 to 6
- cotangent: bfloat16 [2, 2, 2048, 768], P(None, 'dp', 'seq'), may hold values from -6 to 6
- segments: int32 [2, 2, 2048], P(None, 'dp', 'seq'), may hold values from 0 to 3, never falling along the last dimension, each value on 1 to 1024 neighbouring positions
- norm_gain: bfloat16 [768], P('seq'), may hold values from 0.5 to 1.5
- w_in: bfloat16 [768, 3352], P('seq'), may hold values from -0.21875 to 0.21875
- conv_weight: bfloat16 [4, 1792], P(None, 'seq'), may hold values from -3 to 3
- conv_bias: bfloat16 [1792], P('seq'), may hold values from -1.75 to 1.75
- step_bias: float32 [24], replicated, may hold values from -6 to -2
- log_rate: float32 [24], replicated, may hold values from -9 to 0
- skip_gain: float32 [24], replicated, may hold values from 0.5 to 1.5
- gate_gain: bfloat16 [1536], P('seq'), may hold values from 0.5 to 1.5
- w_out: bfloat16 [1536, 768], P('seq'), may hold values from -0.15625 to 0.15625
Outputs:
- activations: bfloat16 [2, 2, 2048, 768], P(None, 'dp', 'seq')
- grad_tokens: bfloat16 [2, 2, 2048, 768], P(None, 'dp', 'seq')
- grad_norm_gain: float32 [768], P('seq')
- grad_w_in: float32 [768, 3352], P('seq')
- grad_conv_weight: float32 [4, 1792], P(None, 'seq')
- grad_conv_bias: float32 [1792], P('seq')
- grad_step_bias: float32 [24], replicated
- grad_log_rate: float32 [24], replicated
- grad_skip_gain: float32 [24], replicated
- grad_gate_gain: float32 [1536], P('seq')
- grad_w_out: float32 [1536, 768], P('seq')
Inputs may be any that keep to these rules, and one draw needn't show every extreme that they name: `segments`: within each sequence the numbers never fall; a change of number starts a document.
All inputs are finite; a program needn't handle non-finite values.
Results may differ from a plain program's by a relative error of at most 0.0095.
Values may be sent and summed in bfloat16 or wider, within the bound.
A program may use at most 448 MiB of HBM per device.

v0:
```python
from functools import partial

import jax
import jax.numpy as jnp
from jax import lax
from jax.sharding import PartitionSpec as P

DI = 1536
H = 24
P_SIZE = 64
N = 128
KC = 4
CH = 1792


EPSILON = 1e-05
HIGHEST = lax.Precision.HIGHEST


def passed_along(array, axis, by):
    devices = lax.axis_size(axis)
    pairs = [(i, i + by) for i in range(devices) if 0 <= i + by < devices]
    return lax.ppermute(array, axis, pairs)


def prefix(array, axis, combine, identity, reverse):
    devices, place = (lax.axis_size(axis), lax.axis_index(axis))
    everything = jax.tree.map(lambda part: lax.all_gather(part, axis), array)
    start = jax.tree.map(
        lambda part, zero: jnp.broadcast_to(jnp.asarray(zero, part.dtype), part.shape),
        array,
        identity,
    )

    def lap(k, before):
        at = devices - 1 - k if reverse else k
        reached = at > place if reverse else at < place
        new = combine(before, jax.tree.map(lambda part: part[at], everything))
        return jax.tree.map(lambda a, b: jnp.where(reached, a, b), new, before)

    return lax.fori_loop(0, devices, lap, start)


def for_sending(array):
    return jax.tree.map(lambda a: a.astype(jnp.bfloat16) if a.dtype == jnp.float32 else a, array)


def rms_scale(values, gain_vec):
    return (
        values * lax.rsqrt(jnp.mean(values * values, axis=-1, keepdims=True) + EPSILON) * gain_vec
    )


def causal_conv(padded, seg_pad, seg_one, kernel, offset):
    length_t = seg_one.shape[0]
    total = jnp.zeros((length_t, padded.shape[1]), jnp.float32) + offset[None, :]
    for tap_index in range(KC):
        window = padded[tap_index : tap_index + length_t]
        same_doc = (seg_pad[tap_index : tap_index + length_t] == seg_one).astype(jnp.float32)
        total = total + kernel[tap_index][None, :] * window * same_doc[:, None]
    return total


def cumulative(step_size, rate):
    return jnp.cumsum(step_size * rate[None, :], axis=0)


def block_state(inner, b_proj, step_size, rate, seg_one, previous):
    cum_decay = cumulative(step_size, rate)
    last_seg = seg_one[-1]
    to_end = (
        jnp.where((seg_one == last_seg)[:, None], jnp.exp(cum_decay[-1][None, :] - cum_decay), 0.0)
        * step_size
    )
    state_part = jnp.einsum("uhp,un->hpn", inner * to_end[:, :, None], b_proj, precision=HIGHEST)
    through = jnp.logical_and(seg_one[0] == last_seg, seg_one[0] == previous).astype(jnp.float32)
    return (state_part, jnp.exp(cum_decay[-1]) * through)


def block_output(inner, b_proj, c_proj, step_size, rate, state_in, seg_one, previous):
    cum_decay = cumulative(step_size, rate)
    length_t = seg_one.shape[0]
    row_index = lax.broadcasted_iota(jnp.int32, (length_t, length_t), 0)
    col_index = lax.broadcasted_iota(jnp.int32, (length_t, length_t), 1)
    allowed = jnp.logical_and(row_index >= col_index, seg_one[:, None] == seg_one[None, :])[
        :, :, None
    ]
    spread = cum_decay[:, None, :] - cum_decay[None, :, :]
    decays = jnp.where(allowed, jnp.exp(jnp.where(allowed, spread, 0.0)), 0.0)
    scores = jnp.dot(c_proj, b_proj.T, precision=HIGHEST)
    weights = decays * scores[:, :, None] * step_size[None, :, :]
    local_part = jnp.einsum("tuh,uhp->thp", weights, inner, precision=HIGHEST)
    carried = (seg_one == previous).astype(jnp.float32)[:, None] * jnp.exp(cum_decay)
    return local_part + carried[:, :, None] * jnp.einsum(
        "tn,hpn->thp", c_proj, state_in, precision=HIGHEST
    )


def prepare(proj_out, tail_rows, kernel, offset, step_bias, log_rate, tail_seg, seg_one):
    length_t = proj_out.shape[0]
    padded = jnp.concatenate([tail_rows, proj_out[:, DI : DI + CH]], axis=0)
    seg_pad = jnp.concatenate([tail_seg, seg_one])
    activated = jax.nn.silu(causal_conv(padded, seg_pad, seg_one, kernel, offset))
    inner = activated[:, :DI].reshape(length_t, H, P_SIZE)
    b_proj = activated[:, DI : DI + N]
    c_proj = activated[:, DI + N :]
    step_size = jax.nn.softplus(proj_out[:, DI + CH :] + step_bias[None, :])
    rate = -jnp.exp(log_rate)
    return (inner, b_proj, c_proj, step_size, rate, proj_out[:, :DI])


def finish(
    inner,
    b_proj,
    c_proj,
    step_size,
    rate,
    gate_in,
    state_in,
    skip_gain,
    gate_gain,
    seg_one,
    previous,
):
    length_t = inner.shape[0]
    mixed = block_output(inner, b_proj, c_proj, step_size, rate, state_in, seg_one, previous)
    mixed = mixed + skip_gain[None, :, None] * inner
    gated = mixed.reshape(length_t, DI) * jax.nn.silu(gate_in)
    return rms_scale(gated, gate_gain)


def chain_link(earlier, later):
    return (earlier[0] * later[0], later[0][:, None, None] * earlier[1] + later[1])


def body(
    tokens,
    cotangent,
    segments,
    norm_gain,
    w_in,
    conv_weight,
    conv_bias,
    step_bias,
    log_rate,
    skip_gain,
    gate_gain,
    w_out,
):
    batches = tokens.shape[0]
    length_t = tokens.shape[2]
    halo_rows = KC - 1
    identity = (jnp.ones((H,), jnp.float32), jnp.zeros((H, P_SIZE, N), jnp.float32))
    totals = None
    head_totals = (
        jnp.zeros((H,), jnp.float32),
        jnp.zeros((H,), jnp.float32),
        jnp.zeros((H,), jnp.float32),
    )
    act_list = []
    grad_list = []
    for micro in range(batches):
        gathered = (
            lax.all_gather(w_in, "seq", axis=0, tiled=True),
            lax.all_gather(w_out, "seq", axis=0, tiled=True),
            lax.all_gather(conv_weight, "seq", axis=1, tiled=True),
            lax.all_gather(conv_bias, "seq", axis=0, tiled=True),
            lax.all_gather(norm_gain, "seq", axis=0, tiled=True),
            lax.all_gather(gate_gain, "seq", axis=0, tiled=True),
        )
        in_full = gathered[0]
        out_full = gathered[1]
        kernel = gathered[2].astype(jnp.float32)
        offset = gathered[3].astype(jnp.float32)
        gain_one = gathered[4].astype(jnp.float32)
        gain_two = gathered[5].astype(jnp.float32)
        resid = tokens[micro, 0].astype(jnp.float32)
        seg_one = segments[micro, 0].astype(jnp.float32) + 1.0
        normed, norm_back = jax.vjp(rms_scale, resid, gain_one)
        normed_low = normed.astype(jnp.bfloat16)
        proj_out = jnp.dot(normed_low, in_full, preferred_element_type=jnp.float32)
        tail_rows, tail_seg = passed_along(
            (proj_out[length_t - halo_rows :, DI : DI + CH], seg_one[length_t - halo_rows :]),
            "seq",
            1,
        )
        previous = tail_seg[halo_rows - 1]
        prepared, prep_back = jax.vjp(
            partial(prepare, tail_seg=tail_seg, seg_one=seg_one),
            proj_out,
            tail_rows,
            kernel,
            offset,
            step_bias,
            log_rate,
        )
        inner, b_proj, c_proj, step_size, rate, gate_in = prepared
        state_out, state_back = jax.vjp(
            partial(block_state, seg_one=seg_one, previous=previous), inner, b_proj, step_size, rate
        )
        state_part, through = state_out
        state_in = prefix((through, state_part), "seq", chain_link, identity, False)[1]
        normed_two, finish_back = jax.vjp(
            partial(finish, seg_one=seg_one, previous=previous),
            inner,
            b_proj,
            c_proj,
            step_size,
            rate,
            gate_in,
            state_in,
            skip_gain,
            gain_two,
        )
        gate_low = normed_two.astype(jnp.bfloat16)
        branch = jnp.dot(gate_low, out_full, preferred_element_type=jnp.float32)
        act_list.append((resid + branch).astype(jnp.bfloat16))
        cot_low = cotangent[micro, 0]
        again = (
            lax.all_gather(w_in, "seq", axis=0, tiled=True),
            lax.all_gather(w_out, "seq", axis=0, tiled=True),
        )
        in_back = again[0]
        out_back = again[1]
        out_term = lax.dot_general(
            gate_low, cot_low, (((0,), (0,)), ((), ())), preferred_element_type=jnp.float32
        )
        grad_gate = lax.dot_general(
            cot_low, out_back, (((1,), (1,)), ((), ())), preferred_element_type=jnp.float32
        )
        g_inner, g_bproj, g_cproj, g_step, g_rate, g_gate_in, g_state_in, g_skip, g_gain_two = (
            finish_back(grad_gate)
        )
        carried = prefix((through, g_state_in), "seq", chain_link, identity, True)[1]
        h_inner, h_bproj, h_step, h_rate = state_back(
            (carried, jnp.sum(carried * state_in, axis=(1, 2)))
        )
        g_proj, g_tail, g_kernel, g_offset, g_bias, g_log = prep_back(
            (
                g_inner + h_inner,
                g_bproj + h_bproj,
                g_cproj,
                g_step + h_step,
                g_rate + h_rate,
                g_gate_in,
            )
        )
        returned = passed_along(g_tail, "seq", -1)
        width_after = proj_out.shape[1] - DI - CH
        g_proj = g_proj + jnp.pad(returned, ((length_t - halo_rows, 0), (DI, width_after)))
        proj_grad_low = g_proj.astype(jnp.bfloat16)
        grad_normed = lax.dot_general(
            proj_grad_low, in_back, (((1,), (1,)), ((), ())), preferred_element_type=jnp.float32
        )
        grad_resid, g_gain_one = norm_back(grad_normed)
        grad_list.append((cot_low.astype(jnp.float32) + grad_resid).astype(jnp.bfloat16))
        in_shard = lax.psum_scatter(
            lax.dot_general(
                normed_low,
                proj_grad_low,
                (((0,), (0,)), ((), ())),
                preferred_element_type=jnp.float32,
            ),
            "seq",
            scatter_dimension=0,
            tiled=True,
        )
        shards = (
            lax.psum_scatter(out_term, "seq", scatter_dimension=0, tiled=True),
            lax.psum_scatter(g_kernel, "seq", scatter_dimension=1, tiled=True),
            lax.psum_scatter(g_offset, "seq", scatter_dimension=0, tiled=True),
            lax.psum_scatter(g_gain_one, "seq", scatter_dimension=0, tiled=True),
            lax.psum_scatter(g_gain_two, "seq", scatter_dimension=0, tiled=True),
        )
        this_round = (in_shard, shards[0], shards[1], shards[2], shards[3], shards[4])
        if totals is None:
            totals = this_round
        else:
            totals = tuple((prior + fresh for prior, fresh in zip(totals, this_round)))
        head_totals = (head_totals[0] + g_bias, head_totals[1] + g_log, head_totals[2] + g_skip)
    summed = jax.tree.map(
        lambda part: part.astype(jnp.float32), lax.psum(for_sending(totals), "dp")
    )
    heads = lax.psum((head_totals[0], head_totals[1], head_totals[2]), ("dp", "seq"))
    activations = jnp.stack(act_list)[:, None]
    grad_tokens = jnp.stack(grad_list)[:, None]
    return (
        activations,
        grad_tokens,
        summed[4],
        summed[0],
        summed[2],
        summed[3],
        heads[0],
        heads[1],
        heads[2],
        summed[5],
        summed[1],
    )


def solution(mesh):
    in_specs = (
        P(None, "dp", "seq", None),
        P(None, "dp", "seq", None),
        P(None, "dp", "seq"),
        P("seq"),
        P("seq", None),
        P(None, "seq"),
        P("seq"),
        P(),
        P(),
        P(),
        P("seq"),
        P("seq", None),
    )
    out_specs = (
        P(None, "dp", "seq", None),
        P(None, "dp", "seq", None),
        P("seq"),
        P("seq", None),
        P(None, "seq"),
        P("seq"),
        P(),
        P(),
        P(),
        P("seq"),
        P("seq", None),
    )
    return jax.shard_map(body, mesh=mesh, in_specs=in_specs, out_specs=out_specs, check_vma=False)
```

profile of v0, /device:TPU:0, one launch (start us, length us, event | category | flops | bytes accessed | tf_op | source)
XLA Modules:
  0.0 1254.8 jit_solution(2993631277636970178)
XLA Ops:
  9.5 4.8 collective-permute-start.3
  23.6 74.6 %all-reduce.42 = (bf16[768]{0:T(1024)(128)(2,1)S(1)}, bf16[1792]{0:T(1024)(128)(2,1)S(1)}, bf16[1536]{0:T(1024)(128)(2,1)}) all-reduce(bf16[768]{0:T(1024)(128)(2,1)S(1)} %dynamic-update-slice.1, bf16[1792]{0:T(1024)(128)(2,1)S(1)} %dynamic-update-slice, bf16[1536]{0:T(1024)(128)(2,1)S(1)} %dynamic-update-slice.2), channel_id=1, replica_groups=mesh['dp'=2,'seq'=16] {'seq'}, use_global_device_ids=true, to_apply=%add.35 | all-reduce | flops 4096 | bytes 16384
  98.3 35.8 %all-gather.4 = bf16[16,112,4]{1,2,0:T(4,128)(2,1)S(1)} all-gather(bf16[1,112,4]{1,2,0:T(4,128)(2,1)} %bitcast.327), channel_id=1, replica_groups=mesh['dp'=2,'seq'=16] {'seq'}, dimensions={0}, use_global_device_ids=true | all-gather | bytes 15232 | tf_op jit(solution)/shard_map/all_gather | solution.py:166
  141.5 3.8 compare_convert_fusion.5
  145.3 5.1 fusion.196
  155.9 3.8 collective-permute-start
  162.6 5.6 fusion.73
  175.6 4.2 collective-permute-start.2
  183.6 5.4 fusion.72
  199.2 37.8 %all-gather.5 = f32[16,1,24]{2,1,0:T(1,128)S(1)} all-gather(f32[1,1,24]{2,1,0:T(1,128)} %bitcast.325), channel_id=1, replica_groups=mesh['dp'=2,'seq'=16] {'seq'}, dimensions={0}, use_global_device_ids=true | all-gather | bytes 1632 | tf_op jit(solution)/shard_map/all_gather | solution.py:28
  237.0 35.9 %all-gather.6 = f32[16,1,24]{2,1,0:T(1,128)S(1)} all-gather(f32[1,1,24]{2,1,0:T(1,128)} %bitcast.326), channel_id=1, replica_groups=mesh['dp'=2,'seq'=16] {'seq'}, dimensions={0}, use_global_device_ids=true | all-gather | bytes 1632 | tf_op jit(solution)/shard_map/all_gather | solution.py:28
  276.5 45.2 %all-gather.18.cloned.1.call-done = f32[384,64,128]{2,1,0:T(8,128)} async-done(((f32[24,64,128]{2,1,0:T(8,128)}), f32[384,64,128]{2,1,0:T(8,128)}) %all-gather.18.cloned.1.call-update) | async-done | bytes 12582928 | tf_op jit(solution)/shard_map/all_gather | solution.py:28
  321.7 21.7 %while.60 = (s32[]{:T(128)}, f32[24,64,128]{2,1,0:T(8,128)S(1)}, s32[]{:T(128)}, f32[16,24]{1,0:T(8,128)S(1)}, f32[16,24,64,128]{3,2,1,0:T(8,128)}, /*index=5*/s32[]{:T(128)}, s32[]{:T(128)}) while((s32[]{:T(128)}, f32[24,64,128]{2,1,0:T(8,128)S(1)}, s32[]{:T(128)}, f32[16,24]{1,0:T(8,128)S(1)}, f32[16,24,64,128]{3,2,1,0:T(8,128)}, ...), condition=%wide.region_3.5_spmd.clone, body=%wide.region_2.4_spmd.clone.sunk | while | flops 786436 | bytes 2359697 | solution.py:41
  345.1 5.0 fusion.44
  351.3 123.3 %all-gather.20.cloned.1.call-done = f32[384,64,128]{2,1,0:T(8,128)} async-done(((f32[24,64,128]{2,1,0:T(8,128)}), f32[384,64,128]{2,1,0:T(8,128)}) %all-gather.20.cloned.1.call-update) | async-done | bytes 12582928 | tf_op jit(solution)/shard_map/all_gather | solution.py:28
  474.6 21.5 %while.61 = (s32[]{:T(128)}, f32[24,64,128]{2,1,0:T(8,128)S(1)}, s32[]{:T(128)}, f32[16,24]{1,0:T(8,128)S(1)}, f32[16,24,64,128]{3,2,1,0:T(8,128)}, /*index=5*/s32[]{:T(128)}, s32[]{:T(128)}) while((s32[]{:T(128)}, f32[24,64,128]{2,1,0:T(8,128)S(1)}, s32[]{:T(128)}, f32[16,24]{1,0:T(8,128)S(1)}, f32[16,24,64,128]{3,2,1,0:T(8,128)}, ...), condition=%wide.region_8.10_spmd.clone, body=%wide.region_7.9_spmd.clone.sunk | while | flops 786436 | bytes 2359697 | solution.py:41
  498.7 4.9 fusion.50
  519.6 5.8 fusion.75
  531.9 5.7 fusion.77
  557.4 106.2 %all-gather.24.cloned.1.call-done = f32[384,64,128]{2,1,0:T(8,128)} async-done(((f32[24,64,128]{2,1,0:T(8,128)}), f32[384,64,128]{2,1,0:T(8,128)}) %all-gather.24.cloned.1.call-update) | async-done | bytes 12582928 | tf_op jit(solution)/shard_map/all_gather | solution.py:28
  663.6 32.3 %while.63 = (s32[]{:T(128)}, f32[24,64,128]{2,1,0:T(8,128)S(1)}, s32[]{:T(128)}, f32[16,24]{1,0:T(8,128)}, f32[16,24,64,128]{3,2,1,0:T(8,128)}, /*index=5*/s32[]{:T(128)}, s32[]{:T(128)}, s32[]{:T(128)}, s32[]{:T(128)}) while((s32[]{:T(128)}, f32[24,64,128]{2,1,0:T(8,128)S(1)}, s32[]{:T(128)}, f32[16,24]{1,0:T(8,128)}, ...), condition=%wide.region_31.33_spmd.clone, body=%wide.region_30.32_spmd.clone.sunk | while | flops 786440 | bytes 2359759 | solution.py:41
  696.0 120.5 %all-gather.22.cloned.1.call-done = f32[384,64,128]{2,1,0:T(8,128)} async-done(((f32[24,64,128]{2,1,0:T(8,128)}), f32[384,64,128]{2,1,0:T(8,128)}) %all-gather.22.cloned.1.call-update) | async-done | bytes 12582928 | tf_op jit(solution)/shard_map/all_gather | solution.py:28
  816.5 32.4 %while.62 = (s32[]{:T(128)}, f32[24,64,128]{2,1,0:T(8,128)S(1)}, s32[]{:T(128)}, f32[16,24]{1,0:T(8,128)}, f32[16,24,64,128]{3,2,1,0:T(8,128)}, /*index=5*/s32[]{:T(128)}, s32[]{:T(128)}, s32[]{:T(128)}, s32[]{:T(128)}) while((s32[]{:T(128)}, f32[24,64,128]{2,1,0:T(8,128)S(1)}, s32[]{:T(128)}, f32[16,24]{1,0:T(8,128)}, ...), condition=%wide.region_17.19_spmd.clone, body=%wide.region_16.18_spmd.clone.sunk | while | flops 786440 | bytes 2359759 | solution.py:41
  868.1 3.7 fusion.220
  907.7 5.8 convolution_add_fusion
  926.9 30.5 %reduce-scatter.8.cloned.1.call-done = f32[96,768]{1,0:T(8,128)} async-done(((f32[1536,768]{1,0:T(8,128)}), f32[96,768]{1,0:T(8,128)}) %reduce-scatter.8.cloned.1.call-update) | async-done | bytes 294928 | tf_op jit(solution)/shard_map/reduce_scatter | solution.py:269
  960.7 41.8 %all-reduce.40 = (f32[24]{0:T(128)}, f32[24]{0:T(128)}, f32[24]{0:T(128)}) all-reduce(f32[24]{0:T(128)S(1)} %add.524, f32[24]{0:T(128)S(1)} %add_multiply_fusion, f32[24]{0:T(128)S(1)} %copy-done.153), channel_id=1, replica_groups=mesh['dp'=2,'seq'=16] {'dp','seq'}, use_global_device_ids=true, to_apply=%region_64.66 | all-reduce | flops 72 | bytes 576 | tf_op jit(solution)/shard_map/psum | solution.py:284
  1002.5 4.5 fusion.235
  1007.0 4.3 fusion.127
  1011.4 135.1 %reduce-scatter.6.cloned.1.call-done = f32[48,3352]{1,0:T(8,128)} async-done(((f32[768,3352]{1,0:T(8,128)}), f32[48,3352]{1,0:T(8,128)}) %reduce-scatter.6.cloned.1.call-update) | async-done | bytes 643600 | tf_op jit(solution)/shard_map/reduce_scatter | solution.py:257
  1148.4 75.3 %all-reduce.41 = (bf16[768]{0:T(1024)(128)(2,1)S(1)}, bf16[1792]{0:T(1024)(128)(2,1)S(1)}, bf16[1536]{0:T(1024)(128)(2,1)S(1)}) all-reduce(f32[768]{0:T(1024)S(1)} %add.533, f32[1792]{0:T(1024)S(1)} %add.536, f32[1536]{0:T(1024)S(1)} %copy-done.90), channel_id=12, replica_groups=mesh['dp'=2,'seq'=16] {'seq'}, use_global_device_ids=true, to_apply=%region_39.41.clone | all-reduce | flops 4096 | bytes 24576
  1231.1 13.1 %all-reduce.47.cloned.1.call-done = (bf16[48,3352]{1,0:T(8,128)(2,1)}, bf16[96,768]{1,0:T(8,128)(2,1)}) async-done(((bf16[48,3352]{1,0:T(8,128)(2,1)}, bf16[96,768]{1,0:T(8,128)(2,1)}), (bf16[48,3352]{1,0:T(8,128)(2,1)}, bf16[96,768]{1,0:T(8,128)(2,1)})) %all-reduce.47.cloned.1.call-update) | async-done | bytes 469264 | tf_op jit(solution)/shard_map/psum | solution.py:282
  (648 shorter events, 279.4 us)
Async XLA Ops:
  7.2 138.1 %all-gather.14.cloned.1.call-start = ((), (), s32[]{:S(2)}) async-start(), calls=%async_computation.3 | async-start | bytes 5640192 | tf_op jit(solution)/shard_map/all_gather | solution.py:164
  7.9 185.7 %all-gather.16.cloned.1.call-start = ((), (), s32[]{:S(2)}) async-start(), calls=%async_computation.4 | async-start | bytes 2506752 | tf_op jit(solution)/shard_map/all_gather | solution.py:165
  8.7 313.0 %all-gather.18.cloned.1.call-start = ((), (), s32[]{:S(2)}) async-start(), calls=%async_computation.5 | async-start | bytes 13369344 | tf_op jit(solution)/shard_map/all_gather | solution.py:28
  9.4 132.1 %copy-start.125 = (f32[128]{0:T(128)}, f32[128]{0:T(128)S(1)}, u32[]{:S(2)}) copy-start(f32[128]{0:T(128)S(1)} %get-tuple-element.774) | copy-start | bytes 1540
  9.4 141.0 %copy-start.127 = (f32[128]{0:T(128)}, f32[128]{0:T(128)S(1)}, u32[]{:S(2)}) copy-start(f32[128]{0:T(128)S(1)} %get-tuple-element.775) | copy-start | bytes 1540
  9.5 130.5 %collective-permute-start.3 = (f32[3]{0:T(128)S(1)}, f32[3]{0:T(128)S(1)}, u32[]{:S(2)}, u32[]{:S(2)}) collective-permute-start(f32[3]{0:T(128)S(1)} %slice_bitcast_fusion), channel_id=1, source_target_pairs={{0,1},{1,2},{2,3},{3,4},{4,5},{5,6},{6,7},{7,8},{8,9},{9,10},{10,1... | collective-permute-start | bytes 44 | tf_op jit(solution)/shard_map/ppermute | solution.py:23
  14.4 123.7 %collective-permute-start.1 = (f32[3]{0:T(128)S(1)}, f32[3]{0:T(128)S(1)}, u32[]{:S(2)}, u32[]{:S(2)}) collective-permute-start(f32[3]{0:T(128)S(1)} %slice_bitcast_fusion.1), channel_id=1, source_target_pairs={{0,1},{1,2},{2,3},{3,4},{4,5},{5,6},{6,7},{7,8},{8,9},{9,10},{10,1... | collective-permute-start | bytes 44 | tf_op jit(solution)/shard_map/ppermute | solution.py:23
  136.1 47.4 %copy-start.59 = (f32[1792]{0:T(1024)}, f32[1792]{0:T(1024)S(1)}, u32[]{:S(2)}) copy-start(f32[1792]{0:T(1024)S(1)} %get-tuple-element.638) | copy-start | bytes 21508
  136.1 47.4 %copy-start.61 = (f32[1792]{0:T(1024)}, f32[1792]{0:T(1024)S(1)}, u32[]{:S(2)}) copy-start(f32[1792]{0:T(1024)S(1)} %get-tuple-element.639) | copy-start | bytes 21508
  136.2 47.4 %copy-start.63 = (f32[1792]{0:T(1024)}, f32[1792]{0:T(1024)S(1)}, u32[]{:S(2)}) copy-start(f32[1792]{0:T(1024)S(1)} %get-tuple-element.640) | copy-start | bytes 21508
  136.2 47.4 %copy-start.65 = (f32[1792]{0:T(1024)}, f32[1792]{0:T(1024)S(1)}, u32[]{:S(2)}) copy-start(f32[1792]{0:T(1024)S(1)} %get-tuple-element.641) | copy-start | bytes 21508
  145.2 38.3 %copy-start.113 = (f32[128]{0:T(128)}, f32[128]{0:T(128)S(1)}, u32[]{:S(2)}) copy-start(f32[128]{0:T(128)S(1)} %get-tuple-element.765) | copy-start | bytes 1540
  145.3 38.3 %copy-start.115 = (f32[128]{0:T(128)}, f32[128]{0:T(128)S(1)}, u32[]{:S(2)}) copy-start(f32[128]{0:T(128)S(1)} %get-tuple-element.766) | copy-start | bytes 1540
  145.3 38.3 %copy-start.117 = (f32[128]{0:T(128)}, f32[128]{0:T(128)S(1)}, u32[]{:S(2)}) copy-start(f32[128]{0:T(128)S(1)} %get-tuple-element.767) | copy-start | bytes 1540
  150.5 356.7 %copy-start.3 = (f32[128,3352]{0,1:T(8,128)}, f32[128,3352]{0,1:T(8,128)S(1)}, u32[]{:S(2)}) copy-start(f32[128,3352]{0,1:T(8,128)S(1)} %fusion.196) | copy-start | bytes 5148676
  155.2 708.5 %copy-start.57 = (f32[128,24]{0,1:T(8,128)}, f32[128,24]{0,1:T(8,128)S(1)}, u32[]{:S(2)}) copy-start(f32[128,24]{0,1:T(8,128)S(1)} %get-tuple-element.772) | copy-start | bytes 36868
  155.9 5.4 collective-permute-start
  171.2 303.4 %all-gather.20.cloned.1.call-start = ((), (), s32[]{:S(2)}) async-start(), calls=%async_computation.6 | async-start | bytes 13369344 | tf_op jit(solution)/shard_map/all_gather | solution.py:28
  175.6 6.6 collective-permute-start.2
  192.0 471.7 %all-gather.24.cloned.1.call-start = ((), (), s32[]{:S(2)}) async-start(), calls=%async_computation.8 | async-start | bytes 13369344 | tf_op jit(solution)/shard_map/all_gather | solution.py:28
  351.3 155.9 %copy-start.129 = (f32[128]{0:T(128)}, f32[128]{0:T(128)S(1)}, u32[]{:S(2)}) copy-start(f32[128]{0:T(128)S(1)} %fusion.211) | copy-start | bytes 1540
  513.3 303.2 %all-gather.22.cloned.1.call-start = ((), (), s32[]{:S(2)}) async-start(), calls=%async_computation.7 | async-start | bytes 13369344 | tf_op jit(solution)/shard_map/all_gather | solution.py:28
  515.9 441.5 %reduce-scatter.8.cloned.1.call-start = ((), (), s32[]{:S(2)}) async-start(), calls=%async_computation.10 | async-start | bytes 5013504 | tf_op jit(solution)/shard_map/reduce_scatter | solution.py:269
  557.4 589.1 %reduce-scatter.6.cloned.1.call-start = ((), (), s32[]{:S(2)}) async-start(), calls=%async_computation.9 | async-start | bytes 11280384 | tf_op jit(solution)/shard_map/reduce_scatter | solution.py:257
  884.1 15.9 %collective-permute-start.5 = (f32[3,1792]{1,0:T(4,128)}, f32[3,1792]{1,0:T(4,128)}, u32[]{:S(2)}, u32[]{:S(2)}) collective-permute-start(f32[3,1792]{1,0:T(4,128)} %copy.299), channel_id=1, source_target_pairs={{1,0},{2,1},{3,2},{4,3},{5,4},{6,5},{7,6},{8,7},{9,8},{10,9},{11,1... | collective-permute-start | bytes 64520 | tf_op jit(solution)/shard_map/ppermute | solution.py:23
  893.2 7.8 collective-permute-start.4
  913.5 312.1 %reduce-scatter.10.cloned.1.call-start = ((), (), s32[]{:S(2)}) async-start(), calls=%async_computation.11 | async-start | bytes 974848
  926.1 76.4 %copy-start.38 = (bf16[128,3352]{0,1:T(8,128)(2,1)S(1)}, bf16[128,3352]{0,1:T(8,128)(2,1)}, u32[]{:S(2)}) copy-start(bf16[128,3352]{0,1:T(8,128)(2,1)} %copy-done.37) | copy-start | bytes 2574340
  960.7 283.6 %all-reduce.47.cloned.1.call-start = ((), (), s32[]{:S(2)}) async-start(), calls=%async_computation.12 | async-start | bytes 958464 | tf_op jit(solution)/shard_map/psum | solution.py:282
  1007.0 141.4 %copy-start.145 = (f32[128]{0:T(128)S(1)}, f32[128]{0:T(128)}, u32[]{:S(2)}) copy-start(f32[128]{0:T(128)} %copy-done.144) | copy-start | bytes 1540
  1007.0 141.4 %copy-start.90 = (f32[1536]{0:T(1024)S(1)}, f32[1536]{0:T(1024)}, u32[]{:S(2)}) copy-start(f32[1536]{0:T(1024)} %add.537) | copy-start | bytes 18436
  1011.3 212.6 %copy-start.48 = (bf16[2,1,128,768]{3,2,1,0:T(8,128)(2,1)S(1)}, bf16[2,1,128,768]{3,2,1,0:T(8,128)(2,1)}, u32[]{:S(2)}) copy-start(bf16[2,1,128,768]{3,2,1,0:T(8,128)(2,1)} %param.22) | copy-start | bytes 1179652
  (138 other events, 1345.2 us)
Sparse Core Ops, SparseCore 0:
  10.8 89.7 all-gather.13
  103.4 61.8 all-gather.15
  171.3 150.3 all-gather.17
  324.3 150.2 all-gather.19
  513.4 150.1 all-gather.23
  666.3 150.1 all-gather.21
  821.7 135.6 reduce-scatter.7
  964.2 182.2 reduce-scatter.5
  1148.8 76.8 reduce-scatter.9
  1229.2 15.0 all-reduce.46
where the time goes:
time: 1270 us; the launch traced here: 1250 us
  waiting for transfers between devices  577 us (45%)
  blocking collectives  304 us (24%)
  other arithmetic  161 us (13%)
  matrix products  93.3 us (7%)
  local copies, waits for them, and re-layouts  72.3 us (6%)
  between operations  25.8 us (2%)
  starting transfers between devices  20.1 us (2%)
    all_gather x4, waiting for transfers between devices, prefix(): everything = jax.tree.map(lambda part: lax.all_gather(part, axis), array)  395 us
    unnamed x2, blocking collectives  150 us
    reduce_scatter x1, waiting for transfers between devices, body(): lax.psum_scatter(lax.dot_general(normed_low, proj_grad_low, (((0,), (0,))...  135 us
    select_n x64, other arithmetic, lap(): return jax.tree.map(lambda a, b: jnp.where(reached, a, b), new, before)  83.7 us
    all_gather x2, blocking collectives, prefix(): everything = jax.tree.map(lambda part: lax.all_gather(part, axis), array)  73.7 us
    psum x1, blocking collectives, body(): lax.psum((head_totals[0], head_totals[1], head_totals[2]), ('dp', 'seq'))  41.8 us
    all_gather x1, blocking collectives, body(): lax.all_gather(conv_weight, 'seq', axis=1, tiled=True)  35.8 us
    reduce_scatter x1, waiting for transfers between devices, body(): lax.psum_scatter(out_term, 'seq', scatter_dimension=0, tiled=True)  30.5 us
  transfers between devices with their start and end apart: 16, of which 9 were waited for; matrix products, arithmetic and copies ran while one was open for 22% of the time, Pallas kernels for 0%

commit v1 on v0

--- a/solution.py
+++ b/solution.py
@@ -1,8 +1,11 @@
+import functools
 from functools import partial
 
 import jax
 import jax.numpy as jnp
 from jax import lax
+from jax.experimental import pallas as pl
+from jax.experimental.pallas import tpu as pltpu
 from jax.sharding import PartitionSpec as P
 
 DI = 1536
@@ -11,6 +14,222 @@
 N = 128
 KC = 4
 CH = 1792
+
+
+MESH = pl.DeviceIdType.MESH
+
+
+def chip(x, y, z):
+    return z * 4 + y * 2 + x
+
+
+def place():
+    core = lax.axis_index("dp")
+    at = lax.axis_index("seq")
+    return at % 2, (at // 2) % 2, at // 4, core
+
+
+def meet_all(planes):
+    barrier = pltpu.get_barrier_semaphore()
+    me = lax.axis_index("seq")
+    core = lax.axis_index("dp")
+    count = planes * 4
+
+    def greet(k, carry):
+        other = lax.rem(me + k, count)
+        for far in range(2):
+
+            @pl.when(jnp.logical_or(k > 0, far != core))
+            def _():
+                pl.semaphore_signal(barrier, inc=1, device_id=(far, other), device_id_type=MESH)
+
+        return carry
+
+    lax.fori_loop(0, count, greet, 0)
+    pl.semaphore_wait(barrier, 2 * count - 1)
+
+
+UP, DOWN, SIDE_X, SIDE_Y, HALF_X, HALF_Y, MATE_Z, MATE_X, MATE_Y, MATE_HX, MATE_HY = range(11)
+
+
+class Gather:
+    def __init__(self, whole, rows, quarter, sems, planes):
+        self.whole, self.rows, self.quarter, self.sems, self.planes = whole, rows, quarter, sems, planes
+        self.x, self.y, self.z, self.core = place()
+
+    def region(self, block, core, part=None):
+        width = self.whole.shape[1] // 2
+        start = pl.multiple_of(block * self.rows, 16)
+        left = pl.multiple_of(core * width, 128)
+        if part is None:
+            return self.whole.at[pl.ds(start, self.rows), pl.ds(left, width)]
+        if self.quarter == "rows":
+            half = self.rows // 2
+            return self.whole.at[pl.ds(pl.multiple_of(start + part * half, 16), half), pl.ds(left, width)]
+        half = width // 2
+        return self.whole.at[pl.ds(start, self.rows), pl.ds(pl.multiple_of(left + part * half, 128), half)]
+
+    def copy(self, kind, far, block, core, part, device):
+        region = self.region(block, core, part)
+        return pltpu.make_async_remote_copy(
+            src_ref=region,
+            dst_ref=region,
+            send_sem=self.sems.at[0, kind, far],
+            recv_sem=self.sems.at[1, kind, far],
+            device_id=device,
+            device_id_type=MESH,
+        )
+
+    def transfers(self, far):
+        x, y, z, c = self.x, self.y, self.z, self.core
+        own = chip(x, y, far)
+        by_x, by_y, across = chip(1 - x, y, far), chip(x, 1 - y, far), chip(1 - x, 1 - y, far)
+        mate = (1 - c, chip(x, y, z))
+        to_x, to_y = (c, chip(1 - x, y, z)), (c, chip(x, 1 - y, z))
+        return {
+            UP: (own, None, (c, chip(x, y, z + 1))),
+            DOWN: (own, None, (c, chip(x, y, z - 1))),
+            SIDE_X: (own, None, to_x),
+            SIDE_Y: (own, None, to_y),
+            HALF_X: (by_y, 1, to_x),
+            HALF_Y: (by_x, 0, to_y),
+            MATE_Z: (own, None, mate),
+            MATE_X: (by_x, None, mate),
+            MATE_Y: (by_y, None, mate),
+            MATE_HX: (across, 1, mate),
+            MATE_HY: (across, 0, mate),
+        }
+
+    def send(self, kind, far):
+        block, part, device = self.transfers(far)[kind]
+        self.copy(kind, far, block, self.core, part, device).start()
+
+    def sent(self, kind, far):
+        block, part, device = self.transfers(far)[kind]
+        self.copy(kind, far, block, self.core, part, device).wait_send()
+
+    def arrived(self, kind, far):
+        x, y = self.x, self.y
+        block, part, core = {
+            UP: (chip(x, y, far), None, 0),
+            DOWN: (chip(x, y, far), None, 0),
+            SIDE_X: (chip(1 - x, y, far), None, 0),
+            SIDE_Y: (chip(x, 1 - y, far), None, 0),
+            HALF_X: (chip(1 - x, 1 - y, far), 1, 0),
+            HALF_Y: (chip(1 - x, 1 - y, far), 0, 0),
+            MATE_Z: (chip(x, y, far), None, 1),
+            MATE_X: (chip(1 - x, y, far), None, 1),
+            MATE_Y: (chip(x, 1 - y, far), None, 1),
+            MATE_HX: (chip(1 - x, 1 - y, far), 1, 1),
+            MATE_HY: (chip(1 - x, 1 - y, far), 0, 1),
+        }[kind]
+        owner = self.core if core == 0 else 1 - self.core
+        self.copy(kind, far, block, owner, part, (1 - self.core, chip(x, y, self.z))).wait_recv()
+
+    def each(self, distance, act):
+        for sign in (-1, 1) if distance else (1,):
+            far = self.z + sign * distance
+            if distance:
+                pl.when(jnp.logical_and(far >= 0, far < self.planes))(functools.partial(act, far, sign))
+            else:
+                act(far, sign)
+
+    def column(self, distance):
+        def act(far, sign):
+            if distance:
+                self.arrived(UP if sign < 0 else DOWN, far)
+            if sign < 0 or not distance:
+                pl.when(self.z < self.planes - 1)(lambda: self.send(UP, far))
+            if sign > 0:
+                pl.when(self.z > 0)(lambda: self.send(DOWN, far))
+            self.send(SIDE_X, far)
+            self.send(SIDE_Y, far)
+            if distance:
+                self.send(MATE_Z, far)
+
+        self.each(distance, act)
+
+    def sides(self, distance):
+        def act(far, sign):
+            self.arrived(SIDE_X, far)
+            self.send(HALF_Y, far)
+            self.send(MATE_X, far)
+            self.arrived(SIDE_Y, far)
+            self.send(HALF_X, far)
+            self.send(MATE_Y, far)
+
+        self.each(distance, act)
+
+    def diagonal(self, distance):
+        def act(far, sign):
+            self.arrived(HALF_Y, far)
+            self.send(MATE_HY, far)
+            self.arrived(HALF_X, far)
+            self.send(MATE_HX, far)
+
+        self.each(distance, act)
+
+    def finish(self):
+        for distance in range(self.planes):
+
+            def act(far, sign):
+                if sign < 0 or not distance:
+                    pl.when(self.z < self.planes - 1)(lambda: self.sent(UP, far))
+                if sign > 0:
+                    pl.when(self.z > 0)(lambda: self.sent(DOWN, far))
+                for kind in (SIDE_X, SIDE_Y, HALF_X, HALF_Y, MATE_X, MATE_Y, MATE_HX, MATE_HY):
+                    self.sent(kind, far)
+                for kind in (MATE_X, MATE_Y, MATE_HX, MATE_HY):
+                    self.arrived(kind, far)
+                if distance:
+                    self.sent(MATE_Z, far)
+                    self.arrived(MATE_Z, far)
+
+            self.each(distance, act)
+
+    def steps(self):
+        do = [lambda: self.column(0), lambda: self.column(1), lambda: self.sides(0), lambda: self.column(2), lambda: self.diagonal(0),
+              lambda: self.sides(1), lambda: self.column(3), lambda: self.diagonal(1), lambda: self.sides(2), lambda: self.diagonal(2),
+              lambda: self.sides(3), lambda: self.diagonal(3)]
+        return do
+
+
+def gather_sems(planes):
+    return pltpu.SemaphoreType.DMA((2, 11, planes))
+
+
+def gather_kernel(planes, in_ref, out_ref, in_full, out_full, in_sems, out_sems):
+    at = lax.axis_index("seq")
+    for ref, full in ((in_ref, in_full), (out_ref, out_full)):
+        rows = ref.shape[0]
+        full[pl.ds(pl.multiple_of(at * rows, 16), rows), :] = ref[...]
+    first = Gather(in_full, in_ref.shape[0], "columns", in_sems, planes)
+    second = Gather(out_full, out_ref.shape[0], "rows", out_sems, planes)
+    meet_all(planes)
+    for step in first.steps():
+        step()
+    for step in second.steps():
+        step()
+    first.finish()
+    second.finish()
+
+
+def gather_weights(w_in, w_out):
+    count = lax.axis_size("seq")
+    if count != 16:
+        return tuple(lax.all_gather(w, "seq", axis=0, tiled=True) for w in (w_in, w_out))
+    wide = jnp.pad(w_in, ((0, 0), (0, 3584 - w_in.shape[1])))
+    whole = [jax.ShapeDtypeStruct((w.shape[0] * count, w.shape[1]), w.dtype) for w in (wide, w_out)]
+    vmem = pl.BlockSpec(memory_space=pltpu.VMEM)
+    full, out = pl.pallas_call(
+        functools.partial(gather_kernel, count // 4),
+        out_shape=whole,
+        in_specs=[vmem, vmem],
+        out_specs=[vmem, vmem],
+        scratch_shapes=[gather_sems(count // 4), gather_sems(count // 4)],
+        compiler_params=pltpu.CompilerParams(collective_id=0, has_side_effects=True, vmem_limit_bytes=40 << 20),
+    )(wide, w_out)
+    return full[:, : w_in.shape[1]], out
 
 
 EPSILON = 1e-05
@@ -62,7 +281,9 @@
 
 
 def cumulative(step_size, rate):
-    return jnp.cumsum(step_size * rate[None, :], axis=0)
+    length_t = step_size.shape[0]
+    lower = jnp.tril(jnp.ones((length_t, length_t), jnp.float32))
+    return jnp.dot(lower, step_size * rate[None, :], precision=HIGHEST)
 
 
 def block_state(inner, b_proj, step_size, rate, seg_one, previous):
@@ -159,10 +380,11 @@
     )
     act_list = []
     grad_list = []
+    both = gather_weights(w_in, w_out)
     for micro in range(batches):
         gathered = (
-            lax.all_gather(w_in, "seq", axis=0, tiled=True),
-            lax.all_gather(w_out, "seq", axis=0, tiled=True),
+            both[0],
+            both[1],
             lax.all_gather(conv_weight, "seq", axis=1, tiled=True),
             lax.all_gather(conv_bias, "seq", axis=0, tiled=True),
             lax.all_gather(norm_gain, "seq", axis=0, tiled=True),
@@ -216,10 +438,7 @@
         branch = jnp.dot(gate_low, out_full, preferred_element_type=jnp.float32)
         act_list.append((resid + branch).astype(jnp.bfloat16))
         cot_low = cotangent[micro, 0]
-        again = (
-            lax.all_gather(w_in, "seq", axis=0, tiled=True),
-            lax.all_gather(w_out, "seq", axis=0, tiled=True),
-        )
+        again = both
         in_back = again[0]
         out_back = again[1]
         out_term = lax.dot_general(

time: 1270 us -> 1330 us (1.047)
  Pallas kernels: 0 us -> 49.6 us
  waiting for transfers between devices: 577 us -> 532 us
  other arithmetic: 161 us -> 192 us
    pallas_call x0 -> x1, Pallas kernels: none -> 49.6 us  [gather_weights(): pl.pallas_call(functools.partial(gather_kernel, count // 4), out_shape=wh...]
    all_gather x4, waiting for transfers between devices: 395 us -> 352 us  [prefix(): everything = jax.tree.map(lambda part: lax.all_gather(part, axis), array)]
    select_n x64, other arithmetic: 83.7 us -> 120 us  [lap(): return jax.tree.map(lambda a, b: jnp.where(reached, a, b), new, before)]
    mul x64, local copies, waits for them, and re-layouts: 22.3 us -> 43.7 us  [chain_link(): later[0][:, None, None] * earlier[1] + later[1]]
  transfers between devices with their start and end apart: 16 -> 14, of which waited for: 9 -> 8; matrix products, arithmetic and copies ran while one was open for 22% -> 23% of each run, Pallas kernels for 0% -> 4%
where the time goes in v1:
time: 1330 us; the launch traced here: 1310 us
  waiting for transfers between devices  532 us (40%)
  blocking collectives  305 us (23%)
  other arithmetic  192 us (14%)
  matrix products  98.5 us (7%)
  local copies, waits for them, and re-layouts  83.4 us (6%)
  Pallas kernels  49.6 us (4%)
  starting transfers between devices  26 us (2%)
  between operations  25.9 us (2%)
    all_gather x4, waiting for transfers between devices, prefix(): everything = jax.tree.map(lambda part: lax.all_gather(part, axis), array)  352 us
    unnamed x2, blocking collectives  149 us
    reduce_scatter x1, waiting for transfers between devices, body(): lax.psum_scatter(lax.dot_general(normed_low, proj_grad_low, (((0,), (0,))...  135 us
    select_n x64, other arithmetic, lap(): return jax.tree.map(lambda a, b: jnp.where(reached, a, b), new, before)  120 us
    all_gather x2, blocking collectives, prefix(): everything = jax.tree.map(lambda part: lax.all_gather(part, axis), array)  74.8 us
    pallas_call x1, Pallas kernels, gather_weights(): pl.pallas_call(functools.partial(gather_kernel, count // 4), out_shape=wh...  49.6 us
    mul x64, local copies, waits for them, and re-layouts, chain_link(): later[0][:, None, None] * earlier[1] + later[1]  43.7 us
    psum x1, blocking collectives, body(): lax.psum((head_totals[0], head_totals[1], head_totals[2]), ('dp', 'seq'))  41.6 us
  transfers between devices with their start and end apart: 14, of which 8 were waited for; matrix products, arithmetic and copies ran while one was open for 23% of the time, Pallas kernels for 4%

profile of v1, /device:TPU:0, one launch (start us, length us, event | category | flops | bytes accessed | tf_op | source)
XLA Modules:
  0.0 1313.4 jit_solution(1107144092940451286)
XLA Ops:
  8.0 4.8 collective-permute-start.3
  23.4 73.4 %all-reduce.43 = (bf16[768]{0:T(1024)(128)(2,1)S(1)}, bf16[1792]{0:T(1024)(128)(2,1)S(1)}, bf16[1536]{0:T(1024)(128)(2,1)}) all-reduce(bf16[768]{0:T(1024)(128)(2,1)S(1)} %dynamic-update-slice.1, bf16[1792]{0:T(1024)(128)(2,1)S(1)} %dynamic-update-slice, bf16[1536]{0:T(1024)(128)(2,1)S(1)} %dynamic-update-slice.2), channel_id=1, replica_groups=mesh['dp'=2,'seq'=16] {'seq'}, use_global_device_ids=true, to_apply=%add.36 | all-reduce | flops 4096 | bytes 16384
  98.7 49.6 %shard_map.203 = (bf16[768,3584]{1,0:T(8,128)(2,1)S(1)}, bf16[1536,768]{1,0:T(8,128)(2,1)S(1)}) custom-call(bf16[48,3584]{1,0:T(8,128)(2,1)S(1)} %pad.107.in_ref, bf16[96,768]{1,0:T(8,128)(2,1)S(1)} %copy-done), custom_call_target="tpu_custom_call" | custom-call | tf_op jit(solution)/shard_map/pallas_call | solution.py:224
  158.6 36.9 %all-gather.4 = bf16[16,112,4]{1,2,0:T(4,128)(2,1)S(1)} all-gather(bf16[1,112,4]{1,2,0:T(4,128)(2,1)S(1)} %bitcast.327), channel_id=1, replica_groups=mesh['dp'=2,'seq'=16] {'seq'}, dimensions={0}, use_global_device_ids=true | all-gather | bytes 15232 | tf_op jit(solution)/shard_map/all_gather | solution.py:388
  195.8 6.0 fusion.8
  212.2 5.4 fusion.81
  232.3 5.4 fusion.80
  245.9 36.8 %all-gather.5 = f32[16,1,24]{2,1,0:T(1,128)} all-gather(f32[1,1,24]{2,1,0:T(1,128)S(1)} %bitcast.325), channel_id=1, replica_groups=mesh['dp'=2,'seq'=16] {'seq'}, dimensions={0}, use_global_device_ids=true | all-gather | bytes 1632 | tf_op jit(solution)/shard_map/all_gather | solution.py:247
  282.8 38.0 %all-gather.6 = f32[16,1,24]{2,1,0:T(1,128)} all-gather(f32[1,1,24]{2,1,0:T(1,128)S(1)} %bitcast.326), channel_id=1, replica_groups=mesh['dp'=2,'seq'=16] {'seq'}, dimensions={0}, use_global_device_ids=true | all-gather | bytes 1632 | tf_op jit(solution)/shard_map/all_gather | solution.py:247
  324.3 45.0 %all-gather.12.cloned.1.call-done = f32[384,64,128]{2,1,0:T(8,128)} async-done(((f32[24,64,128]{2,1,0:T(8,128)}), f32[384,64,128]{2,1,0:T(8,128)}) %all-gather.12.cloned.1.call-update) | async-done | bytes 12582928 | tf_op jit(solution)/shard_map/all_gather | solution.py:247
  369.3 50.5 %while.60 = (s32[]{:T(128)}, f32[24,64,128]{2,1,0:T(8,128)}, s32[]{:T(128)}, f32[16,24]{1,0:T(8,128)}, f32[16,24,64,128]{3,2,1,0:T(8,128)}, /*index=5*/s32[]{:T(128)}, s32[]{:T(128)}) while((s32[]{:T(128)}, f32[24,64,128]{2,1,0:T(8,128)}, s32[]{:T(128)}, f32[16,24]{1,0:T(8,128)}, f32[16,24,64,128]{3,2,1,0:T(8,128)}, ...), condition=%wide.region_2.4_spmd.clone, body=%wide.region_1.3_spmd.clone.sunk | while | flops 786436 | bytes 2359697 | solution.py:260
  421.8 5.1 fusion.52
  430.6 91.8 %all-gather.14.cloned.1.call-done = f32[384,64,128]{2,1,0:T(8,128)} async-done(((f32[24,64,128]{2,1,0:T(8,128)}), f32[384,64,128]{2,1,0:T(8,128)}) %all-gather.14.cloned.1.call-update) | async-done | bytes 12582928 | tf_op jit(solution)/shard_map/all_gather | solution.py:247
  522.4 32.1 %while.61 = (s32[]{:T(128)}, f32[24,64,128]{2,1,0:T(8,128)S(1)}, s32[]{:T(128)}, f32[16,24]{1,0:T(8,128)}, f32[16,24,64,128]{3,2,1,0:T(8,128)}, /*index=5*/s32[]{:T(128)}, s32[]{:T(128)}) while((s32[]{:T(128)}, f32[24,64,128]{2,1,0:T(8,128)S(1)}, s32[]{:T(128)}, f32[16,24]{1,0:T(8,128)}, f32[16,24,64,128]{3,2,1,0:T(8,128)}, ...), condition=%wide.region_6.8_spmd.clone, body=%wide.region_5.7_spmd.clone.sunk | while | flops 786436 | bytes 2359697 | solution.py:260
  556.2 5.1 fusion.58
  564.8 4.2 multiply_reduce_fusion.13
  574.2 8.8 reduce-scatter.8.cloned.1.call-start
  587.3 4.4 fusion.83
  594.5 4.4 fusion.85
  610.5 111.4 %all-gather.18.cloned.1.call-done = f32[384,64,128]{2,1,0:T(8,128)} async-done(((f32[24,64,128]{2,1,0:T(8,128)}), f32[384,64,128]{2,1,0:T(8,128)}) %all-gather.18.cloned.1.call-update) | async-done | bytes 12582928 | tf_op jit(solution)/shard_map/all_gather | solution.py:247
  721.9 49.4 %while.63 = (s32[]{:T(128)}, f32[24,64,128]{2,1,0:T(8,128)}, s32[]{:T(128)}, f32[16,24]{1,0:T(8,128)}, f32[16,24,64,128]{3,2,1,0:T(8,128)}, /*index=5*/s32[]{:T(128)}, s32[]{:T(128)}, s32[]{:T(128)}, s32[]{:T(128)}) while((s32[]{:T(128)}, f32[24,64,128]{2,1,0:T(8,128)}, s32[]{:T(128)}, f32[16,24]{1,0:T(8,128)}, ...), condition=%wide.region_26.28_spmd.clone, body=%wide.region_25.27_spmd.clone.sunk | while | flops 786440 | bytes 2359759 | solution.py:260
  771.3 103.5 %all-gather.16.cloned.1.call-done = f32[384,64,128]{2,1,0:T(8,128)} async-done(((f32[24,64,128]{2,1,0:T(8,128)}), f32[384,64,128]{2,1,0:T(8,128)}) %all-gather.16.cloned.1.call-update) | async-done | bytes 12582928 | tf_op jit(solution)/shard_map/all_gather | solution.py:247
  874.8 32.3 %while.62 = (s32[]{:T(128)}, f32[24,64,128]{2,1,0:T(8,128)S(1)}, s32[]{:T(128)}, f32[16,24]{1,0:T(8,128)}, f32[16,24,64,128]{3,2,1,0:T(8,128)}, /*index=5*/s32[]{:T(128)}, s32[]{:T(128)}, s32[]{:T(128)}, s32[]{:T(128)}) while((s32[]{:T(128)}, f32[24,64,128]{2,1,0:T(8,128)S(1)}, s32[]{:T(128)}, f32[16,24]{1,0:T(8,128)}, ...), condition=%wide.region_14.16_spmd.clone, body=%wide.region_13.15_spmd.clone.sunk | while | flops 786440 | bytes 2359759 | solution.py:260
  942.5 3.5 pad_add_fusion.1
  965.8 5.8 convolution_add_fusion
  984.6 31.4 %reduce-scatter.8.cloned.1.call-done = f32[96,768]{1,0:T(8,128)} async-done(((f32[1536,768]{1,0:T(8,128)}), f32[96,768]{1,0:T(8,128)}) %reduce-scatter.8.cloned.1.call-update) | async-done | bytes 294928 | tf_op jit(solution)/shard_map/reduce_scatter | solution.py:488
  1019.3 41.6 %all-reduce.41 = (f32[24]{0:T(128)}, f32[24]{0:T(128)}, f32[24]{0:T(128)}) all-reduce(f32[24]{0:T(128)S(1)} %add.526, f32[24]{0:T(128)S(1)} %add_multiply_fusion, f32[24]{0:T(128)S(1)} %copy-done.176), channel_id=1, replica_groups=mesh['dp'=2,'seq'=16] {'dp','seq'}, use_global_device_ids=true, to_apply=%region_58.60 | all-reduce | flops 72 | bytes 576 | tf_op jit(solution)/shard_map/psum | solution.py:503
  1061.0 4.4 fusion.4
  1065.5 4.3 fusion.135
  1069.8 135.0 %reduce-scatter.6.cloned.1.call-done = f32[48,3352]{1,0:T(8,128)} async-done(((f32[768,3352]{1,0:T(8,128)}), f32[48,3352]{1,0:T(8,128)}) %reduce-scatter.6.cloned.1.call-update) | async-done | bytes 643600 | tf_op jit(solution)/shard_map/reduce_scatter | solution.py:476
  1206.7 75.4 %all-reduce.42 = (bf16[768]{0:T(1024)(128)(2,1)S(1)}, bf16[1792]{0:T(1024)(128)(2,1)S(1)}, bf16[1536]{0:T(1024)(128)(2,1)S(1)}) all-reduce(f32[768]{0:T(1024)S(1)} %add.535, f32[1792]{0:T(1024)S(1)} %add.538, f32[1536]{0:T(1024)S(1)} %copy-done.103), channel_id=12, replica_groups=mesh['dp'=2,'seq'=16] {'seq'}, use_global_device_ids=true, to_apply=%region_33.35.clone | all-reduce | flops 4096 | bytes 24576
  1289.6 13.2 %all-reduce.48.cloned.1.call-done = (bf16[48,3352]{1,0:T(8,128)(2,1)}, bf16[96,768]{1,0:T(8,128)(2,1)}) async-done(((bf16[48,3352]{1,0:T(8,128)(2,1)}, bf16[96,768]{1,0:T(8,128)(2,1)}), (bf16[48,3352]{1,0:T(8,128)(2,1)}, bf16[96,768]{1,0:T(8,128)(2,1)})) %all-reduce.48.cloned.1.call-update) | async-done | bytes 469264 | tf_op jit(solution)/shard_map/psum | solution.py:501
  (666 shorter events, 331.8 us)
Async XLA Ops:
  7.2 362.2 %all-gather.12.cloned.1.call-start = ((), (), s32[]{:S(2)}) async-start(), calls=%async_computation.3 | async-start | bytes 13369344 | tf_op jit(solution)/shard_map/all_gather | solution.py:247
  7.9 199.5 %copy-start.125 = (f32[128]{0:T(128)}, f32[128]{0:T(128)S(1)}, u32[]{:S(2)}) copy-start(f32[128]{0:T(128)S(1)} %get-tuple-element.776) | copy-start | bytes 1540
  7.9 202.9 %copy-start.126 = (f32[128]{0:T(128)}, f32[128]{0:T(128)S(1)}, u32[]{:S(2)}) copy-start(f32[128]{0:T(128)S(1)} %get-tuple-element.777) | copy-start | bytes 1540
  8.0 198.8 %collective-permute-start.3 = (f32[3]{0:T(128)S(1)}, f32[3]{0:T(128)S(1)}, u32[]{:S(2)}, u32[]{:S(2)}) collective-permute-start(f32[3]{0:T(128)S(1)} %slice_bitcast_fusion), channel_id=1, source_target_pairs={{0,1},{1,2},{2,3},{3,4},{4,5},{5,6},{6,7},{7,8},{8,9},{9,10},{10,1... | collective-permute-start | bytes 44 | tf_op jit(solution)/shard_map/ppermute | solution.py:242
  12.9 191.3 %collective-permute-start.1 = (f32[3]{0:T(128)S(1)}, f32[3]{0:T(128)S(1)}, u32[]{:S(2)}, u32[]{:S(2)}) collective-permute-start(f32[3]{0:T(128)S(1)} %slice_bitcast_fusion.1), channel_id=1, source_target_pairs={{0,1},{1,2},{2,3},{3,4},{4,5},{5,6},{6,7},{7,8},{8,9},{9,10},{10,1... | collective-permute-start | bytes 44 | tf_op jit(solution)/shard_map/ppermute | solution.py:242
  20.8 137.8 %copy-start.163 = (f32[128]{0:T(128)}, f32[128]{0:T(128)S(1)}, u32[]{:S(2)}) copy-start(f32[128]{0:T(128)S(1)} %get-tuple-element.641) | copy-start | bytes 1540
  20.8 130.9 %copy-start.149 = (f32[128]{0:T(128)}, f32[128]{0:T(128)S(1)}, u32[]{:S(2)}) copy-start(f32[128]{0:T(128)S(1)} %fusion.266) | copy-start | bytes 1540
  153.6 57.4 %collective-permute-start = (f32[3,1792]{1,0:T(4,128)S(1)}, f32[3,1792]{1,0:T(4,128)S(1)}, u32[]{:S(2)}, u32[]{:S(2)}) collective-permute-start(f32[3,1792]{1,0:T(4,128)S(1)} %copy.131), channel_id=1, source_target_pairs={{0,1},{1,2},{2,3},{3,4},{4,5},{5,6},{6,7},{7,8},{8,9},{9,10},{10,1... | collective-permute-start | bytes 64520 | tf_op jit(solution)/shard_map/ppermute | solution.py:242
  158.5 53.8 %copy-start.31 = (f32[128,1792]{0,1:T(8,128)}, f32[128,1792]{0,1:T(8,128)S(1)}, u32[]{:S(2)}) copy-start(f32[128,1792]{0,1:T(8,128)S(1)} %slice.210) | copy-start | bytes 2752516
  158.5 69.4 %copy-start.177 = (f32[24]{0:T(128)}, f32[24]{0:T(128)S(1)}, u32[]{:S(2)}) copy-start(f32[24]{0:T(128)S(1)} %exponential_negate_fusion) | copy-start | bytes 292
  158.5 43.2 %copy-start.134 = (f32[128]{0:T(128)}, f32[128]{0:T(128)S(1)}, u32[]{:S(2)}) copy-start(f32[128]{0:T(128)S(1)} %fusion.268) | copy-start | bytes 1540
  195.7 36.5 %copy-start.68 = (f32[1792]{0:T(1024)}, f32[1792]{0:T(1024)S(1)}, u32[]{:S(2)}) copy-start(f32[1792]{0:T(1024)S(1)} %get-tuple-element.642) | copy-start | bytes 21508
  195.7 36.5 %copy-start.70 = (f32[1792]{0:T(1024)}, f32[1792]{0:T(1024)S(1)}, u32[]{:S(2)}) copy-start(f32[1792]{0:T(1024)S(1)} %get-tuple-element.643) | copy-start | bytes 21508
  195.7 36.5 %copy-start.72 = (f32[1792]{0:T(1024)}, f32[1792]{0:T(1024)S(1)}, u32[]{:S(2)}) copy-start(f32[1792]{0:T(1024)S(1)} %get-tuple-element.644) | copy-start | bytes 21508
  195.7 36.5 %copy-start.74 = (f32[1792]{0:T(1024)}, f32[1792]{0:T(1024)S(1)}, u32[]{:S(2)}) copy-start(f32[1792]{0:T(1024)S(1)} %get-tuple-element.645) | copy-start | bytes 21508
  220.7 301.7 %all-gather.14.cloned.1.call-start = ((), (), s32[]{:S(2)}) async-start(), calls=%async_computation.4 | async-start | bytes 13369344 | tf_op jit(solution)/shard_map/all_gather | solution.py:247
  222.5 8.4 collective-permute-start.2
  240.7 481.3 %all-gather.18.cloned.1.call-start = ((), (), s32[]{:S(2)}) async-start(), calls=%async_computation.6 | async-start | bytes 13369344 | tf_op jit(solution)/shard_map/all_gather | solution.py:247
  244.3 38.5 %copy-start.157 = (f32[24]{0:T(128)S(1)}, f32[24]{0:T(128)}, u32[]{:S(2)}) copy-start(f32[24]{0:T(128)} %get-tuple-element.653) | copy-start | bytes 292
  571.6 303.2 %all-gather.16.cloned.1.call-start = ((), (), s32[]{:S(2)}) async-start(), calls=%async_computation.5 | async-start | bytes 13369344 | tf_op jit(solution)/shard_map/all_gather | solution.py:247
  574.2 441.8 %reduce-scatter.8.cloned.1.call-start = ((), (), s32[]{:S(2)}) async-start(), calls=%async_computation.8 | async-start | bytes 5013504 | tf_op jit(solution)/shard_map/reduce_scatter | solution.py:488
  610.5 594.3 %reduce-scatter.6.cloned.1.call-start = ((), (), s32[]{:S(2)}) async-start(), calls=%async_computation.7 | async-start | bytes 11280384 | tf_op jit(solution)/shard_map/reduce_scatter | solution.py:476
  941.2 17.0 %collective-permute-start.5 = (f32[3,1792]{1,0:T(4,128)S(1)}, f32[3,1792]{1,0:T(4,128)S(1)}, u32[]{:S(2)}, u32[]{:S(2)}) collective-permute-start(f32[3,1792]{1,0:T(4,128)S(1)} %copy.157), channel_id=1, source_target_pairs={{1,0},{2,1},{3,2},{4,3},{5,4},{6,5},{7,6},{8,7},{9,8},{10,9},{11,1... | collective-permute-start | bytes 64520 | tf_op jit(solution)/shard_map/ppermute | solution.py:242
  947.7 11.8 collective-permute-start.4
  971.6 312.5 %reduce-scatter.10.cloned.1.call-start = ((), (), s32[]{:S(2)}) async-start(), calls=%async_computation.9 | async-start | bytes 974848
  983.7 35.4 %copy-start.93 = (f32[1792]{0:T(1024)S(1)}, f32[1792]{0:T(1024)}, u32[]{:S(2)}) copy-start(f32[1792]{0:T(1024)} %get-tuple-element.624) | copy-start | bytes 21508
  983.8 35.5 %copy-start.176 = (f32[24]{0:T(128)S(1)}, f32[24]{0:T(128)}, u32[]{:S(2)}) copy-start(f32[24]{0:T(128)} %add.530) | copy-start | bytes 292
  983.8 77.2 %copy-start.50 = (bf16[128,3352]{0,1:T(8,128)(2,1)S(1)}, bf16[128,3352]{0,1:T(8,128)(2,1)}, u32[]{:S(2)}) copy-start(bf16[128,3352]{0,1:T(8,128)(2,1)} %copy-done.49) | copy-start | bytes 2574340
  1019.2 283.6 %all-reduce.48.cloned.1.call-start = ((), (), s32[]{:S(2)}) async-start(), calls=%async_computation.10 | async-start | bytes 958464 | tf_op jit(solution)/shard_map/psum | solution.py:501
  1065.5 141.2 %copy-start.162 = (f32[128]{0:T(128)S(1)}, f32[128]{0:T(128)}, u32[]{:S(2)}) copy-start(f32[128]{0:T(128)} %copy-done.161) | copy-start | bytes 1540
  1065.5 141.3 %copy-start.103 = (f32[1536]{0:T(1024)S(1)}, f32[1536]{0:T(1024)}, u32[]{:S(2)}) copy-start(f32[1536]{0:T(1024)} %add.539) | copy-start | bytes 18436
  1069.8 212.5 %copy-start.46 = (bf16[2,1,128,768]{3,2,1,0:T(8,128)(2,1)S(1)}, bf16[2,1,128,768]{3,2,1,0:T(8,128)(2,1)}, u32[]{:S(2)}) copy-start(bf16[2,1,128,768]{3,2,1,0:T(8,128)(2,1)} %param.22) | copy-start | bytes 1179652
  (160 other events, 1275.3 us)
Sparse Core Ops, SparseCore 0:
  220.8 148.4 all-gather.11
  372.1 150.2 all-gather.13
  571.7 150.1 all-gather.17
  724.6 150.1 all-gather.15
  879.8 136.0 reduce-scatter.7
  1022.6 182.1 reduce-scatter.5
  1207.1 77.0 reduce-scatter.9
  1287.8 14.9 all-reduce.47

commit v2 on v0

--- a/solution.py
+++ b/solution.py
@@ -1,8 +1,11 @@
+import functools
 from functools import partial
 
 import jax
 import jax.numpy as jnp
 from jax import lax
+from jax.experimental import pallas as pl
+from jax.experimental.pallas import tpu as pltpu
 from jax.sharding import PartitionSpec as P
 
 DI = 1536
@@ -62,7 +65,9 @@
 
 
 def cumulative(step_size, rate):
-    return jnp.cumsum(step_size * rate[None, :], axis=0)
+    length_t = step_size.shape[0]
+    lower = jnp.tril(jnp.ones((length_t, length_t), jnp.float32))
+    return jnp.dot(lower, step_size * rate[None, :], precision=HIGHEST)
 
 
 def block_state(inner, b_proj, step_size, rate, seg_one, previous):
@@ -299,6 +304,1252 @@
     )
 
 
+MESH = pl.DeviceIdType.MESH
+
+
+def chip(x, y, z):
+    return z * 4 + y * 2 + x
+
+
+def place():
+    core = lax.axis_index("dp")
+    at = lax.axis_index("seq")
+    return at % 2, (at // 2) % 2, at // 4, core
+
+
+def meet_all(planes):
+    barrier = pltpu.get_barrier_semaphore()
+    me = lax.axis_index("seq")
+    core = lax.axis_index("dp")
+    count = planes * 4
+
+    def greet(k, carry):
+        other = lax.rem(me + k, count)
+        for far in range(2):
+
+            @pl.when(jnp.logical_or(k > 0, far != core))
+            def _():
+                pl.semaphore_signal(barrier, inc=1, device_id=(far, other), device_id_type=MESH)
+
+        return carry
+
+    lax.fori_loop(0, count, greet, 0)
+    pl.semaphore_wait(barrier, 2 * count - 1)
+
+
+UP, DOWN, SIDE_X, SIDE_Y, HALF_X, HALF_Y, MATE_Z, MATE_X, MATE_Y, MATE_HX, MATE_HY = range(11)
+
+
+class Gather:
+    def __init__(self, whole, rows, quarter, sems, planes):
+        self.whole, self.rows, self.quarter, self.sems, self.planes = whole, rows, quarter, sems, planes
+        self.x, self.y, self.z, self.core = place()
+
+    def region(self, block, core, part=None):
+        width = self.whole.shape[1] // 2
+        start = pl.multiple_of(block * self.rows, 16)
+        left = pl.multiple_of(core * width, 128)
+        if part is None:
+            return self.whole.at[pl.ds(start, self.rows), pl.ds(left, width)]
+        if self.quarter == "rows":
+            half = self.rows // 2
+            return self.whole.at[pl.ds(pl.multiple_of(start + part * half, 16), half), pl.ds(left, width)]
+        half = width // 2
+        return self.whole.at[pl.ds(start, self.rows), pl.ds(pl.multiple_of(left + part * half, 128), half)]
+
+    def copy(self, kind, far, block, core, part, device):
+        region = self.region(block, core, part)
+        return pltpu.make_async_remote_copy(
+            src_ref=region,
+            dst_ref=region,
+            send_sem=self.sems.at[0, kind, far],
+            recv_sem=self.sems.at[1, kind, far],
+            device_id=device,
+            device_id_type=MESH,
+        )
+
+    def transfers(self, far):
+        x, y, z, c = self.x, self.y, self.z, self.core
+        own = chip(x, y, far)
+        by_x, by_y, across = chip(1 - x, y, far), chip(x, 1 - y, far), chip(1 - x, 1 - y, far)
+        mate = (1 - c, chip(x, y, z))
+        to_x, to_y = (c, chip(1 - x, y, z)), (c, chip(x, 1 - y, z))
+        return {
+            UP: (own, None, (c, chip(x, y, z + 1))),
+            DOWN: (own, None, (c, chip(x, y, z - 1))),
+            SIDE_X: (own, None, to_x),
+            SIDE_Y: (own, None, to_y),
+            HALF_X: (by_y, 1, to_x),
+            HALF_Y: (by_x, 0, to_y),
+            MATE_Z: (own, None, mate),
+            MATE_X: (by_x, None, mate),
+            MATE_Y: (by_y, None, mate),
+            MATE_HX: (across, 1, mate),
+            MATE_HY: (across, 0, mate),
+        }
+
+    def send(self, kind, far):
+        block, part, device = self.transfers(far)[kind]
+        self.copy(kind, far, block, self.core, part, device).start()
+
+    def sent(self, kind, far):
+        block, part, device = self.transfers(far)[kind]
+        self.copy(kind, far, block, self.core, part, device).wait_send()
+
+    def arrived(self, kind, far):
+        x, y = self.x, self.y
+        block, part, core = {
+            UP: (chip(x, y, far), None, 0),
+            DOWN: (chip(x, y, far), None, 0),
+            SIDE_X: (chip(1 - x, y, far), None, 0),
+            SIDE_Y: (chip(x, 1 - y, far), None, 0),
+            HALF_X: (chip(1 - x, 1 - y, far), 1, 0),
+            HALF_Y: (chip(1 - x, 1 - y, far), 0, 0),
+            MATE_Z: (chip(x, y, far), None, 1),
+            MATE_X: (chip(1 - x, y, far), None, 1),
+            MATE_Y: (chip(x, 1 - y, far), None, 1),
+            MATE_HX: (chip(1 - x, 1 - y, far), 1, 1),
+            MATE_HY: (chip(1 - x, 1 - y, far), 0, 1),
+        }[kind]
+        owner = self.core if core == 0 else 1 - self.core
+        self.copy(kind, far, block, owner, part, (1 - self.core, chip(x, y, self.z))).wait_recv()
+
+    def each(self, distance, act):
+        for sign in (-1, 1) if distance else (1,):
+            far = self.z + sign * distance
+            if distance:
+                pl.when(jnp.logical_and(far >= 0, far < self.planes))(functools.partial(act, far, sign))
+            else:
+                act(far, sign)
+
+    def column(self, distance):
+        def act(far, sign):
+            if distance:
+                self.arrived(UP if sign < 0 else DOWN, far)
+            if sign < 0 or not distance:
+                pl.when(self.z < self.planes - 1)(lambda: self.send(UP, far))
+            if sign > 0:
+                pl.when(self.z > 0)(lambda: self.send(DOWN, far))
+            self.send(SIDE_X, far)
+            self.send(SIDE_Y, far)
+            if distance:
+                self.send(MATE_Z, far)
+
+        self.each(distance, act)
+
+    def sides(self, distance):
+        def act(far, sign):
+            self.arrived(SIDE_X, far)
+            self.send(HALF_Y, far)
+            self.send(MATE_X, far)
+            self.arrived(SIDE_Y, far)
+            self.send(HALF_X, far)
+            self.send(MATE_Y, far)
+
+        self.each(distance, act)
+
+    def diagonal(self, distance):
+        def act(far, sign):
+            self.arrived(HALF_Y, far)
+            self.send(MATE_HY, far)
+            self.arrived(HALF_X, far)
+            self.send(MATE_HX, far)
+
+        self.each(distance, act)
+
+    def finish(self):
+        for distance in range(self.planes):
+
+            def act(far, sign):
+                if sign < 0 or not distance:
+                    pl.when(self.z < self.planes - 1)(lambda: self.sent(UP, far))
+                if sign > 0:
+                    pl.when(self.z > 0)(lambda: self.sent(DOWN, far))
+                for kind in (SIDE_X, SIDE_Y, HALF_X, HALF_Y, MATE_X, MATE_Y, MATE_HX, MATE_HY):
+                    self.sent(kind, far)
+                for kind in (MATE_X, MATE_Y, MATE_HX, MATE_HY):
+                    self.arrived(kind, far)
+                if distance:
+                    self.sent(MATE_Z, far)
+                    self.arrived(MATE_Z, far)
+
+            self.each(distance, act)
+
+    def steps(self):
+        do = [lambda: self.column(0), lambda: self.column(1), lambda: self.sides(0), lambda: self.column(2), lambda: self.diagonal(0),
+              lambda: self.sides(1), lambda: self.column(3), lambda: self.diagonal(1), lambda: self.sides(2), lambda: self.diagonal(2),
+              lambda: self.sides(3), lambda: self.diagonal(3)]
+        return do
+
+
+def gather_sems(planes):
+    return pltpu.SemaphoreType.DMA((2, 11, planes))
+
+
+class Reduce:
+    X, Y, HX, HY, RISE, FALL, MATE, LAST = range(8)
+
+    @staticmethod
+    def scratch(rows, width, quarter, planes):
+        half = width // 2
+        corner = (rows // 2, half) if quarter == "rows" else (rows, half // 2)
+        bf16 = jnp.bfloat16
+        return [
+            pltpu.VMEM((4 * planes * rows, half), bf16),
+            pltpu.VMEM((4, planes, rows, half), bf16),
+            pltpu.VMEM((2, planes) + corner, bf16),
+            pltpu.SemaphoreType.DMA((2, 8, planes)),
+        ]
+
+    def __init__(self, part, out, rows, quarter, scratch, planes):
+        self.part, self.out, self.rows, self.quarter, self.planes = part, out, rows, quarter, planes
+        self.mate_in, self.side_in, self.corner_in, self.sems = scratch
+        self.x, self.y, self.z, self.core = place()
+        self.half = part.shape[1] // 2
+
+    def block(self, owner, part=None):
+        start = pl.multiple_of(owner * self.rows, 16)
+        left = pl.multiple_of(self.core * self.half, 128)
+        if part is None:
+            return pl.ds(start, self.rows), pl.ds(left, self.half)
+        if self.quarter == "rows":
+            return pl.ds(pl.multiple_of(start + part * (self.rows // 2), 16), self.rows // 2), pl.ds(left, self.half)
+        quarter = self.half // 2
+        return pl.ds(start, self.rows), pl.ds(pl.multiple_of(left + part * quarter, 128), quarter)
+
+    def copy(self, kind, far, source, target, device):
+        return pltpu.make_async_remote_copy(
+            src_ref=source,
+            dst_ref=target,
+            send_sem=self.sems.at[0, kind, far],
+            recv_sem=self.sems.at[1, kind, far],
+            device_id=device,
+            device_id_type=MESH,
+        )
+
+    def move(self, kind, far):
+        x, y, z, c = self.x, self.y, self.z, self.core
+        part = self.part
+        to_x, to_y, mate = (c, chip(1 - x, y, z)), (c, chip(x, 1 - y, z)), (1 - c, chip(x, y, z))
+        if kind == self.X:
+            return self.copy(kind, far, part.at[self.block(chip(1 - x, y, far))], self.side_in.at[0, far], to_x)
+        if kind == self.Y:
+            return self.copy(kind, far, part.at[self.block(chip(x, 1 - y, far))], self.side_in.at[1, far], to_y)
+        if kind == self.HX:
+            return self.copy(kind, far, part.at[self.block(chip(1 - x, 1 - y, far), 0)], self.corner_in.at[0, far], to_x)
+        if kind == self.HY:
+            return self.copy(kind, far, part.at[self.block(chip(1 - x, 1 - y, far), 1)], self.corner_in.at[1, far], to_y)
+        if kind == self.RISE:
+            return self.copy(kind, far, part.at[self.block(chip(x, y, far))], self.side_in.at[2, far], (c, chip(x, y, z + 1)))
+        if kind == self.FALL:
+            return self.copy(kind, far, part.at[self.block(chip(x, y, far))], self.side_in.at[3, far], (c, chip(x, y, z - 1)))
+        if kind == self.MATE:
+            rows = pl.ds(pl.multiple_of(far * 4 * self.rows, 16), 4 * self.rows)
+            left = pl.multiple_of((1 - c) * self.half, 128)
+            return self.copy(kind, far, part.at[rows, pl.ds(left, self.half)], self.mate_in.at[rows], mate)
+        left = pl.multiple_of(c * self.half, 128)
+        region = self.out.at[:, pl.ds(left, self.half)]
+        return self.copy(kind, 0, region, region, mate)
+
+    def add(self, at, *refs):
+        total = self.part[at].astype(jnp.float32)
+        for ref in refs:
+            total = total + ref[...].astype(jnp.float32)
+        self.part[at] = low(total)
+
+    def each(self, distance, act):
+        for sign in (-1, 1) if distance else (1,):
+            far = self.z + sign * distance
+            if distance:
+                pl.when(jnp.logical_and(far >= 0, far < self.planes))(functools.partial(act, far, sign))
+            else:
+                act(far, sign)
+
+    def start(self, distance):
+        self.each(distance, lambda far, sign: self.move(self.MATE, far).start())
+
+    def fold(self, distance):
+        def act(far, sign):
+            self.move(self.MATE, far).wait_recv()
+
+            def rows(k, carry):
+                start = pl.multiple_of((far * 4 + k) * self.rows, 16)
+                left = pl.multiple_of(self.core * self.half, 128)
+                self.add((pl.ds(start, self.rows), pl.ds(left, self.half)), self.mate_in.at[pl.ds(start, self.rows)])
+                return carry
+
+            lax.fori_loop(0, 4, rows, 0)
+            self.move(self.HX, far).start()
+            self.move(self.HY, far).start()
+
+        self.each(distance, act)
+
+    def sides(self, distance):
+        x, y = self.x, self.y
+
+        def act(far, sign):
+            self.move(self.HX, far).wait_recv()
+            self.add(self.block(chip(x, 1 - y, far), 0), self.corner_in.at[0, far])
+            self.move(self.Y, far).start()
+            self.move(self.HY, far).wait_recv()
+            self.add(self.block(chip(1 - x, y, far), 1), self.corner_in.at[1, far])
+            self.move(self.X, far).start()
+
+        self.each(distance, act)
+
+    def column(self, distance):
+        x, y, z = self.x, self.y, self.z
+
+        def act(far, sign):
+            self.move(self.X, far).wait_recv()
+            self.move(self.Y, far).wait_recv()
+            at = self.block(chip(x, y, far))
+            if distance:
+                self.add(at, self.side_in.at[0, far], self.side_in.at[1, far])
+                if sign > 0:
+
+                    @pl.when(z > 0)
+                    def _():
+                        self.move(self.RISE, far).wait_recv()
+                        self.add(at, self.side_in.at[2, far])
+
+                    self.move(self.RISE, far).start()
+                else:
+
+                    @pl.when(z < self.planes - 1)
+                    def _():
+                        self.move(self.FALL, far).wait_recv()
+                        self.add(at, self.side_in.at[3, far])
+
+                    self.move(self.FALL, far).start()
+                return
+            total = self.part[at].astype(jnp.float32)
+            total = total + self.side_in[0, far].astype(jnp.float32) + self.side_in[1, far].astype(jnp.float32)
+            left = pl.multiple_of(self.core * self.half, 128)
+            here = (slice(None), pl.ds(left, self.half))
+            self.out[here] = total
+
+            @pl.when(z > 0)
+            def _():
+                self.move(self.RISE, far).wait_recv()
+                self.out[here] = self.out[here] + self.side_in[2, far].astype(jnp.float32)
+
+            @pl.when(z < self.planes - 1)
+            def _():
+                self.move(self.FALL, far).wait_recv()
+                self.out[here] = self.out[here] + self.side_in[3, far].astype(jnp.float32)
+
+            self.move(self.LAST, 0).start()
+
+        self.each(distance, act)
+
+    def finish(self):
+        last = self.move(self.LAST, 0)
+        left = pl.multiple_of((1 - self.core) * self.half, 128)
+        region = self.out.at[:, pl.ds(left, self.half)]
+        self.copy(self.LAST, 0, region, region, (1 - self.core, chip(self.x, self.y, self.z))).wait_recv()
+        last.wait_send()
+        for distance in range(self.planes):
+
+            def act(far, sign):
+                for kind in (self.MATE, self.HX, self.HY, self.X, self.Y):
+                    self.move(kind, far).wait_send()
+                if distance:
+                    self.move(self.RISE if sign > 0 else self.FALL, far).wait_send()
+
+            self.each(distance, act)
+
+    def steps(self):
+        top = self.planes - 1
+        do = [functools.partial(self.start, d) for d in range(top, -1, -1)]
+        do += [functools.partial(self.fold, d) for d in range(top, -1, -1)]
+        for d in range(top, -1, -1):
+            do += [functools.partial(self.sides, d)]
+            if d < top:
+                do += [functools.partial(self.column, d + 1)]
+        return do + [functools.partial(self.column, 0)]
+
+
+class Chain:
+    CUT = 3
+
+    @staticmethod
+    def scratch():
+        half = pltpu.VMEM((N, DI // 2), jnp.bfloat16)
+        wide = pltpu.VMEM((N, DI // 2), jnp.float32)
+        return [half, half, half, half, half, half, wide, wide, pltpu.SemaphoreType.DMA((2, 2 + Chain.CUT))]
+
+    def __init__(self, part, result, factors, scratch, lead, planes):
+        self.part, self.result, self.factors, self.lead, self.planes = part, result, factors, lead, planes
+        self.give, self.take, self.leave, self.come, self.back, self.again, self.total, self.front, self.sems = scratch
+        self.x, self.y, self.z, self.core = place()
+        self.half = DI // 2
+        self.leads = self.core == lead
+        self.ahead = 1 if lead == 0 else -1
+        self.first = self.z == (0 if lead == 0 else planes - 1)
+        self.last = self.z == (planes - 1 if lead == 0 else 0)
+
+    def own(self):
+        return pl.ds(pl.multiple_of(self.core * self.half, 128), self.half)
+
+    def other(self):
+        return pl.ds(pl.multiple_of((1 - self.core) * self.half, 128), self.half)
+
+    def copy(self, k, source, target, device):
+        return pltpu.make_async_remote_copy(
+            src_ref=source,
+            dst_ref=target,
+            send_sem=self.sems.at[0, k],
+            recv_sem=self.sems.at[1, k],
+            device_id=device,
+            device_id_type=MESH,
+        )
+
+    def mate(self):
+        return (1 - self.core, chip(self.x, self.y, self.z))
+
+    def trade(self):
+        return self.copy(0, self.give, self.take, self.mate())
+
+    def returned(self):
+        return self.copy(1, self.back, self.again, self.mate())
+
+    def hop(self, k):
+        cut = self.half // self.CUT
+        at = (slice(None), pl.ds(k * cut, cut))
+        return self.copy(
+            2 + k, self.leave.at[at], self.come.at[at], (self.core, chip(self.x, self.y, self.z + self.ahead))
+        )
+
+    def start(self):
+        self.give[...] = low(self.part[:, self.other()])
+        self.trade().start()
+
+    def rows(self):
+        return self.factors[self.lead, 0:1, self.own()], self.factors[1 - self.lead, 0:1, self.own()]
+
+    def merge(self):
+        self.trade().wait_recv()
+        own = self.part[:, self.own()]
+        got = self.take[...].astype(jnp.float32)
+        ahead, behind = jnp.where(self.leads, own, got), jnp.where(self.leads, got, own)
+        _, following = self.rows()
+        self.front[...] = ahead
+        self.total[...] = following * ahead + behind
+
+        @pl.when(self.first)
+        def _():
+            self.come[...] = jnp.zeros(self.come.shape, self.come.dtype)
+            self.leave[...] = low(self.total[...])
+            for k in range(self.CUT):
+                self.hop(k).start()
+
+    def pass_on(self):
+        leading, following = self.rows()
+        cut = self.half // self.CUT
+
+        @pl.when(jnp.logical_not(self.first))
+        def _():
+            for k in range(self.CUT):
+                self.hop(k).wait_recv()
+
+                @pl.when(jnp.logical_not(self.last))
+                def _():
+                    at = (slice(None), slice(k * cut, (k + 1) * cut))
+                    both = (leading * following)[:, k * cut : (k + 1) * cut]
+                    self.leave[at] = low(both * self.come[at].astype(jnp.float32) + self.total[at])
+                    self.hop(k).start()
+
+        came = self.come[...].astype(jnp.float32)
+        later = low(leading * came + self.front[...])
+        self.back[...] = jnp.where(self.leads, later.astype(jnp.float32), came).astype(jnp.bfloat16)
+        self.returned().start()
+        self.result[:, self.own()] = jnp.where(self.leads, came, later.astype(jnp.float32)).astype(jnp.bfloat16)
+
+    def close(self):
+        self.returned().wait_recv()
+        self.result[:, self.other()] = self.again[...]
+
+    def finish(self):
+        self.trade().wait_send()
+        self.returned().wait_send()
+
+        @pl.when(jnp.logical_not(self.last))
+        def _():
+            for k in range(self.CUT):
+                self.hop(k).wait_send()
+
+
+VMEM = pl.BlockSpec(memory_space=pltpu.VMEM)
+ROWS = 256
+HALO = 16
+WIDE = 2048
+TRANS = (((0,), (0,)), ((), ()))
+TRANS_B = (((1,), (1,)), ((), ()))
+
+
+def dot(a, b, dims=(((1,), (0,)), ((), ()))):
+    return lax.dot_general(a, b, dims, preferred_element_type=jnp.float32)
+
+
+def low(a):
+    return a.astype(jnp.bfloat16)
+
+
+class Shuffle:
+    def __init__(self, source, target, sems, offset=0, back=False):
+        self.source, self.target, self.sems, self.offset, self.back = source, target, sems, offset, back
+        self.x, self.y, self.z, self.core = place()
+
+    def piece(self, k):
+        x, y, z, c = self.x, self.y, self.z, self.core
+        rows = 128
+        if self.back:
+            source = self.source.at[pl.ds(rows * k, rows)]
+            target = self.target.at[x]
+        else:
+            source = self.source.at[k]
+            if len(self.target.shape) == len(self.source.shape):
+                target = self.target.at[self.offset + x]
+            else:
+                target = self.target.at[pl.ds(pl.multiple_of(self.offset + rows * x, 16), rows)]
+        stays = jnp.logical_and(x == k, y == c)
+        local = pltpu.make_async_copy(source, target, self.sems.at[1, x])
+        remote = pltpu.make_async_remote_copy(
+            src_ref=source,
+            dst_ref=target,
+            send_sem=self.sems.at[0, k],
+            recv_sem=self.sems.at[1, x],
+            device_id=(y, chip(k, c, z)),
+            device_id_type=MESH,
+        )
+        return stays, local, remote
+
+    def start(self):
+        for k in range(2):
+            stays, local, remote = self.piece(k)
+            pl.when(stays)(local.start)
+            pl.when(jnp.logical_not(stays))(remote.start)
+
+    def arrived(self):
+        x, y, z, c = self.x, self.y, self.z, self.core
+        for k in range(2):
+            if self.back:
+                target = self.target.at[k]
+            elif len(self.target.shape) == len(self.source.shape):
+                target = self.target.at[self.offset + k]
+            else:
+                target = self.target.at[pl.ds(self.offset + 128 * k, 128)]
+            stays = jnp.logical_and(x == k, y == c)
+            local = pltpu.make_async_copy(target, target, self.sems.at[1, k])
+            remote = pltpu.make_async_remote_copy(
+                src_ref=target,
+                dst_ref=target,
+                send_sem=self.sems.at[0, k],
+                recv_sem=self.sems.at[1, k],
+                device_id=(y, chip(k, c, z)),
+                device_id_type=MESH,
+            )
+            pl.when(stays)(local.wait)
+            pl.when(jnp.logical_not(stays))(remote.wait_recv)
+
+    def finish(self):
+        for k in range(2):
+            stays, local, remote = self.piece(k)
+            pl.when(jnp.logical_not(stays))(remote.wait_send)
+
+
+class Before:
+    def __init__(self, source, target, sems, planes):
+        self.source, self.target, self.sems, self.planes = source, target, sems, planes
+        self.x, self.y, self.z, self.core = place()
+
+    def piece(self, m):
+        x, y, z, c = self.x, self.y, self.z, self.core
+        source = self.source(m)
+        return pltpu.make_async_remote_copy(
+            src_ref=source,
+            dst_ref=self.target,
+            send_sem=self.sems.at[0, m],
+            recv_sem=self.sems.at[1, 0],
+            device_id=(1 - y, chip(m, c, z + y)),
+            device_id_type=MESH,
+        )
+
+    def when_sending(self):
+        return jnp.logical_and(self.x == 1, jnp.logical_or(self.y == 0, self.z < self.planes - 1))
+
+    def start(self):
+        @pl.when(self.when_sending())
+        def _():
+            for m in range(2):
+                self.piece(m).start()
+
+    def arrived(self):
+        pl.when(self.z + self.core > 0)(self.piece(0).wait_recv)
+
+    def finish(self):
+        @pl.when(self.when_sending())
+        def _():
+            for m in range(2):
+                self.piece(m).wait_send()
+
+
+class ToAll:
+    def __init__(self, table, sems, planes):
+        self.table, self.sems, self.count = table, sems, planes * 4
+        self.me, self.core = lax.axis_index("seq"), lax.axis_index("dp")
+
+    def copy(self, block, other):
+        return pltpu.make_async_remote_copy(
+            src_ref=self.table.at[block],
+            dst_ref=self.table.at[block],
+            send_sem=self.sems.at[0, other],
+            recv_sem=self.sems.at[1, block],
+            device_id=(self.core, other),
+            device_id_type=MESH,
+        )
+
+    def over(self, act):
+        def one(k, carry):
+            act(lax.rem(self.me + k, self.count))
+            return carry
+
+        lax.fori_loop(1, self.count, one, 0)
+
+    def start(self):
+        self.over(lambda other: self.copy(self.me, other).start())
+
+    def arrived(self):
+        self.over(lambda other: self.copy(other, self.me).wait_recv())
+
+    def finish(self):
+        self.over(lambda other: self.copy(self.me, other).wait_send())
+
+
+def enter_kernel(
+    planes, tok_ref, seg_ref, small_ref, wa_ref,
+    whole, table, tok, seg, normed_ref, proj_ref, conv_ref, gain_ref, ngain_ref,
+    normed_all, gather_sem, tok_sem, seg_sem, end_sem, segend_sem, small_sem,
+):
+    at = lax.axis_index("seq")
+    x, y, z, c = place()
+    whole[pl.ds(pl.multiple_of(at * 48, 16), 48), :] = wa_ref[...]
+    table[at] = small_ref[...]
+
+    @pl.when(z + c == 0)
+    def _():
+        tok[0:HALO, :] = jnp.zeros((HALO, tok.shape[1]), tok.dtype)
+        seg[0] = jnp.full((8, 128), -1.0, jnp.float32)
+
+    gather = Gather(whole, 48, "columns", gather_sem, planes)
+    tokens = Shuffle(tok_ref, tok, tok_sem, HALO)
+    numbers = Shuffle(seg_ref, seg, seg_sem, 1)
+    ends = Before(lambda m: tok_ref.at[m, pl.ds(128 - HALO, HALO)], tok.at[pl.ds(0, HALO)], end_sem, planes)
+    segends = Before(lambda m: seg_ref.at[m], seg.at[0], segend_sem, planes)
+    small = ToAll(table, small_sem, planes)
+    meet_all(planes)
+    moves = [tokens, ends, numbers, segends, small]
+    for move in moves:
+        move.start()
+    steps = gather.steps()
+    for step in steps[:3]:
+        step()
+    for move in moves:
+        move.arrived()
+    conv_ref[...] = jnp.concatenate([table[k, :, 0:112] for k in range(16)], axis=1)
+    gate = jnp.concatenate([table[k, :, 0:96] for k in range(16)], axis=1)
+    gain_ref[...] = gate
+    ngain_ref[...] = jnp.concatenate([table[k, :, 0:48] for k in range(16)], axis=1)
+    gain = ngain_ref[5:6, :]
+    u = tok[...].astype(jnp.float32)
+    r = lax.rsqrt(jnp.mean(u * u, axis=-1, keepdims=True) + EPSILON)
+    normed_all[...] = low(u * r * gain)
+    normed_ref[...] = normed_all[HALO:, :]
+    for step in steps[3:]:
+        step()
+    gather.finish()
+    for move in moves:
+        move.finish()
+
+    def columns(k, carry):
+        at_k = pl.ds(pl.multiple_of(k * 512, 512), 512)
+        proj_ref[:, at_k] = dot(normed_all[...], whole[:, at_k])
+        return carry
+
+    lax.fori_loop(0, WIDE // 512, columns, 0)
+
+
+def enter(tokens, segf, small, wa, planes):
+    f32, bf16 = jnp.float32, jnp.bfloat16
+    shape = jax.ShapeDtypeStruct
+    two = pltpu.SemaphoreType.DMA((2, 2))
+    return pl.pallas_call(
+        functools.partial(enter_kernel, planes),
+        out_shape=[
+            shape((768, WIDE), bf16),
+            shape((16, 8, 128), f32),
+            shape((HALO + ROWS, 768), bf16),
+            shape((3, 8, 128), f32),
+            shape((ROWS, 768), bf16),
+            shape((HALO + ROWS, WIDE), f32),
+            shape((8, CH), f32),
+            shape((8, DI), f32),
+            shape((8, 768), f32),
+        ],
+        in_specs=[VMEM] * 4,
+        out_specs=[VMEM] * 9,
+        scratch_shapes=[
+            pltpu.VMEM((HALO + ROWS, 768), bf16),
+            gather_sems(planes), two, two, two, two,
+            pltpu.SemaphoreType.DMA((2, 16)),
+        ],
+        compiler_params=pltpu.CompilerParams(collective_id=0, has_side_effects=True, vmem_limit_bytes=48 << 20),
+    )(tokens, segf, small, wa)
+
+
+TILE = 128
+TILES = DI // TILE
+
+
+class Names:
+    def __init__(self, names, refs):
+        for name, ref in zip(names, refs, strict=True):
+            setattr(self, name, ref)
+
+
+def at_tile(j):
+    return pl.ds(pl.multiple_of(j * TILE, TILE), TILE)
+
+
+def at_rows(k, rows):
+    return pl.ds(pl.multiple_of(k * rows, rows), rows)
+
+
+def loop(low_end, high_end, act):
+    def one(k, carry):
+        act(k)
+        return carry
+
+    lax.fori_loop(low_end, high_end, one, 0)
+
+
+def iota(shape, dim):
+    return lax.broadcasted_iota(jnp.int32, shape, dim)
+
+
+def pieces(a):
+    high = low(a)
+    rest = a - high.astype(jnp.float32)
+    middle = low(rest)
+    return high, middle, low(rest - middle.astype(jnp.float32))
+
+
+def packed(a):
+    a = jnp.where(iota(a.shape, 1) < H, a, 0.0)
+    high, middle, rest = (part.astype(jnp.float32) for part in pieces(a))
+    return low(high + pltpu.roll(middle, 32, 1) + pltpu.roll(rest, 64, 1))
+
+
+def spread_matrix(width, first=0):
+    row, col = iota((128, width), 0), iota((128, width), 1) + first
+    return low(jnp.where(jnp.logical_and(row % 32 == col // P_SIZE, row < 96), 1.0, 0.0))
+
+
+def head_sums(a, j):
+    row, col = iota((TILE, 128), 0), iota((TILE, 128), 1)
+    pick = low(jnp.where(row // P_SIZE + 2 * j == col, 1.0, 0.0))
+    high, middle, rest = pieces(a)
+    return dot(high, pick) + dot(middle, pick) + dot(rest, pick)
+
+
+def sigmoid(v):
+    return 1.0 / (1.0 + jnp.exp(-v))
+
+
+REST_IN = ["wa", "tok", "seg", "normed", "proj", "conv", "gain", "ngain", "heads", "wz", "wout", "cot"]
+REST_OUT = ["act_out", "tokens_out", "grad_a", "grad_z", "grad_out", "small_out"]
+
+
+def rest_scratch(planes):
+    f32, bf16 = jnp.float32, jnp.bfloat16
+    v = pltpu.VMEM
+    dma = pltpu.SemaphoreType.DMA
+    two = dma((2, 2))
+    return {
+        "wz_full": v((768, DI), bf16), "wout_full": v((DI, 768), bf16), "wz_sem": gather_sems(planes), "wout_sem": gather_sems(planes),
+        "cot_own": v((ROWS, 768), bf16), "cot_sem": two, "act_sem": two, "back_sem": two,
+        "segcol": v((384, 128), f32), "same": v((KC, ROWS + HALO, 128), f32),
+        "pre": v((ROWS, CH), f32), "inner": v((ROWS, DI), f32), "bproj": v((ROWS, N), bf16), "cproj": v((ROWS, N), bf16),
+        "cumt": v((H, 8, ROWS), f32), "bar": v((ROWS, ROWS), f32), "scores": v((ROWS, ROWS), f32),
+        "step": v((ROWS, 128), f32), "cum": v((ROWS, 128), f32), "ein": v((ROWS, 128), f32), "eout": v((ROWS, 128), f32),
+        "stepx": v((ROWS, DI), f32), "einx": v((ROWS, DI), f32), "eoutx": v((ROWS, DI), f32), "cumx": v((ROWS, DI), f32),
+        "xs": v((ROWS, DI), bf16), "xso": v((ROWS, DI), bf16),
+        "part": v((N, DI), f32), "factors": v((2, 8, DI), f32), "factor_sem": dma((2,)), "skipx": v((8, DI), f32),
+        "state": v((N, DI), bf16), "dstate": v((N, DI), bf16),
+        "y": v((ROWS, DI), f32), "z": v((ROWS, DI), f32), "gated": v((ROWS, DI), bf16), "act_own": v((ROWS, 768), bf16),
+        "dz": v((ROWS, DI), bf16), "dy": v((ROWS, DI), bf16), "dyin": v((ROWS, DI), bf16),
+        "ggain": v((8, DI), f32), "gskip": v((8, DI), f32),
+        "dscores": v((ROWS, ROWS), f32), "dxs": v((ROWS, DI), f32), "sums": v((3, ROWS, 128), f32),
+        "dpre": v((ROWS + HALO, CH), f32), "dx": v((ROWS, WIDE), bf16), "tail": v((8, CH), f32), "tail_in": v((8, CH), f32), "tail_sem": dma((2,)),
+        "gconv": v((8, CH), f32), "gtok": v((ROWS, 768), bf16),
+        "table": v((16, 8, 128), f32), "inbox": v((2, 16, 8, 128), f32), "table_sem": dma((2, 2, 16)),
+        "part_a": v((768, WIDE), bf16), "part_z": v((768, DI), bf16), "part_out": v((DI, 768), bf16),
+    }
+
+
+def rest_kernel(planes, names, *refs):
+    r = Names(REST_IN + REST_OUT + names, refs[: len(REST_IN) + len(REST_OUT) + len(names)])
+    extra = list(refs[len(REST_IN) + len(REST_OUT) + len(names) :])
+    chain_f, chain_b = extra[0:9], extra[9:18]
+    red_a, red_z, red_out = extra[18:22], extra[22:26], extra[26:30]
+    x, y, z, c = place()
+    me = chip(x, y, z)
+    mate = (1 - c, me)
+    f32 = jnp.float32
+    r.wz_full[pl.ds(pl.multiple_of(me * 48, 16), 48), :] = r.wz[...]
+    r.wout_full[pl.ds(pl.multiple_of(me * 96, 16), 96), :] = r.wout[...]
+    gather_z = Gather(r.wz_full, 48, "columns", r.wz_sem, planes)
+    gather_out = Gather(r.wout_full, 96, "rows", r.wout_sem, planes)
+    cots = Shuffle(r.cot, r.cot_own, r.cot_sem)
+    meet_all(planes)
+    cots.start()
+    waiting = [step for pair in zip(gather_z.steps(), gather_out.steps()) for step in pair]
+
+    def background(count):
+        for _ in range(min(count, len(waiting))):
+            waiting.pop(0)()
+
+    background(2)
+
+    for k in range(3):
+        r.segcol[128 * k : 128 * k + 128, :] = jnp.transpose(jnp.broadcast_to(r.seg[k, 0:1, :], (128, 128)))
+    seg = r.segcol[128:384, :]
+    for k in range(KC):
+        r.same[k] = jnp.zeros((ROWS + HALO, 128), f32)
+        r.same[k, 8 : 8 + ROWS, :] = jnp.where(r.segcol[125 + k : 125 + k + ROWS, :] == seg, 1.0, 0.0)
+
+    def convolve(j):
+        at = at_tile(j)
+        total = jnp.broadcast_to(r.conv[4:5, at], (ROWS, TILE))
+        for k in range(KC):
+            total = total + r.conv[k : k + 1, at] * r.proj[13 + k : 13 + k + ROWS, at] * r.same[k, 8 : 8 + ROWS, :]
+        r.pre[:, at] = total
+        return total * sigmoid(total)
+
+    def inner(j):
+        r.inner[:, at_tile(j)] = convolve(j)
+
+    loop(0, TILES, inner)
+    r.bproj[...] = low(convolve(TILES))
+    r.cproj[...] = low(convolve(TILES + 1))
+    background(4)
+
+    raw = r.proj[HALO:, CH : CH + 128] + r.heads[0:1, :]
+    step = jnp.maximum(raw, 0.0) + jnp.log1p(jnp.exp(-jnp.abs(raw)))
+    rate = -jnp.exp(r.heads[1:2, :])
+    lower = jnp.where(iota((ROWS, ROWS), 0) >= iota((ROWS, ROWS), 1), 1.0, 0.0)
+    cum = jnp.dot(lower, step * rate, precision=HIGHEST, preferred_element_type=f32)
+    r.step[...] = step
+    r.cum[...] = cum
+    across = jnp.transpose(cum)
+    for h in range(H):
+        r.cumt[h] = jnp.broadcast_to(across[h : h + 1, :], (8, ROWS))
+    last = cum[ROWS - 1 : ROWS, :]
+    before = r.segcol[127:128, :]
+    first_seg, last_seg = seg[0:1, :], seg[ROWS - 1 : ROWS, :]
+    r.ein[...] = jnp.where(seg == before, jnp.exp(cum), 0.0)
+    r.eout[...] = jnp.where(seg == last_seg, jnp.exp(last - cum), 0.0)
+    through = jnp.logical_and(first_seg == last_seg, first_seg == before)
+    factor = jnp.where(through, jnp.exp(last), 0.0)
+    segrow = jnp.concatenate([r.seg[1, 0:1, :], r.seg[2, 0:1, :]], axis=1)
+    allowed = jnp.logical_and(jnp.concatenate([seg, seg], axis=1) == segrow, iota((ROWS, ROWS), 0) >= iota((ROWS, ROWS), 1))
+    r.bar[...] = jnp.where(allowed, 0.0, -1e30)
+    rows = packed(jnp.concatenate([jnp.broadcast_to(factor, (8, 128)), jnp.broadcast_to(r.heads[2:3, :], (8, 128))], axis=0))
+    both = dot(rows, spread_matrix(DI))
+    r.factors[c] = both[0:8, :]
+    r.skipx[...] = both[8:16, :]
+    share = pltpu.make_async_remote_copy(
+        src_ref=r.factors.at[c], dst_ref=r.factors.at[c], send_sem=r.factor_sem.at[0], recv_sem=r.factor_sem.at[1],
+        device_id=mate, device_id_type=MESH,
+    )
+    share.start()
+    spreads = [(r.stepx, packed(step)), (r.einx, packed(r.ein[...])), (r.eoutx, packed(r.eout[...])), (r.cumx, packed(cum))]
+    r.stepx[...] = dot(spreads[0][1], spread_matrix(DI))
+    r.einx[...] = dot(spreads[1][1], spread_matrix(DI))
+    r.eoutx[...] = dot(spreads[2][1], spread_matrix(DI))
+    r.cumx[...] = dot(spreads[3][1], spread_matrix(DI))
+
+    def outgoing(j):
+        at = at_tile(j)
+        scaled = r.stepx[:, at] * r.inner[:, at]
+        r.xs[:, at] = low(scaled)
+        xso = low(scaled * r.eoutx[:, at])
+        r.xso[:, at] = xso
+        r.part[:, at] = dot(r.bproj[...], xso, TRANS)
+
+    loop(0, TILES, outgoing)
+    forward = Chain(r.part, r.state, r.factors, chain_f, 0, planes)
+    forward.start()
+    r.scores[...] = dot(r.cproj[...], r.bproj[...], TRANS_B)
+    background(4)
+
+    first_half = iota((1, TILE), 1) < P_SIZE
+
+    def decays(j, band):
+        size = 128 * (band + 1)
+        rows = slice(128 * band, 128 * band + 128)
+        tile = r.cumx[rows, at_tile(j)]
+        turned = pltpu.roll(tile, P_SIZE, 1)
+        out = []
+        for k in range(2):
+            column = jnp.where(first_half, tile, turned) if k == 0 else jnp.where(first_half, turned, tile)
+            wide = column if band == 0 else jnp.concatenate([column, column], axis=1)
+            out.append(jnp.exp(wide - r.cumt[2 * j + k, 0:1, 0:size] + r.bar[rows, 0:size]))
+        return out
+
+    def halves(tile):
+        zero = jnp.zeros_like(tile)
+        return jnp.where(first_half, tile, zero), jnp.where(first_half, zero, tile)
+
+    def within(j):
+        at = at_tile(j)
+        for band in range(2):
+            size = 128 * (band + 1)
+            rows = slice(128 * band, 128 * band + 128)
+            inside = halves(r.xs[0:size, at])
+            total = 0.0
+            for decay, xs in zip(decays(j, band), inside):
+                total = total + dot(low(decay * r.scores[rows, 0:size]), xs)
+            r.y[rows, at] = total
+
+    def turn(chain, when):
+        for k in range(planes):
+            if when[k]:
+                position = k if chain.lead == 0 else planes - 1 - k
+                pl.when(z == position)(chain.pass_on)
+
+    loop(0, 2, within)
+    share.wait_recv()
+    forward.merge()
+    turn(forward, [1, 0, 0, 0])
+    loop(2, 5, within)
+    background(2)
+    turn(forward, [0, 1, 0, 0])
+    loop(5, 8, within)
+    background(4)
+    turn(forward, [0, 0, 1, 0])
+    loop(8, 12, within)
+    background(4)
+    turn(forward, [0, 0, 0, 1])
+    forward.close()
+
+    def carried(j):
+        at = at_tile(j)
+        r.y[:, at] = r.y[:, at] + r.einx[:, at] * dot(r.cproj[...], r.state[:, at])
+
+    loop(0, TILES, carried)
+    background(100)
+    gather_z.finish()
+    gather_out.finish()
+    cots.arrived()
+
+    def projections(j):
+        at = pl.ds(pl.multiple_of(j * 512, 512), 512)
+        r.z[:, at] = dot(r.normed[...], r.wz_full[:, at])
+        r.dxs[:, at] = dot(r.cot_own[...], r.wout_full[at, :], TRANS_B)
+
+    loop(0, 3, projections)
+    r.ggain[...] = jnp.zeros((8, DI), f32)
+    r.gskip[...] = jnp.zeros((8, DI), f32)
+
+    def gate(k):
+        rows = at_rows(k, 16)
+        inner, gate_in = r.inner[rows, :], r.z[rows, :]
+        mixed = r.y[rows, :] + r.skipx[0:1, :] * inner
+        sig = sigmoid(gate_in)
+        silu = gate_in * sig
+        v = mixed * silu
+        scale = lax.rsqrt(jnp.mean(v * v, axis=-1, keepdims=True) + EPSILON)
+        gain = r.gain[6:7, :]
+        r.gated[rows, :] = low(v * scale * gain)
+        dgated = r.dxs[rows, :]
+        weighed = dgated * (v * scale)
+        r.ggain[...] = r.ggain[...] + weighed[0:8, :] + weighed[8:16, :]
+        a = gain * dgated
+        dv = scale * (a - v * (scale * scale) * jnp.mean(v * a, axis=-1, keepdims=True))
+        dmixed = dv * silu
+        r.z[rows, :] = dmixed
+        r.dy[rows, :] = low(dmixed)
+        r.dyin[rows, :] = low(dmixed * r.einx[rows, :])
+        r.dz[rows, :] = low(dv * mixed * (sig * (1.0 + gate_in * (1.0 - sig))))
+        skip = dmixed * inner
+        r.gskip[...] = r.gskip[...] + skip[0:8, :] + skip[8:16, :]
+
+    loop(0, ROWS // 16, gate)
+
+    def incoming(j):
+        at = at_tile(j)
+        r.part[:, at] = dot(r.cproj[...], r.dyin[:, at], TRANS)
+
+    loop(0, TILES, incoming)
+    backward = Chain(r.part, r.dstate, r.factors, chain_b, 1, planes)
+    backward.start()
+
+    def weights(j):
+        at = at_rows(j, 256)
+        r.part_out[at, :] = low(dot(r.gated[:, at], r.cot_own[...], TRANS))
+        r.part_z[:, at] = low(dot(r.normed[...], r.dz[:, at], TRANS))
+
+    loop(0, 2, weights)
+    backward.merge()
+    turn(backward, [1, 0, 0, 0])
+    loop(2, 6, weights)
+    turn(backward, [0, 1, 0, 0])
+    reduce_out = Reduce(r.part_out, r.grad_out, 96, "rows", red_out, planes)
+    reduce_z = Reduce(r.part_z, r.grad_z, 48, "columns", red_z, planes)
+    waiting.extend(step for pair in zip(reduce_out.steps(), reduce_z.steps()) for step in pair)
+    background(8)
+
+    def project_out(k):
+        rows = at_rows(k, 64)
+        branch = dot(r.gated[rows, :], r.wout_full[...])
+        r.act_own[rows, :] = low(r.tok[pl.ds(pl.multiple_of(HALO + k * 64, 16), 64), :].astype(f32) + branch)
+
+    loop(0, 4, project_out)
+    acts = Shuffle(r.act_own, r.act_out, r.act_sem, back=True)
+    acts.start()
+    turn(backward, [0, 0, 1, 0])
+
+    r.dscores[...] = jnp.zeros((ROWS, ROWS), f32)
+    r.sums[...] = jnp.zeros((3, ROWS, 128), f32)
+
+    def within_back(j):
+        at = at_tile(j)
+        upper = lower = 0.0
+        for band in range(2):
+            size = 128 * (band + 1)
+            rows = slice(128 * band, 128 * band + 128)
+            xs = r.xs[0:size, at]
+            grads = 0.0
+            for decay, dy in zip(decays(j, band), halves(r.dy[rows, at])):
+                weight = low(decay * r.scores[rows, 0:size])
+                grads = grads + decay * dot(dy, xs, TRANS_B)
+                upper = upper + dot(weight[:, 0:128], dy, TRANS)
+                if band:
+                    lower = lower + dot(weight[:, 128:256], dy, TRANS)
+            r.dscores[rows, 0:size] = r.dscores[rows, 0:size] + grads
+        r.dxs[0:128, at] = upper
+        r.dxs[128:256, at] = lower
+        gain = r.dy[:, at].astype(f32) * r.y[:, at] - r.xs[:, at].astype(f32) * r.dxs[:, at]
+        r.sums[0] = r.sums[0] + head_sums(gain, j)
+
+    loop(0, 3, within_back)
+    turn(backward, [0, 0, 0, 1])
+    background(6)
+    loop(3, 6, within_back)
+    backward.close()
+    background(6)
+    loop(6, 9, within_back)
+    background(4)
+    loop(9, 12, within_back)
+    background(4)
+
+    def last_sums(j):
+        at = at_tile(j)
+        xs = r.xs[:, at].astype(f32)
+        far = r.eoutx[:, at] * dot(r.bproj[...], r.dstate[:, at])
+        total = r.dxs[:, at] + far
+        r.sums[1] = r.sums[1] + head_sums(xs * far, j)
+        inner = r.inner[:, at]
+        r.sums[2] = r.sums[2] + head_sums(inner * total, j)
+        r.dxs[:, at] = r.skipx[0:1, at] * r.z[:, at] + r.stepx[:, at] * total
+
+    loop(0, TILES, last_sums)
+    dscores = low(r.dscores[...])
+    dbproj = dot(dscores, r.cproj[...], TRANS) + dot(r.xso[...], r.dstate[...], TRANS_B)
+    dcproj = dot(dscores, r.bproj[...]) + dot(r.dyin[...], r.state[...], TRANS_B)
+    pick = jnp.where(iota((DI, 128), 0) // P_SIZE == iota((DI, 128), 1), 1.0, 0.0)
+    crossing = jnp.sum(r.dstate[...].astype(f32) * r.state[...].astype(f32), axis=0, keepdims=True) * r.factors[c, 0:1, :]
+    rows = jnp.concatenate([jnp.broadcast_to(crossing, (8, DI)), r.gskip[...]], axis=0)
+    rows = jnp.dot(rows, pick, precision=HIGHEST, preferred_element_type=f32)
+    at_end, gskip = rows[0:1, :], jnp.sum(rows[8:16, :], axis=0, keepdims=True)
+    upper = jnp.where(iota((ROWS, ROWS), 0) <= iota((ROWS, ROWS), 1), 1.0, 0.0)
+    strict = jnp.where(iota((ROWS, ROWS), 0) > iota((ROWS, ROWS), 1), 1.0, 0.0)
+    dlog = (
+        jnp.dot(upper, r.sums[0], precision=HIGHEST, preferred_element_type=f32)
+        + jnp.dot(strict, r.sums[1], precision=HIGHEST, preferred_element_type=f32)
+        + at_end
+    )
+    step = r.step[...]
+    dstep = r.sums[2] + rate * dlog
+    draw = dstep * sigmoid(r.proj[HALO:, CH : CH + 128] + r.heads[0:1, :])
+    lanes = iota((1, 128), 1) < H
+    draw = jnp.where(lanes, draw, 0.0)
+    gbias = jnp.sum(draw, axis=0, keepdims=True)
+    glog = jnp.where(lanes, jnp.sum(step * dlog, axis=0, keepdims=True) * rate, 0.0)
+    r.dx[:, CH : CH + 128] = low(draw)
+    r.dx[:, CH + 128 :] = jnp.zeros((ROWS, WIDE - CH - 128), jnp.bfloat16)
+
+    def unconvolve(j, grad):
+        at = at_tile(j)
+        pre = r.pre[:, at]
+        sig = sigmoid(pre)
+        grad = grad * (sig * (1.0 + pre * (1.0 - sig)))
+        r.dpre[0:8, at] = jnp.zeros((8, TILE), f32)
+        r.dpre[8 + ROWS :, at] = jnp.zeros((8, TILE), f32)
+        r.dpre[8 : 8 + ROWS, at] = grad
+        taps = [
+            jnp.sum(grad * r.same[k, 8 : 8 + ROWS, :] * r.proj[13 + k : 13 + k + ROWS, at], axis=0, keepdims=True) for k in range(KC)
+        ]
+        taps += [jnp.sum(grad, axis=0, keepdims=True), jnp.zeros((3, TILE), f32)]
+        r.gconv[:, at] = jnp.concatenate(taps, axis=0)
+        total = 0.0
+        for k in range(KC):
+            rows = slice(3 - k, 3 - k + 8 + ROWS)
+            total = total + r.conv[k : k + 1, at] * (r.same[k, rows, :] * r.dpre[rows, at])
+        r.tail[:, at] = total[0:8, :]
+        r.dx[:, at] = low(total[8:, :])
+        r.dpre[0:8, at] = total[ROWS : ROWS + 8, :]
+
+    loop(0, TILES, lambda j: unconvolve(j, r.dxs[:, at_tile(j)]))
+    unconvolve(TILES, dbproj)
+    unconvolve(TILES + 1, dcproj)
+    tails = [
+        pltpu.make_async_remote_copy(
+            src_ref=r.tail, dst_ref=r.tail_in, send_sem=r.tail_sem.at[0], recv_sem=r.tail_sem.at[1],
+            device_id=(1 - c, chip(x, y, z - 1 + c)), device_id_type=MESH,
+        )
+    ]
+    pl.when(z + c > 0)(tails[0].start)
+
+    @pl.when(z + c == planes)
+    def _():
+        r.tail_in[...] = jnp.zeros((8, CH), f32)
+
+    pl.when(z + c < planes)(tails[0].wait_recv)
+    r.dx[ROWS - 16 :, 0:CH] = low(
+        jnp.concatenate([r.dx[ROWS - 16 : ROWS - 8, 0:CH].astype(f32), r.dpre[0:8, :] + r.tail_in[...]], axis=0)
+    )
+
+    def weights_a(j):
+        at = at_rows(j, 512)
+        r.part_a[:, at] = low(dot(r.normed[...], r.dx[:, at], TRANS))
+
+    loop(0, 4, weights_a)
+    background(100)
+    reduce_a = Reduce(r.part_a, r.grad_a, 48, "columns", red_a, planes)
+    last_steps = reduce_a.steps()
+    for step in last_steps[:8]:
+        step()
+    ngain = jnp.zeros((8, 768), f32)
+    for k in range(8):
+        rows = slice(32 * k, 32 * k + 32)
+        dnormed = dot(r.dz[rows, :], r.wz_full[...], TRANS_B) + dot(r.dx[rows, :], r.wa[...], TRANS_B)
+        u = r.tok[HALO + 32 * k : HALO + 32 * k + 32, :].astype(f32)
+        scale = lax.rsqrt(jnp.mean(u * u, axis=-1, keepdims=True) + EPSILON)
+        weighed = dnormed * u * scale
+        ngain = ngain + weighed[0:8] + weighed[8:16] + weighed[16:24] + weighed[24:32]
+        a = r.ngain[5:6, :] * dnormed
+        grad = scale * (a - u * (scale * scale) * jnp.mean(u * a, axis=-1, keepdims=True))
+        r.gtok[rows, :] = low(r.cot_own[rows, :].astype(f32) + grad)
+    grads = Shuffle(r.gtok, r.tokens_out, r.back_sem, back=True)
+    grads.start()
+    ngain = jnp.sum(ngain, axis=0, keepdims=True)
+    ggain = jnp.sum(r.ggain[...], axis=0, keepdims=True)
+    lane_heads = jnp.concatenate([gbias[:, 0:H], glog[:, 0:H], gskip[:, 0:H], jnp.zeros((1, 128 - 3 * H), f32)], axis=1)
+    for k in range(16):
+        convs = jnp.concatenate([r.gconv[0:5, 112 * k : 112 * k + 112], jnp.zeros((5, 16), f32)], axis=1)
+        first = jnp.concatenate([ngain[:, 48 * k : 48 * k + 48], jnp.zeros((1, 80), f32)], axis=1)
+        second = jnp.concatenate([ggain[:, 96 * k : 96 * k + 96], jnp.zeros((1, 32), f32)], axis=1)
+        r.table[k] = jnp.concatenate([convs, first, second, lane_heads], axis=0)
+
+    def to_all(k, act):
+        other = lax.rem(me + k, 16)
+        for far in range(2):
+            copy = pltpu.make_async_remote_copy(
+                src_ref=r.table.at[other], dst_ref=r.inbox.at[c, me], send_sem=r.table_sem.at[0, far, other],
+                recv_sem=r.table_sem.at[1, c, me], device_id=(far, other), device_id_type=MESH,
+            )
+            pl.when(jnp.logical_or(k > 0, far != c))(functools.partial(act, copy))
+
+    def from_all(k):
+        other = lax.rem(me + k, 16)
+        for far in range(2):
+            copy = pltpu.make_async_remote_copy(
+                src_ref=r.table.at[other], dst_ref=r.inbox.at[far, other], send_sem=r.table_sem.at[0, far, other],
+                recv_sem=r.table_sem.at[1, far, other], device_id=(far, other), device_id_type=MESH,
+            )
+            pl.when(jnp.logical_or(k > 0, far != c))(copy.wait_recv)
+
+    loop(0, 16, lambda k: to_all(k, lambda copy: copy.start()))
+    r.inbox[c, me] = r.table[me]
+    for step in last_steps[8:]:
+        step()
+    loop(0, 16, from_all)
+    r.small_out[...] = jnp.sum(jnp.sum(r.inbox[...], axis=0), axis=0)
+    loop(0, 16, lambda k: to_all(k, lambda copy: copy.wait_send()))
+    for item in (reduce_out, reduce_z, reduce_a, forward, backward, cots, acts, grads):
+        item.finish()
+    acts.arrived()
+    grads.arrived()
+    share.wait_send()
+    pl.when(z + c > 0)(tails[0].wait_send)
+
+
+def rest(given, planes):
+    f32, bf16 = jnp.float32, jnp.bfloat16
+    shape = jax.ShapeDtypeStruct
+    named = rest_scratch(planes)
+    extra = Chain.scratch() + Chain.scratch()
+    extra += Reduce.scratch(48, WIDE, "columns", planes) + Reduce.scratch(48, DI, "columns", planes) + Reduce.scratch(96, 768, "rows", planes)
+    return pl.pallas_call(
+        functools.partial(rest_kernel, planes, list(named)),
+        out_shape=[
+            shape((2, 128, 768), bf16), shape((2, 128, 768), bf16), shape((48, WIDE), f32),
+            shape((48, DI), f32), shape((96, 768), f32), shape((8, 128), f32),
+        ],
+        in_specs=[VMEM] * len(REST_IN),
+        out_specs=[VMEM] * len(REST_OUT),
+        scratch_shapes=list(named.values()) + extra,
+        compiler_params=pltpu.CompilerParams(collective_id=1, has_side_effects=True, vmem_limit_bytes=62 << 20),
+    )(*given)
+
+
+def fast_body(
+    planes, tokens, cotangent, segments, norm_gain, w_in, conv_weight, conv_bias, step_bias, log_rate, skip_gain, gate_gain, w_out
+):
+    f32 = jnp.float32
+    segf = jnp.broadcast_to((segments.astype(f32) + 1.0)[:, 0, None, :], (2, 8, 128))
+
+    def padded(rows):
+        return jnp.pad(rows.astype(f32), ((0, 0), (0, 128 - rows.shape[1])))
+
+    nothing = jnp.zeros((1, 128), f32)
+    small = jnp.concatenate(
+        [padded(conv_weight), padded(conv_bias[None]), padded(norm_gain[None]), padded(gate_gain[None]), nothing], axis=0
+    )
+    heads = jnp.concatenate([padded(jnp.stack([step_bias, log_rate, skip_gain])), jnp.zeros((5, 128), f32)], axis=0)
+    wa = jnp.pad(w_in[:, DI:], ((0, 0), (0, WIDE - (w_in.shape[1] - DI))))
+    wa_full, table, tok, seg, normed, proj, conv, gain, ngain = enter(tokens[:, 0], segf, small, wa, planes)
+    acts, grad_tokens, grad_a, grad_z, grad_out, sums = rest(
+        (wa_full, tok, seg, normed, proj, conv, gain, ngain, heads, w_in[:, :DI], w_out, cotangent[:, 0]), planes
+    )
+    return (
+        acts[:, None],
+        grad_tokens[:, None],
+        sums[5, 0:48],
+        jnp.concatenate([grad_z, grad_a[:, : w_in.shape[1] - DI]], axis=1),
+        sums[0:4, 0:112],
+        sums[4, 0:112],
+        sums[7, 0:H],
+        sums[7, H : 2 * H],
+        sums[7, 2 * H : 3 * H],
+        sums[6, 0:96],
+        grad_out,
+    )
+
+
 def solution(mesh):
     in_specs = (
         P(None, "dp", "seq", None),
@@ -327,4 +1578,5 @@
         P("seq"),
         P("seq", None),
     )
-    return jax.shard_map(body, mesh=mesh, in_specs=in_specs, out_specs=out_specs, check_vma=False)
+    work = partial(fast_body, mesh.shape["seq"] // 4) if mesh.shape["seq"] == 16 else body
+    return jax.shard_map(work, mesh=mesh, in_specs=in_specs, out_specs=out_specs, check_vma=False)

time: 1270 us -> 203 us (0.16); the launches traced: 1250 us -> 202 us
  waiting for transfers between devices: 577 us -> 0 us
  blocking collectives: 304 us -> 0 us
  Pallas kernels: 0 us -> 176 us
  other arithmetic: 161 us -> 5.24 us
  matrix products: 93.3 us -> 0 us
  local copies, waits for them, and re-layouts: 72.3 us -> 19.9 us
  between operations: 25.8 us -> 0.72 us
  starting transfers between devices: 20.1 us -> 0 us
    all_gather x6 -> x0, waiting for transfers between devices: 395 us -> none  [the longest x4 395 us: prefix(): everything = jax.tree.map(lambda part: lax.all_gather(part, axis), array)]
    pallas_call x0 -> x2, Pallas kernels: none -> 176 us  [the longest x1 141 us: rest(): pl.pallas_call(functools.partial(rest_kernel, planes, list(named)), out_s...]
    reduce_scatter x2 -> x0, waiting for transfers between devices: 166 us -> none  [the longest x1 135 us: body(): lax.psum_scatter(lax.dot_general(normed_low, proj_grad_low, (((0,), (0,))...]
    unnamed x2 -> x0, blocking collectives: 150 us -> none
    all_gather x3 -> x0, blocking collectives: 109 us -> none  [the longest x2 73.7 us: prefix(): everything = jax.tree.map(lambda part: lax.all_gather(part, axis), array)]
    dot_general x36 -> x0, matrix products: 93.3 us -> none  [the longest x6 25.3 us: block_output(): local_part = jnp.einsum('tuh,uhp->thp', weights, inner, precision=HIGHEST)]
    select_n x64 -> x0, other arithmetic: 83.7 us -> none  [lap(): return jax.tree.map(lambda a, b: jnp.where(reached, a, b), new, before)]
    psum x2 -> x0, blocking collectives: 44.2 us -> none  [the longest x1 41.8 us: body(): lax.psum((head_totals[0], head_totals[1], head_totals[2]), ('dp', 'seq'))]
  transfers between devices with their start and end apart: 16 -> 0, of which waited for: 9 -> 0; matrix products, arithmetic and copies ran while one was open for 22% -> 0% of each run, Pallas kernels for 0% -> 0%
where the time goes in v2:
time: 203 us; the launch traced here: 202 us
  Pallas kernels  176 us (87%)
  local copies, waits for them, and re-layouts  19.9 us (10%)
  other arithmetic  5.24 us (3%)
    pallas_call x1, Pallas kernels, rest(): pl.pallas_call(functools.partial(rest_kernel, planes, list(named)), out_s...  141 us
    pallas_call x1, Pallas kernels, enter(): pl.pallas_call(functools.partial(enter_kernel, planes), out_shape=[shape(...  35.1 us
    unnamed x23, local copies, waits for them, and re-layouts  9.58 us

profile of v2, /device:TPU:0, one launch (start us, length us, event | category | flops | bytes accessed | tf_op | source)
XLA Modules:
  0.0 202.2 jit_solution(6586477041395440685)
XLA Ops:
  0.6 0.7 pad_convert_fusion.3
  1.3 0.7 convert_add_fusion
  2.0 0.7 pad_convert_fusion.1
  2.7 0.7 pad_convert_fusion
  3.4 0.7 select_maximum_fusion
  4.1 0.6 concatenate.10.refs_8_
  4.7 1.6 slice.31.refs_9_
  6.3 0.9 slice.30
  7.2 0.0 copy-start.2
  7.2 1.0 copy-done.2
  8.2 35.1 %shard_map.203 = (bf16[768,2048]{1,0:T(8,128)(2,1)}, f32[16,8,128]{2,1,0:T(8,128)}, bf16[272,768]{1,0:T(8,128)(2,1)S(1)}, f32[3,8,128]{2,1,0:T(8,128)S(1)}, bf16...) custom-call(bf16[2,128,768]{2,1,0:T(8,128)(2,1)S(1)} %bitcast.27, ...), custom_call_target="tpu_custom_call" | custom-call | tf_op jit(solution)/shard_map/pallas_call | solution.py:987
  43.3 0.0 copy-start
  43.3 1.4 copy-done
  44.7 0.8 copy-done.1
  45.5 0.7 copy-done.3
  46.2 0.6 copy-done.4
  46.8 0.6 copy-done.5
  47.5 0.6 copy-done.6
  48.1 0.6 copy-done.7
  48.7 141.2 %shard_map.204 = (bf16[2,128,768]{2,1,0:T(8,128)(2,1)}, bf16[2,128,768]{2,1,0:T(8,128)(2,1)}, f32[48,2048]{1,0:T(8,128)}, f32[48,1536]{1,0:T(8,128)}, f32[96,768]{1,0:T(8,128)}, /*index=5*/f32[8,128]{1,0:T(8,128)}) custom-call(bf16[768,2048]{1,0:T(8,128)(2,1)} %get-tuple-element.25.refs_0_, bf16[272,768]{1,0:T(8,128)(2,1)} %copy-done.1, ...), custom_call_target="tpu_custom_call" | custom-call | tf_op jit(solution)/shard_map/pallas_call | solution.py:1506
  189.9 0.0 copy-start.8
  189.9 0.0 copy-start.9
  189.9 1.2 slice_bitcast_fusion
  191.2 1.2 slice_bitcast_fusion.4
  192.3 1.2 slice_bitcast_fusion.5
  193.5 1.4 slice_bitcast_fusion.1
  194.9 1.2 slice.34
  196.1 1.0 slice.33
  197.1 1.8 pad_maximum_fusion
  199.0 1.8 copy.28
  200.7 0.7 copy.29
  201.5 0.7 copy.30
  (12 shorter events, 0.1 us)
Async XLA Ops:
  7.2 1.0 copy-start.2
  43.3 1.4 copy-start
  44.7 0.8 copy-start.1
  45.5 0.7 copy-start.3
  46.2 0.6 copy-start.4
  46.8 0.6 copy-start.5
  47.5 0.6 copy-start.6
  48.1 0.6 copy-start.7
  189.9 10.8 %copy-start.8 = (bf16[2,128,768]{2,1,0:T(8,128)(2,1)S(1)}, bf16[2,128,768]{2,1,0:T(8,128)(2,1)}, u32[]{:S(2)}) copy-start(bf16[2,128,768]{2,1,0:T(8,128)(2,1)} %get-tuple-element.34) | copy-start | bytes 1179652
  189.9 11.6 %copy-start.9 = (f32[96,768]{1,0:T(8,128)S(1)}, f32[96,768]{1,0:T(8,128)}, u32[]{:S(2)}) copy-start(f32[96,768]{1,0:T(8,128)} %get-tuple-element.76) | copy-start | bytes 884740

commit v3 on v2

--- a/solution.py
+++ b/solution.py
@@ -337,7 +337,7 @@
     pl.semaphore_wait(barrier, 2 * count - 1)
 
 
-UP, DOWN, SIDE_X, SIDE_Y, HALF_X, HALF_Y, MATE_Z, MATE_X, MATE_Y, MATE_HX, MATE_HY = range(11)
+COLUMN, SIDE_X, SIDE_Y, HALF_X, HALF_Y, MATE_Z, MATE_X, MATE_Y, MATE_HX, MATE_HY = range(10)
 
 
 class Gather:
@@ -357,26 +357,25 @@
         half = width // 2
         return self.whole.at[pl.ds(start, self.rows), pl.ds(pl.multiple_of(left + part * half, 128), half)]
 
-    def copy(self, kind, far, block, core, part, device):
+    def copy(self, kind, leaves, lands, block, core, part, device):
         region = self.region(block, core, part)
         return pltpu.make_async_remote_copy(
             src_ref=region,
             dst_ref=region,
-            send_sem=self.sems.at[0, kind, far],
-            recv_sem=self.sems.at[1, kind, far],
+            send_sem=self.sems.at[0, kind, leaves],
+            recv_sem=self.sems.at[1, kind, lands],
             device_id=device,
             device_id_type=MESH,
         )
 
-    def transfers(self, far):
+    def out(self, kind, far):
         x, y, z, c = self.x, self.y, self.z, self.core
-        own = chip(x, y, far)
-        by_x, by_y, across = chip(1 - x, y, far), chip(x, 1 - y, far), chip(1 - x, 1 - y, far)
+        if kind == COLUMN:
+            return self.copy(kind, far, z, chip(x, y, z), c, None, (c, chip(x, y, far)))
+        own, by_x, by_y, across = chip(x, y, far), chip(1 - x, y, far), chip(x, 1 - y, far), chip(1 - x, 1 - y, far)
         mate = (1 - c, chip(x, y, z))
         to_x, to_y = (c, chip(1 - x, y, z)), (c, chip(x, 1 - y, z))
-        return {
-            UP: (own, None, (c, chip(x, y, z + 1))),
-            DOWN: (own, None, (c, chip(x, y, z - 1))),
+        block, part, device = {
             SIDE_X: (own, None, to_x),
             SIDE_Y: (own, None, to_y),
             HALF_X: (by_y, 1, to_x),
@@ -386,59 +385,61 @@
             MATE_Y: (by_y, None, mate),
             MATE_HX: (across, 1, mate),
             MATE_HY: (across, 0, mate),
-        }
+        }[kind]
+        return self.copy(kind, far, far, block, c, part, device)
 
     def send(self, kind, far):
-        block, part, device = self.transfers(far)[kind]
-        self.copy(kind, far, block, self.core, part, device).start()
-
-    def sent(self, kind, far):
-        block, part, device = self.transfers(far)[kind]
-        self.copy(kind, far, block, self.core, part, device).wait_send()
+        self.out(kind, far).start()
 
     def arrived(self, kind, far):
         x, y = self.x, self.y
-        block, part, core = {
-            UP: (chip(x, y, far), None, 0),
-            DOWN: (chip(x, y, far), None, 0),
-            SIDE_X: (chip(1 - x, y, far), None, 0),
-            SIDE_Y: (chip(x, 1 - y, far), None, 0),
-            HALF_X: (chip(1 - x, 1 - y, far), 1, 0),
-            HALF_Y: (chip(1 - x, 1 - y, far), 0, 0),
-            MATE_Z: (chip(x, y, far), None, 1),
-            MATE_X: (chip(1 - x, y, far), None, 1),
-            MATE_Y: (chip(x, 1 - y, far), None, 1),
-            MATE_HX: (chip(1 - x, 1 - y, far), 1, 1),
-            MATE_HY: (chip(1 - x, 1 - y, far), 0, 1),
+        own, by_x, by_y, across = chip(x, y, far), chip(1 - x, y, far), chip(x, 1 - y, far), chip(1 - x, 1 - y, far)
+        block, part, mine = {
+            COLUMN: (own, None, True),
+            SIDE_X: (by_x, None, True),
+            SIDE_Y: (by_y, None, True),
+            HALF_X: (across, 1, True),
+            HALF_Y: (across, 0, True),
+            MATE_Z: (own, None, False),
+            MATE_X: (by_x, None, False),
+            MATE_Y: (by_y, None, False),
+            MATE_HX: (across, 1, False),
+            MATE_HY: (across, 0, False),
         }[kind]
-        owner = self.core if core == 0 else 1 - self.core
-        self.copy(kind, far, block, owner, part, (1 - self.core, chip(x, y, self.z))).wait_recv()
+        core = self.core if mine else 1 - self.core
+        self.copy(kind, far, far, block, core, part, (1 - self.core, chip(x, y, self.z))).wait_recv()
 
     def each(self, distance, act):
         for sign in (-1, 1) if distance else (1,):
             far = self.z + sign * distance
             if distance:
-                pl.when(jnp.logical_and(far >= 0, far < self.planes))(functools.partial(act, far, sign))
+                pl.when(jnp.logical_and(far >= 0, far < self.planes))(functools.partial(act, far))
             else:
-                act(far, sign)
+                act(far)
+
+    def begin_sides(self):
+        self.send(SIDE_X, self.z)
+        self.send(SIDE_Y, self.z)
+
+    def begin_column(self):
+        for distance in range(1, self.planes):
+            self.each(distance, lambda far: self.send(COLUMN, far))
+
+    def begin(self):
+        self.begin_sides()
+        self.begin_column()
 
     def column(self, distance):
-        def act(far, sign):
-            if distance:
-                self.arrived(UP if sign < 0 else DOWN, far)
-            if sign < 0 or not distance:
-                pl.when(self.z < self.planes - 1)(lambda: self.send(UP, far))
-            if sign > 0:
-                pl.when(self.z > 0)(lambda: self.send(DOWN, far))
+        def act(far):
+            self.arrived(COLUMN, far)
             self.send(SIDE_X, far)
             self.send(SIDE_Y, far)
-            if distance:
-                self.send(MATE_Z, far)
+            self.send(MATE_Z, far)
 
         self.each(distance, act)
 
     def sides(self, distance):
-        def act(far, sign):
+        def act(far):
             self.arrived(SIDE_X, far)
             self.send(HALF_Y, far)
             self.send(MATE_X, far)
@@ -449,7 +450,7 @@
         self.each(distance, act)
 
     def diagonal(self, distance):
-        def act(far, sign):
+        def act(far):
             self.arrived(HALF_Y, far)
             self.send(MATE_HY, far)
             self.arrived(HALF_X, far)
@@ -457,37 +458,32 @@
 
         self.each(distance, act)
 
+    def whole_here(self):
+        for distance in range(self.planes):
+
+            def act(far):
+                for kind in (MATE_X, MATE_Y, MATE_HX, MATE_HY) + ((MATE_Z,) if distance else ()):
+                    self.arrived(kind, far)
+
+            self.each(distance, act)
+
     def finish(self):
         for distance in range(self.planes):
 
-            def act(far, sign):
-                if sign < 0 or not distance:
-                    pl.when(self.z < self.planes - 1)(lambda: self.sent(UP, far))
-                if sign > 0:
-                    pl.when(self.z > 0)(lambda: self.sent(DOWN, far))
-                for kind in (SIDE_X, SIDE_Y, HALF_X, HALF_Y, MATE_X, MATE_Y, MATE_HX, MATE_HY):
-                    self.sent(kind, far)
-                for kind in (MATE_X, MATE_Y, MATE_HX, MATE_HY):
-                    self.arrived(kind, far)
-                if distance:
-                    self.sent(MATE_Z, far)
-                    self.arrived(MATE_Z, far)
+            def act(far):
+                kinds = (SIDE_X, SIDE_Y, HALF_X, HALF_Y, MATE_X, MATE_Y, MATE_HX, MATE_HY)
+                for kind in kinds + ((MATE_Z, COLUMN) if distance else ()):
+                    self.out(kind, far).wait_send()
 
             self.each(distance, act)
 
-    def steps(self):
-        do = [lambda: self.column(0), lambda: self.column(1), lambda: self.sides(0), lambda: self.column(2), lambda: self.diagonal(0),
-              lambda: self.sides(1), lambda: self.column(3), lambda: self.diagonal(1), lambda: self.sides(2), lambda: self.diagonal(2),
-              lambda: self.sides(3), lambda: self.diagonal(3)]
-        return do
-
 
 def gather_sems(planes):
-    return pltpu.SemaphoreType.DMA((2, 11, planes))
+    return pltpu.SemaphoreType.DMA((2, 10, planes))
 
 
 class Reduce:
-    X, Y, HX, HY, RISE, FALL, MATE, LAST = range(8)
+    X, Y, HX, HY, COLUMN, MATE, LAST = range(7)
 
     @staticmethod
     def scratch(rows, width, quarter, planes):
@@ -496,9 +492,9 @@
         bf16 = jnp.bfloat16
         return [
             pltpu.VMEM((4 * planes * rows, half), bf16),
-            pltpu.VMEM((4, planes, rows, half), bf16),
+            pltpu.VMEM((3, planes, rows, half), bf16),
             pltpu.VMEM((2, planes) + corner, bf16),
-            pltpu.SemaphoreType.DMA((2, 8, planes)),
+            pltpu.SemaphoreType.DMA((2, 7, planes)),
         ]
 
     def __init__(self, part, out, rows, quarter, scratch, planes):
@@ -539,10 +535,15 @@
             return self.copy(kind, far, part.at[self.block(chip(1 - x, 1 - y, far), 0)], self.corner_in.at[0, far], to_x)
         if kind == self.HY:
             return self.copy(kind, far, part.at[self.block(chip(1 - x, 1 - y, far), 1)], self.corner_in.at[1, far], to_y)
-        if kind == self.RISE:
-            return self.copy(kind, far, part.at[self.block(chip(x, y, far))], self.side_in.at[2, far], (c, chip(x, y, z + 1)))
-        if kind == self.FALL:
-            return self.copy(kind, far, part.at[self.block(chip(x, y, far))], self.side_in.at[3, far], (c, chip(x, y, z - 1)))
+        if kind == self.COLUMN:
+            return pltpu.make_async_remote_copy(
+                src_ref=part.at[self.block(chip(x, y, far))],
+                dst_ref=self.side_in.at[2, z],
+                send_sem=self.sems.at[0, kind, far],
+                recv_sem=self.sems.at[1, kind, z],
+                device_id=(c, chip(x, y, far)),
+                device_id_type=MESH,
+            )
         if kind == self.MATE:
             rows = pl.ds(pl.multiple_of(far * 4 * self.rows, 16), 4 * self.rows)
             left = pl.multiple_of((1 - c) * self.half, 128)
@@ -603,45 +604,27 @@
         def act(far, sign):
             self.move(self.X, far).wait_recv()
             self.move(self.Y, far).wait_recv()
-            at = self.block(chip(x, y, far))
             if distance:
-                self.add(at, self.side_in.at[0, far], self.side_in.at[1, far])
-                if sign > 0:
-
-                    @pl.when(z > 0)
-                    def _():
-                        self.move(self.RISE, far).wait_recv()
-                        self.add(at, self.side_in.at[2, far])
-
-                    self.move(self.RISE, far).start()
-                else:
-
-                    @pl.when(z < self.planes - 1)
-                    def _():
-                        self.move(self.FALL, far).wait_recv()
-                        self.add(at, self.side_in.at[3, far])
-
-                    self.move(self.FALL, far).start()
-                return
-            total = self.part[at].astype(jnp.float32)
-            total = total + self.side_in[0, far].astype(jnp.float32) + self.side_in[1, far].astype(jnp.float32)
-            left = pl.multiple_of(self.core * self.half, 128)
-            here = (slice(None), pl.ds(left, self.half))
-            self.out[here] = total
-
-            @pl.when(z > 0)
-            def _():
-                self.move(self.RISE, far).wait_recv()
+                self.add(self.block(chip(x, y, far)), self.side_in.at[0, far], self.side_in.at[1, far])
+                self.move(self.COLUMN, far).start()
+
+        self.each(distance, act)
+
+    def close(self):
+        z = self.z
+        at = self.block(chip(self.x, self.y, z))
+        left = pl.multiple_of(self.core * self.half, 128)
+        here = (slice(None), pl.ds(left, self.half))
+        total = self.part[at].astype(jnp.float32)
+        self.out[here] = total + self.side_in[0, z].astype(jnp.float32) + self.side_in[1, z].astype(jnp.float32)
+        for distance in range(self.planes - 1, 0, -1):
+
+            def act(far, sign):
+                self.copy(self.COLUMN, far, self.side_in.at[2, far], self.side_in.at[2, far], (self.core, chip(self.x, self.y, far))).wait_recv()
                 self.out[here] = self.out[here] + self.side_in[2, far].astype(jnp.float32)
 
-            @pl.when(z < self.planes - 1)
-            def _():
-                self.move(self.FALL, far).wait_recv()
-                self.out[here] = self.out[here] + self.side_in[3, far].astype(jnp.float32)
-
-            self.move(self.LAST, 0).start()
-
-        self.each(distance, act)
+            self.each(distance, act)
+        self.move(self.LAST, 0).start()
 
     def finish(self):
         last = self.move(self.LAST, 0)
@@ -655,23 +638,13 @@
                 for kind in (self.MATE, self.HX, self.HY, self.X, self.Y):
                     self.move(kind, far).wait_send()
                 if distance:
-                    self.move(self.RISE if sign > 0 else self.FALL, far).wait_send()
+                    self.move(self.COLUMN, far).wait_send()
 
             self.each(distance, act)
 
-    def steps(self):
-        top = self.planes - 1
-        do = [functools.partial(self.start, d) for d in range(top, -1, -1)]
-        do += [functools.partial(self.fold, d) for d in range(top, -1, -1)]
-        for d in range(top, -1, -1):
-            do += [functools.partial(self.sides, d)]
-            if d < top:
-                do += [functools.partial(self.column, d + 1)]
-        return do + [functools.partial(self.column, 0)]
-
 
 class Chain:
-    CUT = 3
+    CUT = 6
 
     @staticmethod
     def scratch():
@@ -927,87 +900,6 @@
         self.over(lambda other: self.copy(self.me, other).wait_send())
 
 
-def enter_kernel(
-    planes, tok_ref, seg_ref, small_ref, wa_ref,
-    whole, table, tok, seg, normed_ref, proj_ref, conv_ref, gain_ref, ngain_ref,
-    normed_all, gather_sem, tok_sem, seg_sem, end_sem, segend_sem, small_sem,
-):
-    at = lax.axis_index("seq")
-    x, y, z, c = place()
-    whole[pl.ds(pl.multiple_of(at * 48, 16), 48), :] = wa_ref[...]
-    table[at] = small_ref[...]
-
-    @pl.when(z + c == 0)
-    def _():
-        tok[0:HALO, :] = jnp.zeros((HALO, tok.shape[1]), tok.dtype)
-        seg[0] = jnp.full((8, 128), -1.0, jnp.float32)
-
-    gather = Gather(whole, 48, "columns", gather_sem, planes)
-    tokens = Shuffle(tok_ref, tok, tok_sem, HALO)
-    numbers = Shuffle(seg_ref, seg, seg_sem, 1)
-    ends = Before(lambda m: tok_ref.at[m, pl.ds(128 - HALO, HALO)], tok.at[pl.ds(0, HALO)], end_sem, planes)
-    segends = Before(lambda m: seg_ref.at[m], seg.at[0], segend_sem, planes)
-    small = ToAll(table, small_sem, planes)
-    meet_all(planes)
-    moves = [tokens, ends, numbers, segends, small]
-    for move in moves:
-        move.start()
-    steps = gather.steps()
-    for step in steps[:3]:
-        step()
-    for move in moves:
-        move.arrived()
-    conv_ref[...] = jnp.concatenate([table[k, :, 0:112] for k in range(16)], axis=1)
-    gate = jnp.concatenate([table[k, :, 0:96] for k in range(16)], axis=1)
-    gain_ref[...] = gate
-    ngain_ref[...] = jnp.concatenate([table[k, :, 0:48] for k in range(16)], axis=1)
-    gain = ngain_ref[5:6, :]
-    u = tok[...].astype(jnp.float32)
-    r = lax.rsqrt(jnp.mean(u * u, axis=-1, keepdims=True) + EPSILON)
-    normed_all[...] = low(u * r * gain)
-    normed_ref[...] = normed_all[HALO:, :]
-    for step in steps[3:]:
-        step()
-    gather.finish()
-    for move in moves:
-        move.finish()
-
-    def columns(k, carry):
-        at_k = pl.ds(pl.multiple_of(k * 512, 512), 512)
-        proj_ref[:, at_k] = dot(normed_all[...], whole[:, at_k])
-        return carry
-
-    lax.fori_loop(0, WIDE // 512, columns, 0)
-
-
-def enter(tokens, segf, small, wa, planes):
-    f32, bf16 = jnp.float32, jnp.bfloat16
-    shape = jax.ShapeDtypeStruct
-    two = pltpu.SemaphoreType.DMA((2, 2))
-    return pl.pallas_call(
-        functools.partial(enter_kernel, planes),
-        out_shape=[
-            shape((768, WIDE), bf16),
-            shape((16, 8, 128), f32),
-            shape((HALO + ROWS, 768), bf16),
-            shape((3, 8, 128), f32),
-            shape((ROWS, 768), bf16),
-            shape((HALO + ROWS, WIDE), f32),
-            shape((8, CH), f32),
-            shape((8, DI), f32),
-            shape((8, 768), f32),
-        ],
-        in_specs=[VMEM] * 4,
-        out_specs=[VMEM] * 9,
-        scratch_shapes=[
-            pltpu.VMEM((HALO + ROWS, 768), bf16),
-            gather_sems(planes), two, two, two, two,
-            pltpu.SemaphoreType.DMA((2, 16)),
-        ],
-        compiler_params=pltpu.CompilerParams(collective_id=0, has_side_effects=True, vmem_limit_bytes=48 << 20),
-    )(tokens, segf, small, wa)
-
-
 TILE = 128
 TILES = DI // TILE
 
@@ -1059,24 +951,28 @@
 def head_sums(a, j):
     row, col = iota((TILE, 128), 0), iota((TILE, 128), 1)
     pick = low(jnp.where(row // P_SIZE + 2 * j == col, 1.0, 0.0))
-    high, middle, rest = pieces(a)
-    return dot(high, pick) + dot(middle, pick) + dot(rest, pick)
+    high, middle, _ = pieces(a)
+    return dot(jnp.concatenate([high, middle], axis=1), jnp.concatenate([pick, pick], axis=0))
 
 
 def sigmoid(v):
     return 1.0 / (1.0 + jnp.exp(-v))
 
 
-REST_IN = ["wa", "tok", "seg", "normed", "proj", "conv", "gain", "ngain", "heads", "wz", "wout", "cot"]
-REST_OUT = ["act_out", "tokens_out", "grad_a", "grad_z", "grad_out", "small_out"]
-
-
-def rest_scratch(planes):
+GIVEN = ["tok_in", "cot", "seg_in", "small_in", "w_in", "wout"]
+MADE = ["act_out", "tokens_out", "grad_a", "grad_z", "grad_out", "small_out"]
+
+
+def block_scratch(planes):
     f32, bf16 = jnp.float32, jnp.bfloat16
     v = pltpu.VMEM
     dma = pltpu.SemaphoreType.DMA
     two = dma((2, 2))
     return {
+        "wa": v((768, WIDE), bf16), "wa_sem": gather_sems(planes), "tok": v((HALO + ROWS, 768), bf16), "seg": v((3, 8, 128), f32),
+        "normed": v((HALO + ROWS, 768), bf16), "proj": v((HALO + ROWS, WIDE), f32), "conv": v((8, CH), f32), "gain": v((8, DI), f32),
+        "ngain": v((8, 768), f32), "ngrad": v((8, 768), f32), "given": v((16, 8, 128), f32), "numbers": v((2, 8, 128), f32),
+        "tok_sem": two, "end_sem": two, "seg_sem": two, "segend_sem": two, "given_sem": dma((2, 16)),
         "wz_full": v((768, DI), bf16), "wout_full": v((DI, 768), bf16), "wz_sem": gather_sems(planes), "wout_sem": gather_sems(planes),
         "cot_own": v((ROWS, 768), bf16), "cot_sem": two, "act_sem": two, "back_sem": two,
         "segcol": v((384, 128), f32), "same": v((KC, ROWS + HALO, 128), f32),
@@ -1091,36 +987,71 @@
         "dz": v((ROWS, DI), bf16), "dy": v((ROWS, DI), bf16), "dyin": v((ROWS, DI), bf16),
         "ggain": v((8, DI), f32), "gskip": v((8, DI), f32),
         "dscores": v((ROWS, ROWS), f32), "dxs": v((ROWS, DI), f32), "sums": v((3, ROWS, 128), f32),
-        "dpre": v((ROWS + HALO, CH), f32), "dx": v((ROWS, WIDE), bf16), "tail": v((8, CH), f32), "tail_in": v((8, CH), f32), "tail_sem": dma((2,)),
+        "dpre": v((2, ROWS + HALO, TILE), f32), "late": v((8, CH), f32), "dx": v((HALO + ROWS, WIDE), bf16), "tail": v((8, CH), f32), "tail_in": v((8, CH), f32), "tail_sem": dma((2,)),
         "gconv": v((8, CH), f32), "gtok": v((ROWS, 768), bf16),
         "table": v((16, 8, 128), f32), "inbox": v((2, 16, 8, 128), f32), "table_sem": dma((2, 2, 16)),
-        "part_a": v((768, WIDE), bf16), "part_z": v((768, DI), bf16), "part_out": v((DI, 768), bf16),
+        "part_a": v((2, 768, WIDE // 2), bf16), "part_z": v((768, DI), bf16), "part_out": v((DI, 768), bf16),
     }
 
 
-def rest_kernel(planes, names, *refs):
-    r = Names(REST_IN + REST_OUT + names, refs[: len(REST_IN) + len(REST_OUT) + len(names)])
-    extra = list(refs[len(REST_IN) + len(REST_OUT) + len(names) :])
-    chain_f, chain_b = extra[0:9], extra[9:18]
-    red_a, red_z, red_out = extra[18:22], extra[22:26], extra[26:30]
+def block_kernel(planes, names, *refs):
+    r = Names(GIVEN + MADE + names, refs[: len(GIVEN) + len(MADE) + len(names)])
+    extra = list(refs[len(GIVEN) + len(MADE) + len(names) :])
+    chain_f, chain_b = extra[0:9], extra[9:15] + extra[6:8] + extra[15:16]
+    red_a, red_b, red_z, red_out = extra[16:20], extra[20:24], extra[24:28], extra[28:32]
     x, y, z, c = place()
     me = chip(x, y, z)
     mate = (1 - c, me)
     f32 = jnp.float32
-    r.wz_full[pl.ds(pl.multiple_of(me * 48, 16), 48), :] = r.wz[...]
+    r.wa[pl.ds(pl.multiple_of(me * 48, 16), 48), 0:CH] = r.w_in[:, DI : DI + CH]
+    step_columns = r.w_in[:, DI + CH :]
+    fill = jnp.zeros((48, WIDE - CH - H), step_columns.dtype)
+    r.wa[pl.ds(pl.multiple_of(me * 48, 16), 48), CH:] = jnp.concatenate([step_columns, fill], axis=1)
+    r.wz_full[pl.ds(pl.multiple_of(me * 48, 16), 48), :] = r.w_in[:, 0:DI]
     r.wout_full[pl.ds(pl.multiple_of(me * 96, 16), 96), :] = r.wout[...]
+    r.given[me] = r.small_in[0:8, :]
+    for m in range(2):
+        r.numbers[m] = jnp.broadcast_to(r.seg_in[m : m + 1, :].astype(f32) + 1.0, (8, 128))
+
+    @pl.when(z + c == 0)
+    def _():
+        r.tok[0:HALO, :] = jnp.zeros((HALO, 768), r.tok.dtype)
+        r.seg[0] = jnp.full((8, 128), -1.0, f32)
+
+    gather_a = Gather(r.wa, 48, "columns", r.wa_sem, planes)
     gather_z = Gather(r.wz_full, 48, "columns", r.wz_sem, planes)
     gather_out = Gather(r.wout_full, 96, "rows", r.wout_sem, planes)
     cots = Shuffle(r.cot, r.cot_own, r.cot_sem)
+    moves = [
+        Shuffle(r.tok_in, r.tok, r.tok_sem, HALO),
+        Before(lambda m: r.tok_in.at[m, pl.ds(128 - HALO, HALO)], r.tok.at[pl.ds(0, HALO)], r.end_sem, planes),
+        Shuffle(r.numbers, r.seg, r.seg_sem, 1),
+        Before(lambda m: r.numbers.at[m], r.seg.at[0], r.segend_sem, planes),
+        ToAll(r.given, r.given_sem, planes),
+    ]
     meet_all(planes)
-    cots.start()
-    waiting = [step for pair in zip(gather_z.steps(), gather_out.steps()) for step in pair]
-
-    def background(count):
-        for _ in range(min(count, len(waiting))):
-            waiting.pop(0)()
-
-    background(2)
+    gather_a.begin()
+    for item in moves:
+        item.start()
+    gather_a.column(1)
+    gather_a.sides(0)
+    for item in moves:
+        item.arrived()
+    r.conv[...] = jnp.concatenate([r.given[k, :, 0:112] for k in range(16)], axis=1)
+    r.gain[...] = jnp.concatenate([r.given[k, :, 0:96] for k in range(16)], axis=1)
+    r.ngain[...] = jnp.concatenate([r.given[k, :, 0:48] for k in range(16)], axis=1)
+    gather_a.column(2)
+    gather_a.column(3)
+    gather_z.begin_column()
+    gather_out.begin_column()
+    gather_a.sides(1)
+    gather_a.diagonal(0)
+    u = r.tok[...].astype(f32)
+    r.normed[...] = low(u * lax.rsqrt(jnp.mean(u * u, axis=-1, keepdims=True) + EPSILON) * r.ngain[5:6, :])
+    gather_a.sides(2)
+    for gather in (gather_z, gather_out):
+        gather.begin_sides()
+    gather_a.diagonal(1)
 
     for k in range(3):
         r.segcol[128 * k : 128 * k + 128, :] = jnp.transpose(jnp.broadcast_to(r.seg[k, 0:1, :], (128, 128)))
@@ -1128,6 +1059,28 @@
     for k in range(KC):
         r.same[k] = jnp.zeros((ROWS + HALO, 128), f32)
         r.same[k, 8 : 8 + ROWS, :] = jnp.where(r.segcol[125 + k : 125 + k + ROWS, :] == seg, 1.0, 0.0)
+    gather_a.sides(3)
+    gather_a.diagonal(2)
+    for gather in (gather_z, gather_out):
+        for d in range(1, planes):
+            gather.column(d)
+    cots.start()
+    gather_a.diagonal(3)
+    gather_a.whole_here()
+
+    def sides(d):
+        gather_z.sides(d)
+        gather_out.sides(d)
+
+    def diagonal(d):
+        gather_z.diagonal(d)
+        gather_out.diagonal(d)
+
+    def project(k):
+        at_k = pl.ds(pl.multiple_of(k * 512, 512), 512)
+        r.proj[:, at_k] = dot(r.normed[...], r.wa[:, at_k])
+
+    project(WIDE // 512 - 1)
 
     def convolve(j):
         at = at_tile(j)
@@ -1137,17 +1090,12 @@
         r.pre[:, at] = total
         return total * sigmoid(total)
 
-    def inner(j):
-        r.inner[:, at_tile(j)] = convolve(j)
-
-    loop(0, TILES, inner)
     r.bproj[...] = low(convolve(TILES))
     r.cproj[...] = low(convolve(TILES + 1))
-    background(4)
-
-    raw = r.proj[HALO:, CH : CH + 128] + r.heads[0:1, :]
+
+    raw = r.proj[HALO:, CH : CH + 128] + r.small_in[8:9, :]
     step = jnp.maximum(raw, 0.0) + jnp.log1p(jnp.exp(-jnp.abs(raw)))
-    rate = -jnp.exp(r.heads[1:2, :])
+    rate = -jnp.exp(r.small_in[9:10, :])
     lower = jnp.where(iota((ROWS, ROWS), 0) >= iota((ROWS, ROWS), 1), 1.0, 0.0)
     cum = jnp.dot(lower, step * rate, precision=HIGHEST, preferred_element_type=f32)
     r.step[...] = step
@@ -1165,7 +1113,7 @@
     segrow = jnp.concatenate([r.seg[1, 0:1, :], r.seg[2, 0:1, :]], axis=1)
     allowed = jnp.logical_and(jnp.concatenate([seg, seg], axis=1) == segrow, iota((ROWS, ROWS), 0) >= iota((ROWS, ROWS), 1))
     r.bar[...] = jnp.where(allowed, 0.0, -1e30)
-    rows = packed(jnp.concatenate([jnp.broadcast_to(factor, (8, 128)), jnp.broadcast_to(r.heads[2:3, :], (8, 128))], axis=0))
+    rows = packed(jnp.concatenate([jnp.broadcast_to(factor, (8, 128)), jnp.broadcast_to(r.small_in[10:11, :], (8, 128))], axis=0))
     both = dot(rows, spread_matrix(DI))
     r.factors[c] = both[0:8, :]
     r.skipx[...] = both[8:16, :]
@@ -1176,23 +1124,33 @@
     share.start()
     spreads = [(r.stepx, packed(step)), (r.einx, packed(r.ein[...])), (r.eoutx, packed(r.eout[...])), (r.cumx, packed(cum))]
     r.stepx[...] = dot(spreads[0][1], spread_matrix(DI))
-    r.einx[...] = dot(spreads[1][1], spread_matrix(DI))
     r.eoutx[...] = dot(spreads[2][1], spread_matrix(DI))
-    r.cumx[...] = dot(spreads[3][1], spread_matrix(DI))
-
-    def outgoing(j):
+    loop(0, WIDE // 512 - 1, project)
+
+    def trade_order(k):
+        return lax.rem(k + TILES // 2 * (1 - c), TILES)
+
+    def outgoing(k):
+        j = trade_order(k)
         at = at_tile(j)
-        scaled = r.stepx[:, at] * r.inner[:, at]
+        inner = convolve(j)
+        r.inner[:, at] = inner
+        scaled = r.stepx[:, at] * inner
         r.xs[:, at] = low(scaled)
         xso = low(scaled * r.eoutx[:, at])
         r.xso[:, at] = xso
         r.part[:, at] = dot(r.bproj[...], xso, TRANS)
 
-    loop(0, TILES, outgoing)
+    loop(0, TILES // 2, outgoing)
     forward = Chain(r.part, r.state, r.factors, chain_f, 0, planes)
     forward.start()
+    loop(TILES // 2, TILES, outgoing)
+    share.wait_recv()
+    forward.merge()
     r.scores[...] = dot(r.cproj[...], r.bproj[...], TRANS_B)
-    background(4)
+    r.einx[...] = dot(spreads[1][1], spread_matrix(DI))
+    r.cumx[...] = dot(spreads[3][1], spread_matrix(DI))
+    sides(0)
 
     first_half = iota((1, TILE), 1) < P_SIZE
 
@@ -1229,19 +1187,19 @@
                 position = k if chain.lead == 0 else planes - 1 - k
                 pl.when(z == position)(chain.pass_on)
 
-    loop(0, 2, within)
-    share.wait_recv()
-    forward.merge()
     turn(forward, [1, 0, 0, 0])
-    loop(2, 5, within)
-    background(2)
+    loop(0, 4, within)
     turn(forward, [0, 1, 0, 0])
-    loop(5, 8, within)
-    background(4)
+    sides(1)
+    diagonal(0)
+    loop(4, 8, within)
     turn(forward, [0, 0, 1, 0])
+    sides(2)
+    diagonal(1)
     loop(8, 12, within)
-    background(4)
+    sides(3)
     turn(forward, [0, 0, 0, 1])
+    diagonal(2)
     forward.close()
 
     def carried(j):
@@ -1249,14 +1207,14 @@
         r.y[:, at] = r.y[:, at] + r.einx[:, at] * dot(r.cproj[...], r.state[:, at])
 
     loop(0, TILES, carried)
-    background(100)
-    gather_z.finish()
-    gather_out.finish()
+    diagonal(3)
+    gather_z.whole_here()
+    gather_out.whole_here()
     cots.arrived()
 
     def projections(j):
         at = pl.ds(pl.multiple_of(j * 512, 512), 512)
-        r.z[:, at] = dot(r.normed[...], r.wz_full[:, at])
+        r.z[:, at] = dot(r.normed[HALO:, :], r.wz_full[:, at])
         r.dxs[:, at] = dot(r.cot_own[...], r.wout_full[at, :], TRANS_B)
 
     loop(0, 3, projections)
@@ -1292,34 +1250,55 @@
         at = at_tile(j)
         r.part[:, at] = dot(r.cproj[...], r.dyin[:, at], TRANS)
 
-    loop(0, TILES, incoming)
+    loop(0, TILES // 2, lambda k: incoming(trade_order(k)))
     backward = Chain(r.part, r.dstate, r.factors, chain_b, 1, planes)
     backward.start()
-
-    def weights(j):
+    loop(TILES // 2, TILES, lambda k: incoming(trade_order(k)))
+    reduce_out = Reduce(r.part_out, r.grad_out, 96, "rows", red_out, planes)
+    reduce_z = Reduce(r.part_z, r.grad_z, 48, "columns", red_z, planes)
+    every = range(planes - 1, -1, -1)
+
+    def weights_out(j):
         at = at_rows(j, 256)
         r.part_out[at, :] = low(dot(r.gated[:, at], r.cot_own[...], TRANS))
-        r.part_z[:, at] = low(dot(r.normed[...], r.dz[:, at], TRANS))
-
-    loop(0, 2, weights)
+
+    loop(0, 2, weights_out)
     backward.merge()
     turn(backward, [1, 0, 0, 0])
-    loop(2, 6, weights)
+    loop(2, 6, weights_out)
+    for d in every:
+        reduce_out.start(d)
+
+    def weights_z(k):
+        half = lax.rem(k // 3 + 1 + c, 2)
+        at = pl.ds(pl.multiple_of(half * (DI // 2) + k % 3 * 256, 256), 256)
+        r.part_z[:, at] = low(dot(r.normed[HALO:, :], r.dz[:, at], TRANS))
+
+    loop(0, 3, weights_z)
+    for d in every:
+        reduce_z.start(d)
+    loop(3, 6, weights_z)
+    for d in every:
+        reduce_out.fold(d)
     turn(backward, [0, 1, 0, 0])
-    reduce_out = Reduce(r.part_out, r.grad_out, 96, "rows", red_out, planes)
-    reduce_z = Reduce(r.part_z, r.grad_z, 48, "columns", red_z, planes)
-    waiting.extend(step for pair in zip(reduce_out.steps(), reduce_z.steps()) for step in pair)
-    background(8)
+    for d in every:
+        reduce_z.fold(d)
 
     def project_out(k):
-        rows = at_rows(k, 64)
-        branch = dot(r.gated[rows, :], r.wout_full[...])
-        r.act_own[rows, :] = low(r.tok[pl.ds(pl.multiple_of(HALO + k * 64, 16), 64), :].astype(f32) + branch)
-
-    loop(0, 4, project_out)
+        at = at_rows(k, 256)
+        r.act_own[:, at] = low(r.tok[HALO:, at].astype(f32) + dot(r.gated[...], r.wout_full[:, at]))
+
+    loop(0, 3, project_out)
     acts = Shuffle(r.act_own, r.act_out, r.act_sem, back=True)
     acts.start()
-    turn(backward, [0, 0, 1, 0])
+
+    def reduce_sides(d):
+        reduce_out.sides(d)
+        reduce_z.sides(d)
+
+    def reduce_column(d):
+        reduce_out.column(d)
+        reduce_z.column(d)
 
     r.dscores[...] = jnp.zeros((ROWS, ROWS), f32)
     r.sums[...] = jnp.zeros((3, ROWS, 128), f32)
@@ -1344,16 +1323,19 @@
         gain = r.dy[:, at].astype(f32) * r.y[:, at] - r.xs[:, at].astype(f32) * r.dxs[:, at]
         r.sums[0] = r.sums[0] + head_sums(gain, j)
 
-    loop(0, 3, within_back)
+    loop(0, 2, within_back)
+    turn(backward, [0, 0, 1, 0])
+    reduce_sides(3)
+    loop(2, 5, within_back)
+    reduce_sides(2)
+    reduce_column(3)
+    loop(5, 8, within_back)
+    reduce_sides(1)
+    reduce_column(2)
     turn(backward, [0, 0, 0, 1])
-    background(6)
-    loop(3, 6, within_back)
+    loop(8, 12, within_back)
     backward.close()
-    background(6)
-    loop(6, 9, within_back)
-    background(4)
-    loop(9, 12, within_back)
-    background(4)
+    reduce_sides(0)
 
     def last_sums(j):
         at = at_tile(j)
@@ -1365,7 +1347,53 @@
         r.sums[2] = r.sums[2] + head_sums(inner * total, j)
         r.dxs[:, at] = r.skipx[0:1, at] * r.z[:, at] + r.stepx[:, at] * total
 
-    loop(0, TILES, last_sums)
+    def unconvolve(j, grad):
+        at = at_tile(j)
+        pre = r.pre[:, at]
+        sig = sigmoid(pre)
+        grad = grad * (sig * (1.0 + pre * (1.0 - sig)))
+        slot = j % 2
+        r.dpre[slot, 0:8, :] = jnp.zeros((8, TILE), f32)
+        r.dpre[slot, 8 + ROWS :, :] = jnp.zeros((8, TILE), f32)
+        r.dpre[slot, 8 : 8 + ROWS, :] = grad
+        taps = [
+            jnp.sum(grad * r.same[k, 8 : 8 + ROWS, :] * r.proj[13 + k : 13 + k + ROWS, at], axis=0, keepdims=True) for k in range(KC)
+        ]
+        taps += [jnp.sum(grad, axis=0, keepdims=True), jnp.zeros((3, TILE), f32)]
+        r.gconv[:, at] = jnp.concatenate(taps, axis=0)
+        total = 0.0
+        for k in range(KC):
+            rows = slice(3 - k, 3 - k + 8 + ROWS)
+            total = total + r.conv[k : k + 1, at] * (r.same[k, rows, :] * r.dpre[slot, rows, :])
+        r.tail[:, at] = total[0:8, :]
+        r.dx[0:HALO, at] = low(jnp.concatenate([jnp.zeros((8, TILE), f32), total[0:8, :]], axis=0))
+        r.dx[HALO:, at] = low(total[8:, :])
+        r.late[:, at] = total[ROWS : ROWS + 8, :]
+
+    reduce_first = Reduce(r.part_a.at[0], r.grad_a.at[0], 48, "columns", red_a, planes)
+    reduce_second = Reduce(r.part_a.at[1], r.grad_a.at[1], 48, "columns", red_b, planes)
+
+    def weights_a(group, k):
+        half = lax.rem(k + 1 + c, 2)
+        at = pl.ds(pl.multiple_of(half * (WIDE // 4), 512), 512)
+        from_ = pl.ds(pl.multiple_of(group * (WIDE // 2) + half * (WIDE // 4), 512), 512)
+        r.part_a[group, :, at] = low(dot(r.normed[...], r.dx[:, from_], TRANS))
+
+    def columns_back(j):
+        last_sums(j)
+        unconvolve(j, r.dxs[:, at_tile(j)])
+
+    r.dx[0:HALO, CH:] = jnp.zeros((HALO, WIDE - CH), jnp.bfloat16)
+    r.dx[HALO:, CH + 128 :] = jnp.zeros((ROWS, WIDE - CH - 128), jnp.bfloat16)
+    loop(0, 8, columns_back)
+    weights_a(0, 0)
+    for d in every:
+        reduce_first.start(d)
+    weights_a(0, 1)
+    reduce_column(1)
+    loop(8, 12, columns_back)
+    for d in every:
+        reduce_first.fold(d)
     dscores = low(r.dscores[...])
     dbproj = dot(dscores, r.cproj[...], TRANS) + dot(r.xso[...], r.dstate[...], TRANS_B)
     dcproj = dot(dscores, r.bproj[...]) + dot(r.dyin[...], r.state[...], TRANS_B)
@@ -1383,36 +1411,12 @@
     )
     step = r.step[...]
     dstep = r.sums[2] + rate * dlog
-    draw = dstep * sigmoid(r.proj[HALO:, CH : CH + 128] + r.heads[0:1, :])
+    draw = dstep * sigmoid(r.proj[HALO:, CH : CH + 128] + r.small_in[8:9, :])
     lanes = iota((1, 128), 1) < H
     draw = jnp.where(lanes, draw, 0.0)
     gbias = jnp.sum(draw, axis=0, keepdims=True)
     glog = jnp.where(lanes, jnp.sum(step * dlog, axis=0, keepdims=True) * rate, 0.0)
-    r.dx[:, CH : CH + 128] = low(draw)
-    r.dx[:, CH + 128 :] = jnp.zeros((ROWS, WIDE - CH - 128), jnp.bfloat16)
-
-    def unconvolve(j, grad):
-        at = at_tile(j)
-        pre = r.pre[:, at]
-        sig = sigmoid(pre)
-        grad = grad * (sig * (1.0 + pre * (1.0 - sig)))
-        r.dpre[0:8, at] = jnp.zeros((8, TILE), f32)
-        r.dpre[8 + ROWS :, at] = jnp.zeros((8, TILE), f32)
-        r.dpre[8 : 8 + ROWS, at] = grad
-        taps = [
-            jnp.sum(grad * r.same[k, 8 : 8 + ROWS, :] * r.proj[13 + k : 13 + k + ROWS, at], axis=0, keepdims=True) for k in range(KC)
-        ]
-        taps += [jnp.sum(grad, axis=0, keepdims=True), jnp.zeros((3, TILE), f32)]
-        r.gconv[:, at] = jnp.concatenate(taps, axis=0)
-        total = 0.0
-        for k in range(KC):
-            rows = slice(3 - k, 3 - k + 8 + ROWS)
-            total = total + r.conv[k : k + 1, at] * (r.same[k, rows, :] * r.dpre[rows, at])
-        r.tail[:, at] = total[0:8, :]
-        r.dx[:, at] = low(total[8:, :])
-        r.dpre[0:8, at] = total[ROWS : ROWS + 8, :]
-
-    loop(0, TILES, lambda j: unconvolve(j, r.dxs[:, at_tile(j)]))
+    r.dx[HALO:, CH : CH + 128] = low(draw)
     unconvolve(TILES, dbproj)
     unconvolve(TILES + 1, dcproj)
     tails = [
@@ -1427,35 +1431,55 @@
     def _():
         r.tail_in[...] = jnp.zeros((8, CH), f32)
 
+    weights_a(1, 0)
+    for d in every:
+        reduce_second.start(d)
+    weights_a(1, 1)
+    reduce_first.sides(3)
+    reduce_column(0)
+    for d in every:
+        reduce_second.fold(d)
+    reduce_first.sides(2)
+    reduce_out.close()
+    reduce_z.close()
     pl.when(z + c < planes)(tails[0].wait_recv)
-    r.dx[ROWS - 16 :, 0:CH] = low(
-        jnp.concatenate([r.dx[ROWS - 16 : ROWS - 8, 0:CH].astype(f32), r.dpre[0:8, :] + r.tail_in[...]], axis=0)
+    r.dx[HALO + ROWS - 16 :, 0:CH] = low(
+        jnp.concatenate([r.dx[HALO + ROWS - 16 : HALO + ROWS - 8, 0:CH].astype(f32), r.late[...] + r.tail_in[...]], axis=0)
     )
 
-    def weights_a(j):
-        at = at_rows(j, 512)
-        r.part_a[:, at] = low(dot(r.normed[...], r.dx[:, at], TRANS))
-
-    loop(0, 4, weights_a)
-    background(100)
-    reduce_a = Reduce(r.part_a, r.grad_a, 48, "columns", red_a, planes)
-    last_steps = reduce_a.steps()
-    for step in last_steps[:8]:
-        step()
-    ngain = jnp.zeros((8, 768), f32)
-    for k in range(8):
-        rows = slice(32 * k, 32 * k + 32)
-        dnormed = dot(r.dz[rows, :], r.wz_full[...], TRANS_B) + dot(r.dx[rows, :], r.wa[...], TRANS_B)
-        u = r.tok[HALO + 32 * k : HALO + 32 * k + 32, :].astype(f32)
+    def back_in(k):
+        at = at_rows(k, 256)
+        r.y[:, at] = dot(r.dz[...], r.wz_full[at, :], TRANS_B) + dot(r.dx[HALO:, :], r.wa[at, :], TRANS_B)
+
+    loop(0, 3, back_in)
+    reduce_first.sides(1)
+    reduce_first.column(3)
+    reduce_second.sides(3)
+    r.ngrad[...] = jnp.zeros((8, 768), f32)
+
+    def norm_back(k):
+        rows = at_rows(k, 16)
+        dnormed = r.y[rows, 0:768]
+        u = r.tok[pl.ds(pl.multiple_of(HALO + 16 * k, 16), 16), :].astype(f32)
         scale = lax.rsqrt(jnp.mean(u * u, axis=-1, keepdims=True) + EPSILON)
         weighed = dnormed * u * scale
-        ngain = ngain + weighed[0:8] + weighed[8:16] + weighed[16:24] + weighed[24:32]
+        r.ngrad[...] = r.ngrad[...] + weighed[0:8] + weighed[8:16]
         a = r.ngain[5:6, :] * dnormed
         grad = scale * (a - u * (scale * scale) * jnp.mean(u * a, axis=-1, keepdims=True))
         r.gtok[rows, :] = low(r.cot_own[rows, :].astype(f32) + grad)
+
+    loop(0, 8, norm_back)
+    reduce_first.sides(0)
+    reduce_first.column(2)
+    reduce_second.sides(2)
+    reduce_second.column(3)
+    loop(8, 16, norm_back)
     grads = Shuffle(r.gtok, r.tokens_out, r.back_sem, back=True)
     grads.start()
-    ngain = jnp.sum(ngain, axis=0, keepdims=True)
+    reduce_first.column(1)
+    reduce_second.sides(1)
+    reduce_second.column(2)
+    ngain = jnp.sum(r.ngrad[...], axis=0, keepdims=True)
     ggain = jnp.sum(r.ggain[...], axis=0, keepdims=True)
     lane_heads = jnp.concatenate([gbias[:, 0:H], glog[:, 0:H], gskip[:, 0:H], jnp.zeros((1, 128 - 3 * H), f32)], axis=1)
     for k in range(16):
@@ -1484,12 +1508,16 @@
 
     loop(0, 16, lambda k: to_all(k, lambda copy: copy.start()))
     r.inbox[c, me] = r.table[me]
-    for step in last_steps[8:]:
-        step()
+    reduce_second.sides(0)
+    reduce_first.column(0)
+    reduce_second.column(1)
+    reduce_first.close()
+    reduce_second.column(0)
+    reduce_second.close()
     loop(0, 16, from_all)
     r.small_out[...] = jnp.sum(jnp.sum(r.inbox[...], axis=0), axis=0)
     loop(0, 16, lambda k: to_all(k, lambda copy: copy.wait_send()))
-    for item in (reduce_out, reduce_z, reduce_a, forward, backward, cots, acts, grads):
+    for item in moves + [gather_a, gather_z, gather_out, reduce_out, reduce_z, reduce_first, reduce_second, forward, backward, cots, acts, grads]:
         item.finish()
     acts.arrived()
     grads.arrived()
@@ -1497,56 +1525,69 @@
     pl.when(z + c > 0)(tails[0].wait_send)
 
 
-def rest(given, planes):
+def block(given, planes):
     f32, bf16 = jnp.float32, jnp.bfloat16
     shape = jax.ShapeDtypeStruct
-    named = rest_scratch(planes)
-    extra = Chain.scratch() + Chain.scratch()
-    extra += Reduce.scratch(48, WIDE, "columns", planes) + Reduce.scratch(48, DI, "columns", planes) + Reduce.scratch(96, 768, "rows", planes)
+    named = block_scratch(planes)
+    extra = Chain.scratch() + Chain.scratch()[:6] + Chain.scratch()[8:]
+    extra += Reduce.scratch(48, WIDE // 2, "columns", planes) + Reduce.scratch(48, WIDE // 2, "columns", planes) + Reduce.scratch(48, DI, "columns", planes)
+    extra += Reduce.scratch(96, 768, "rows", planes)
     return pl.pallas_call(
-        functools.partial(rest_kernel, planes, list(named)),
+        functools.partial(block_kernel, planes, list(named)),
         out_shape=[
-            shape((2, 128, 768), bf16), shape((2, 128, 768), bf16), shape((48, WIDE), f32),
+            shape((2, 128, 768), bf16), shape((2, 128, 768), bf16), shape((2, 48, WIDE // 2), f32),
             shape((48, DI), f32), shape((96, 768), f32), shape((8, 128), f32),
         ],
-        in_specs=[VMEM] * len(REST_IN),
-        out_specs=[VMEM] * len(REST_OUT),
+        in_specs=[VMEM] * len(GIVEN),
+        out_specs=[VMEM] * len(MADE),
         scratch_shapes=list(named.values()) + extra,
-        compiler_params=pltpu.CompilerParams(collective_id=1, has_side_effects=True, vmem_limit_bytes=62 << 20),
+        compiler_params=pltpu.CompilerParams(collective_id=0, has_side_effects=True, vmem_limit_bytes=62 << 20),
     )(*given)
+
+
+def deliver_kernel(acts, tokens, grad_a, grad_z, grad_out, sums, *out):
+    out[0][...] = acts[...]
+    out[1][...] = tokens[...]
+    out[2][...] = sums[5:6, 0:48]
+    out[3][:, 0:DI] = grad_z[...]
+    out[3][:, DI : DI + WIDE // 2] = grad_a[0]
+    out[3][:, DI + WIDE // 2 :] = grad_a[1, :, 0 : CH + H - WIDE // 2]
+    out[4][...] = sums[0:4, 0:112]
+    out[5][...] = sums[4:5, 0:112]
+    out[6][...] = sums[7:8, 0:H]
+    out[7][...] = sums[7:8, H : 2 * H]
+    out[8][...] = sums[7:8, 2 * H : 3 * H]
+    out[9][...] = sums[6:7, 0:96]
+    out[10][...] = grad_out[...]
+
+
+def deliver(made):
+    f32, bf16 = jnp.float32, jnp.bfloat16
+    shapes = [
+        ((2, 128, 768), bf16), ((2, 128, 768), bf16), ((1, 48), f32), ((48, DI + CH + H), f32), ((4, 112), f32), ((1, 112), f32),
+        ((1, H), f32), ((1, H), f32), ((1, H), f32), ((1, 96), f32), ((96, 768), f32),
+    ]
+    return pl.pallas_call(
+        deliver_kernel,
+        out_shape=[jax.ShapeDtypeStruct(*s) for s in shapes],
+        in_specs=[VMEM] * len(made),
+        out_specs=[VMEM] * len(shapes),
+    )(*made)
 
 
 def fast_body(
     planes, tokens, cotangent, segments, norm_gain, w_in, conv_weight, conv_bias, step_bias, log_rate, skip_gain, gate_gain, w_out
 ):
-    f32 = jnp.float32
-    segf = jnp.broadcast_to((segments.astype(f32) + 1.0)[:, 0, None, :], (2, 8, 128))
-
-    def padded(rows):
-        return jnp.pad(rows.astype(f32), ((0, 0), (0, 128 - rows.shape[1])))
-
-    nothing = jnp.zeros((1, 128), f32)
-    small = jnp.concatenate(
-        [padded(conv_weight), padded(conv_bias[None]), padded(norm_gain[None]), padded(gate_gain[None]), nothing], axis=0
-    )
-    heads = jnp.concatenate([padded(jnp.stack([step_bias, log_rate, skip_gain])), jnp.zeros((5, 128), f32)], axis=0)
-    wa = jnp.pad(w_in[:, DI:], ((0, 0), (0, WIDE - (w_in.shape[1] - DI))))
-    wa_full, table, tok, seg, normed, proj, conv, gain, ngain = enter(tokens[:, 0], segf, small, wa, planes)
-    acts, grad_tokens, grad_a, grad_z, grad_out, sums = rest(
-        (wa_full, tok, seg, normed, proj, conv, gain, ngain, heads, w_in[:, :DI], w_out, cotangent[:, 0]), planes
-    )
+    def at_row(row, values):
+        values = values.astype(jnp.float32).reshape(-1, values.shape[-1])
+        return jnp.pad(values, ((row, 16 - row - values.shape[0]), (0, 128 - values.shape[1])))
+
+    rows = ((0, conv_weight), (4, conv_bias), (5, norm_gain), (6, gate_gain), (8, step_bias), (9, log_rate), (10, skip_gain))
+    small = sum(at_row(row, values) for row, values in rows)
+    made = block((tokens[:, 0], cotangent[:, 0], segments[:, 0], small, w_in, w_out), planes)
+    out = deliver(made)
     return (
-        acts[:, None],
-        grad_tokens[:, None],
-        sums[5, 0:48],
-        jnp.concatenate([grad_z, grad_a[:, : w_in.shape[1] - DI]], axis=1),
-        sums[0:4, 0:112],
-        sums[4, 0:112],
-        sums[7, 0:H],
-        sums[7, H : 2 * H],
-        sums[7, 2 * H : 3 * H],
-        sums[6, 0:96],
-        grad_out,
+        out[0][:, None], out[1][:, None], out[2][0], out[3], out[4], out[5][0], out[6][0], out[7][0], out[8][0], out[9][0], out[10],
     )
 
 

time: 203 us -> 137 us (0.67); the launches traced: 202 us -> 134 us
  Pallas kernels: 176 us -> 132 us
  local copies, waits for them, and re-layouts: 19.9 us -> 0.7 us
  other arithmetic: 5.24 us -> 0.61 us
    pallas_call x2, Pallas kernels: 176 us -> 132 us  [the longest x1 129 us: block(): pl.pallas_call(functools.partial(block_kernel, planes, list(named)), out_...]
    unnamed x23 -> x14, local copies, waits for them, and re-layouts: 9.58 us -> 0.7 us
    squeeze x4 -> x0, local copies, waits for them, and re-layouts: 4.95 us -> none  [the longest x1 1.36 us: fast_body(): sums[7, 2 * H:3 * H]]
    slice x4 -> x0, local copies, waits for them, and re-layouts: 4.77 us -> none  [the longest x1 1.58 us: fast_body(): w_in[:, :DI]]
where the time goes in v3:
time: 137 us; the launch traced here: 134 us
  Pallas kernels  132 us (96%)
    pallas_call x1, Pallas kernels, block(): pl.pallas_call(functools.partial(block_kernel, planes, list(named)), out_...  129 us

profile of v3, /device:TPU:0, one launch (start us, length us, event | category | flops | bytes accessed | tf_op | source)
XLA Modules:
  0.0 134.0 jit_solution(12682299820431139603)
XLA Ops:
  0.6 0.0 copy-start.6
  0.7 0.0 copy-start.2
  0.7 0.0 copy-start.3
  0.7 0.0 copy-start.4
  0.7 0.0 copy-start.5
  0.7 0.0 copy-start
  0.7 0.0 copy-start.1
  0.7 0.6 copy-done.6
  1.3 0.0 copy-done.2
  1.3 0.0 copy-done.3
  1.3 0.0 copy-done.4
  1.3 0.0 copy-done.5
  1.4 0.0 copy-done
  1.4 0.0 copy-done.1
  1.4 0.6 pad_add_fusion.refs_3_
  2.0 129.2 %shard_map.203 = (bf16[2,128,768]{2,1,0:T(8,128)(2,1)}, bf16[2,128,768]{2,1,0:T(8,128)(2,1)}, f32[2,48,1024]{2,1,0:T(8,128)}, f32[48,1536]{1,0:T(8,128)}, f32[96,768]{1,0:T(8,128)}, /*index=5*/f32[8,128]{1,0:T(8,128)}) custom-call(bf16[2,128,768]{2,1,0:T(8,128)(2,1)} %bitcast.21, bf16[2,128,768]{2,1,0:T(8,128)(2,1)} %bitcast.22, s32[2,128]{1,0:T(2,128)} %bitcast.23, ...), custom_call_target="tpu_custom_call" | custom-call | tf_op jit(solution)/shard_map/pallas_call | solution.py:1535
  131.2 2.7 %shard_map.204 = (bf16[2,128,768]{2,1,0:T(8,128)(2,1)}, bf16[2,128,768]{2,1,0:T(8,128)(2,1)}, f32[1,48]{1,0:T(1,128)}, f32[48,3352]{1,0:T(8,128)}, f32[4,112]{1,...) custom-call(bf16[2,128,768]{2,1,0:T(8,128)(2,1)} %get-tuple-element., ...), custom_call_target="tpu_custom_call" | custom-call | tf_op jit(solution)/shard_map/pallas_call | solution.py:1570
Async XLA Ops:
  0.6 0.7 copy-start.6
  0.7 0.7 copy-start.2
  0.7 0.7 copy-start.3
  0.7 0.7 copy-start.4
  0.7 0.7 copy-start.5
  0.7 0.7 copy-start
  0.7 0.7 copy-start.1

commit v4 on v3

--- a/solution.py
+++ b/solution.py
@@ -317,7 +317,7 @@
     return at % 2, (at // 2) % 2, at // 4, core
 
 
-def meet_all(planes):
+def greet_all(planes):
     barrier = pltpu.get_barrier_semaphore()
     me = lax.axis_index("seq")
     core = lax.axis_index("dp")
@@ -334,7 +334,10 @@
         return carry
 
     lax.fori_loop(0, count, greet, 0)
-    pl.semaphore_wait(barrier, 2 * count - 1)
+
+
+def meet_all(planes):
+    pl.semaphore_wait(pltpu.get_barrier_semaphore(), 8 * planes - 1)
 
 
 COLUMN, SIDE_X, SIDE_Y, HALF_X, HALF_Y, MATE_Z, MATE_X, MATE_Y, MATE_HX, MATE_HY = range(10)
@@ -632,15 +635,22 @@
         region = self.out.at[:, pl.ds(left, self.half)]
         self.copy(self.LAST, 0, region, region, (1 - self.core, chip(self.x, self.y, self.z))).wait_recv()
         last.wait_send()
+
+    def drain(self, kinds):
         for distance in range(self.planes):
 
             def act(far, sign):
-                for kind in (self.MATE, self.HX, self.HY, self.X, self.Y):
-                    self.move(kind, far).wait_send()
-                if distance:
-                    self.move(self.COLUMN, far).wait_send()
+                for kind in kinds:
+                    if distance or kind != self.COLUMN:
+                        self.move(kind, far).wait_send()
 
             self.each(distance, act)
+
+    def drain_early(self):
+        self.drain((self.MATE, self.HX, self.HY))
+
+    def drain_late(self):
+        self.drain((self.X, self.Y, self.COLUMN))
 
 
 class Chain:
@@ -971,7 +981,7 @@
     return {
         "wa": v((768, WIDE), bf16), "wa_sem": gather_sems(planes), "tok": v((HALO + ROWS, 768), bf16), "seg": v((3, 8, 128), f32),
         "normed": v((HALO + ROWS, 768), bf16), "proj": v((HALO + ROWS, WIDE), f32), "conv": v((8, CH), f32), "gain": v((8, DI), f32),
-        "ngain": v((8, 768), f32), "ngrad": v((8, 768), f32), "given": v((16, 8, 128), f32), "numbers": v((2, 8, 128), f32),
+        "ngain": v((8, 768), f32), "ngrad": v((8, 768), f32), "scale": v((ROWS, 128), f32), "given": v((16, 8, 128), f32), "numbers": v((2, 8, 128), f32),
         "tok_sem": two, "end_sem": two, "seg_sem": two, "segend_sem": two, "given_sem": dma((2, 16)),
         "wz_full": v((768, DI), bf16), "wout_full": v((DI, 768), bf16), "wz_sem": gather_sems(planes), "wout_sem": gather_sems(planes),
         "cot_own": v((ROWS, 768), bf16), "cot_sem": two, "act_sem": two, "back_sem": two,
@@ -987,7 +997,7 @@
         "dz": v((ROWS, DI), bf16), "dy": v((ROWS, DI), bf16), "dyin": v((ROWS, DI), bf16),
         "ggain": v((8, DI), f32), "gskip": v((8, DI), f32),
         "dscores": v((ROWS, ROWS), f32), "dxs": v((ROWS, DI), f32), "sums": v((3, ROWS, 128), f32),
-        "dpre": v((2, ROWS + HALO, TILE), f32), "late": v((8, CH), f32), "dx": v((HALO + ROWS, WIDE), bf16), "tail": v((8, CH), f32), "tail_in": v((8, CH), f32), "tail_sem": dma((2,)),
+        "dpre": v((KC, ROWS + HALO, TILE), f32), "late": v((8, CH), f32), "dx": v((HALO + ROWS, WIDE), bf16), "tail": v((8, CH), f32), "tail_in": v((8, CH), f32), "tail_sem": dma((2,)),
         "gconv": v((8, CH), f32), "gtok": v((ROWS, 768), bf16),
         "table": v((16, 8, 128), f32), "inbox": v((2, 16, 8, 128), f32), "table_sem": dma((2, 2, 16)),
         "part_a": v((2, 768, WIDE // 2), bf16), "part_z": v((768, DI), bf16), "part_out": v((DI, 768), bf16),
@@ -1003,6 +1013,7 @@
     me = chip(x, y, z)
     mate = (1 - c, me)
     f32 = jnp.float32
+    greet_all(planes)
     r.wa[pl.ds(pl.multiple_of(me * 48, 16), 48), 0:CH] = r.w_in[:, DI : DI + CH]
     step_columns = r.w_in[:, DI + CH :]
     fill = jnp.zeros((48, WIDE - CH - H), step_columns.dtype)
@@ -1030,9 +1041,9 @@
         ToAll(r.given, r.given_sem, planes),
     ]
     meet_all(planes)
-    gather_a.begin()
     for item in moves:
         item.start()
+    gather_a.begin()
     gather_a.column(1)
     gather_a.sides(0)
     for item in moves:
@@ -1042,15 +1053,12 @@
     r.ngain[...] = jnp.concatenate([r.given[k, :, 0:48] for k in range(16)], axis=1)
     gather_a.column(2)
     gather_a.column(3)
-    gather_z.begin_column()
-    gather_out.begin_column()
     gather_a.sides(1)
     gather_a.diagonal(0)
     u = r.tok[...].astype(f32)
     r.normed[...] = low(u * lax.rsqrt(jnp.mean(u * u, axis=-1, keepdims=True) + EPSILON) * r.ngain[5:6, :])
+    gather_z.begin_column()
     gather_a.sides(2)
-    for gather in (gather_z, gather_out):
-        gather.begin_sides()
     gather_a.diagonal(1)
 
     for k in range(3):
@@ -1060,21 +1068,14 @@
         r.same[k] = jnp.zeros((ROWS + HALO, 128), f32)
         r.same[k, 8 : 8 + ROWS, :] = jnp.where(r.segcol[125 + k : 125 + k + ROWS, :] == seg, 1.0, 0.0)
     gather_a.sides(3)
+    gather_z.begin_sides()
     gather_a.diagonal(2)
-    for gather in (gather_z, gather_out):
-        for d in range(1, planes):
-            gather.column(d)
+    for d in range(1, planes):
+        gather_z.column(d)
     cots.start()
+    gather_out.begin()
     gather_a.diagonal(3)
     gather_a.whole_here()
-
-    def sides(d):
-        gather_z.sides(d)
-        gather_out.sides(d)
-
-    def diagonal(d):
-        gather_z.diagonal(d)
-        gather_out.diagonal(d)
 
     def project(k):
         at_k = pl.ds(pl.multiple_of(k * 512, 512), 512)
@@ -1150,7 +1151,9 @@
     r.scores[...] = dot(r.cproj[...], r.bproj[...], TRANS_B)
     r.einx[...] = dot(spreads[1][1], spread_matrix(DI))
     r.cumx[...] = dot(spreads[3][1], spread_matrix(DI))
-    sides(0)
+    gather_z.sides(0)
+    for d in range(1, planes):
+        gather_out.column(d)
 
     first_half = iota((1, TILE), 1) < P_SIZE
 
@@ -1190,16 +1193,24 @@
     turn(forward, [1, 0, 0, 0])
     loop(0, 4, within)
     turn(forward, [0, 1, 0, 0])
-    sides(1)
-    diagonal(0)
+    gather_z.sides(1)
+    gather_z.diagonal(0)
+    gather_out.sides(0)
     loop(4, 8, within)
     turn(forward, [0, 0, 1, 0])
-    sides(2)
-    diagonal(1)
+    gather_z.sides(2)
+    gather_z.diagonal(1)
+    gather_out.sides(1)
+    gather_out.diagonal(0)
     loop(8, 12, within)
-    sides(3)
+    gather_z.sides(3)
+    gather_z.diagonal(2)
+    for item in moves + [gather_a]:
+        item.finish()
     turn(forward, [0, 0, 0, 1])
-    diagonal(2)
+    gather_out.sides(2)
+    gather_out.diagonal(1)
+    gather_z.diagonal(3)
     forward.close()
 
     def carried(j):
@@ -1207,44 +1218,60 @@
         r.y[:, at] = r.y[:, at] + r.einx[:, at] * dot(r.cproj[...], r.state[:, at])
 
     loop(0, TILES, carried)
-    diagonal(3)
     gather_z.whole_here()
+
+    def project_z(j):
+        at = at_rows(j, 512)
+        r.z[:, at] = dot(r.normed[HALO:, :], r.wz_full[:, at])
+
+    loop(0, 3, project_z)
+    gather_out.sides(3)
+    gather_out.diagonal(2)
+
+    def gated_values(rows):
+        gate_in = r.z[rows, :]
+        sig = sigmoid(gate_in)
+        mixed = r.y[rows, :] + r.skipx[0:1, :] * r.inner[rows, :]
+        return gate_in, sig, mixed, mixed * (gate_in * sig)
+
+    def gate(k):
+        rows = at_rows(k, 16)
+        _, _, _, v = gated_values(rows)
+        scale = lax.rsqrt(jnp.mean(v * v, axis=-1, keepdims=True) + EPSILON)
+        r.scale[rows, :] = jnp.broadcast_to(scale, (16, 128))
+        r.gated[rows, :] = low(v * scale * r.gain[6:7, :])
+
+    loop(0, ROWS // 16, gate)
+    gather_out.diagonal(3)
     gather_out.whole_here()
     cots.arrived()
 
-    def projections(j):
-        at = pl.ds(pl.multiple_of(j * 512, 512), 512)
-        r.z[:, at] = dot(r.normed[HALO:, :], r.wz_full[:, at])
+    def project_cot(j):
+        at = at_rows(j, 512)
         r.dxs[:, at] = dot(r.cot_own[...], r.wout_full[at, :], TRANS_B)
 
-    loop(0, 3, projections)
+    loop(0, 3, project_cot)
     r.ggain[...] = jnp.zeros((8, DI), f32)
     r.gskip[...] = jnp.zeros((8, DI), f32)
 
-    def gate(k):
+    def gate_back(k):
         rows = at_rows(k, 16)
-        inner, gate_in = r.inner[rows, :], r.z[rows, :]
-        mixed = r.y[rows, :] + r.skipx[0:1, :] * inner
-        sig = sigmoid(gate_in)
-        silu = gate_in * sig
-        v = mixed * silu
-        scale = lax.rsqrt(jnp.mean(v * v, axis=-1, keepdims=True) + EPSILON)
-        gain = r.gain[6:7, :]
-        r.gated[rows, :] = low(v * scale * gain)
+        gate_in, sig, mixed, v = gated_values(rows)
+        scale = r.scale[rows, 0:1]
         dgated = r.dxs[rows, :]
         weighed = dgated * (v * scale)
         r.ggain[...] = r.ggain[...] + weighed[0:8, :] + weighed[8:16, :]
-        a = gain * dgated
+        a = r.gain[6:7, :] * dgated
         dv = scale * (a - v * (scale * scale) * jnp.mean(v * a, axis=-1, keepdims=True))
-        dmixed = dv * silu
+        dmixed = dv * (gate_in * sig)
         r.z[rows, :] = dmixed
         r.dy[rows, :] = low(dmixed)
         r.dyin[rows, :] = low(dmixed * r.einx[rows, :])
         r.dz[rows, :] = low(dv * mixed * (sig * (1.0 + gate_in * (1.0 - sig))))
-        skip = dmixed * inner
+        skip = dmixed * r.inner[rows, :]
         r.gskip[...] = r.gskip[...] + skip[0:8, :] + skip[8:16, :]
 
-    loop(0, ROWS // 16, gate)
+    loop(0, ROWS // 16, gate_back)
 
     def incoming(j):
         at = at_tile(j)
@@ -1258,16 +1285,24 @@
     reduce_z = Reduce(r.part_z, r.grad_z, 48, "columns", red_z, planes)
     every = range(planes - 1, -1, -1)
 
-    def weights_out(j):
-        at = at_rows(j, 256)
+    def project_out(k):
+        at = at_rows(k, 256)
+        r.act_own[:, at] = low(r.tok[HALO:, at].astype(f32) + dot(r.gated[...], r.wout_full[:, at]))
+
+    loop(0, 3, project_out)
+    acts = Shuffle(r.act_own, r.act_out, r.act_sem, back=True)
+    acts.start()
+
+    def weights_out(k):
+        far = lax.rem(z + 1 + k, planes)
+        at = pl.ds(pl.multiple_of(far * (DI // planes), 128), DI // planes)
         r.part_out[at, :] = low(dot(r.gated[:, at], r.cot_own[...], TRANS))
+        reduce_out.move(reduce_out.MATE, far).start()
 
     loop(0, 2, weights_out)
     backward.merge()
     turn(backward, [1, 0, 0, 0])
-    loop(2, 6, weights_out)
-    for d in every:
-        reduce_out.start(d)
+    loop(2, planes, weights_out)
 
     def weights_z(k):
         half = lax.rem(k // 3 + 1 + c, 2)
@@ -1277,20 +1312,18 @@
     loop(0, 3, weights_z)
     for d in every:
         reduce_z.start(d)
-    loop(3, 6, weights_z)
     for d in every:
         reduce_out.fold(d)
     turn(backward, [0, 1, 0, 0])
+    loop(3, 6, weights_z)
     for d in every:
         reduce_z.fold(d)
 
-    def project_out(k):
+    def back_z(k):
         at = at_rows(k, 256)
-        r.act_own[:, at] = low(r.tok[HALO:, at].astype(f32) + dot(r.gated[...], r.wout_full[:, at]))
-
-    loop(0, 3, project_out)
-    acts = Shuffle(r.act_own, r.act_out, r.act_sem, back=True)
-    acts.start()
+        r.einx[:, at] = dot(r.dz[...], r.wz_full[at, :], TRANS_B)
+
+    loop(0, 3, back_z)
 
     def reduce_sides(d):
         reduce_out.sides(d)
@@ -1322,6 +1355,9 @@
         r.dxs[128:256, at] = lower
         gain = r.dy[:, at].astype(f32) * r.y[:, at] - r.xs[:, at].astype(f32) * r.dxs[:, at]
         r.sums[0] = r.sums[0] + head_sums(gain, j)
+        inside = r.dxs[:, at]
+        r.sums[2] = r.sums[2] + head_sums(r.inner[:, at] * inside, j)
+        r.dxs[:, at] = r.skipx[0:1, at] * r.z[:, at] + r.stepx[:, at] * inside
 
     loop(0, 2, within_back)
     turn(backward, [0, 0, 1, 0])
@@ -1334,37 +1370,33 @@
     reduce_column(2)
     turn(backward, [0, 0, 0, 1])
     loop(8, 12, within_back)
+    for item in (gather_z, gather_out, cots, forward):
+        item.finish()
+    share.wait_send()
     backward.close()
     reduce_sides(0)
 
     def last_sums(j):
         at = at_tile(j)
-        xs = r.xs[:, at].astype(f32)
         far = r.eoutx[:, at] * dot(r.bproj[...], r.dstate[:, at])
-        total = r.dxs[:, at] + far
-        r.sums[1] = r.sums[1] + head_sums(xs * far, j)
-        inner = r.inner[:, at]
-        r.sums[2] = r.sums[2] + head_sums(inner * total, j)
-        r.dxs[:, at] = r.skipx[0:1, at] * r.z[:, at] + r.stepx[:, at] * total
+        r.sums[1] = r.sums[1] + head_sums(r.inner[:, at] * far, j)
+        return r.dxs[:, at] + r.stepx[:, at] * far
 
     def unconvolve(j, grad):
         at = at_tile(j)
         pre = r.pre[:, at]
         sig = sigmoid(pre)
         grad = grad * (sig * (1.0 + pre * (1.0 - sig)))
-        slot = j % 2
-        r.dpre[slot, 0:8, :] = jnp.zeros((8, TILE), f32)
-        r.dpre[slot, 8 + ROWS :, :] = jnp.zeros((8, TILE), f32)
-        r.dpre[slot, 8 : 8 + ROWS, :] = grad
-        taps = [
-            jnp.sum(grad * r.same[k, 8 : 8 + ROWS, :] * r.proj[13 + k : 13 + k + ROWS, at], axis=0, keepdims=True) for k in range(KC)
-        ]
+        taps = []
+        for k in range(KC):
+            kept = grad if k == KC - 1 else grad * r.same[k, 8 : 8 + ROWS, :]
+            r.dpre[k, 8 : 8 + ROWS, :] = kept
+            taps.append(jnp.sum(kept * r.proj[13 + k : 13 + k + ROWS, at], axis=0, keepdims=True))
         taps += [jnp.sum(grad, axis=0, keepdims=True), jnp.zeros((3, TILE), f32)]
         r.gconv[:, at] = jnp.concatenate(taps, axis=0)
         total = 0.0
         for k in range(KC):
-            rows = slice(3 - k, 3 - k + 8 + ROWS)
-            total = total + r.conv[k : k + 1, at] * (r.same[k, rows, :] * r.dpre[slot, rows, :])
+            total = total + r.conv[k : k + 1, at] * r.dpre[k, 3 - k : 3 - k + 8 + ROWS, :]
         r.tail[:, at] = total[0:8, :]
         r.dx[0:HALO, at] = low(jnp.concatenate([jnp.zeros((8, TILE), f32), total[0:8, :]], axis=0))
         r.dx[HALO:, at] = low(total[8:, :])
@@ -1380,11 +1412,11 @@
         r.part_a[group, :, at] = low(dot(r.normed[...], r.dx[:, from_], TRANS))
 
     def columns_back(j):
-        last_sums(j)
-        unconvolve(j, r.dxs[:, at_tile(j)])
+        unconvolve(j, last_sums(j))
 
     r.dx[0:HALO, CH:] = jnp.zeros((HALO, WIDE - CH), jnp.bfloat16)
     r.dx[HALO:, CH + 128 :] = jnp.zeros((ROWS, WIDE - CH - 128), jnp.bfloat16)
+    r.dpre[...] = jnp.zeros((KC, ROWS + HALO, TILE), f32)
     loop(0, 8, columns_back)
     weights_a(0, 0)
     for d in every:
@@ -1406,11 +1438,11 @@
     strict = jnp.where(iota((ROWS, ROWS), 0) > iota((ROWS, ROWS), 1), 1.0, 0.0)
     dlog = (
         jnp.dot(upper, r.sums[0], precision=HIGHEST, preferred_element_type=f32)
-        + jnp.dot(strict, r.sums[1], precision=HIGHEST, preferred_element_type=f32)
+        + jnp.dot(strict, r.step[...] * r.sums[1], precision=HIGHEST, preferred_element_type=f32)
         + at_end
     )
     step = r.step[...]
-    dstep = r.sums[2] + rate * dlog
+    dstep = r.sums[1] + r.sums[2] + rate * dlog
     draw = dstep * sigmoid(r.proj[HALO:, CH : CH + 128] + r.small_in[8:9, :])
     lanes = iota((1, 128), 1) < H
     draw = jnp.where(lanes, draw, 0.0)
@@ -1449,7 +1481,7 @@
 
     def back_in(k):
         at = at_rows(k, 256)
-        r.y[:, at] = dot(r.dz[...], r.wz_full[at, :], TRANS_B) + dot(r.dx[HALO:, :], r.wa[at, :], TRANS_B)
+        r.y[:, at] = r.einx[:, at] + dot(r.dx[HALO:, :], r.wa[at, :], TRANS_B)
 
     loop(0, 3, back_in)
     reduce_first.sides(1)
@@ -1508,21 +1540,31 @@
 
     loop(0, 16, lambda k: to_all(k, lambda copy: copy.start()))
     r.inbox[c, me] = r.table[me]
+    for item in (reduce_out, reduce_z):
+        item.drain_early()
+        item.drain_late()
+        item.finish()
+    for item in (backward, acts):
+        item.finish()
+    acts.arrived()
     reduce_second.sides(0)
     reduce_first.column(0)
     reduce_second.column(1)
     reduce_first.close()
+    reduce_first.drain_early()
+    reduce_second.drain_early()
+    reduce_first.drain_late()
+    loop(0, 16, lambda k: to_all(k, lambda copy: copy.wait_send()))
+    pl.when(z + c > 0)(tails[0].wait_send)
     reduce_second.column(0)
     reduce_second.close()
     loop(0, 16, from_all)
     r.small_out[...] = jnp.sum(jnp.sum(r.inbox[...], axis=0), axis=0)
-    loop(0, 16, lambda k: to_all(k, lambda copy: copy.wait_send()))
-    for item in moves + [gather_a, gather_z, gather_out, reduce_out, reduce_z, reduce_first, reduce_second, forward, backward, cots, acts, grads]:
-        item.finish()
-    acts.arrived()
+    reduce_second.drain_late()
+    grads.finish()
     grads.arrived()
-    share.wait_send()
-    pl.when(z + c > 0)(tails[0].wait_send)
+    reduce_first.finish()
+    reduce_second.finish()
 
 
 def block(given, planes):

time: 137 us -> 134 us (0.978); the launches traced: 134 us -> 133 us
  no operation moved by 1% of the time
where the time goes in v4:
time: 134 us; the launch traced here: 133 us
  Pallas kernels  131 us (98%)
    pallas_call x1, Pallas kernels, block(): pl.pallas_call(functools.partial(block_kernel, planes, list(named)), out_...  128 us

profile of v4, /device:TPU:0, one launch (start us, length us, event | category | flops | bytes accessed | tf_op | source)
XLA Modules:
  0.0 132.6 jit_solution(11285563089371300439)
XLA Ops:
  0.6 0.0 copy-start.6
  0.7 0.0 copy-start.2
  0.7 0.0 copy-start.3
  0.7 0.0 copy-start.4
  0.7 0.0 copy-start.5
  0.7 0.0 copy-start
  0.7 0.0 copy-start.1
  0.7 0.6 copy-done.6
  1.3 0.0 copy-done.2
  1.3 0.0 copy-done.3
  1.3 0.0 copy-done.4
  1.3 0.0 copy-done.5
  1.4 0.0 copy-done
  1.4 0.0 copy-done.1
  1.4 0.6 pad_add_fusion.refs_3_
  2.0 127.9 %shard_map.203 = (bf16[2,128,768]{2,1,0:T(8,128)(2,1)}, bf16[2,128,768]{2,1,0:T(8,128)(2,1)}, f32[2,48,1024]{2,1,0:T(8,128)}, f32[48,1536]{1,0:T(8,128)}, f32[96,768]{1,0:T(8,128)}, /*index=5*/f32[8,128]{1,0:T(8,128)}) custom-call(bf16[2,128,768]{2,1,0:T(8,128)(2,1)} %bitcast.21, bf16[2,128,768]{2,1,0:T(8,128)(2,1)} %bitcast.22, s32[2,128]{1,0:T(2,128)} %bitcast.23, ...), custom_call_target="tpu_custom_call" | custom-call | tf_op jit(solution)/shard_map/pallas_call | solution.py:1577
  129.9 2.7 %shard_map.204 = (bf16[2,128,768]{2,1,0:T(8,128)(2,1)}, bf16[2,128,768]{2,1,0:T(8,128)(2,1)}, f32[1,48]{1,0:T(1,128)}, f32[48,3352]{1,0:T(8,128)}, f32[4,112]{1,...) custom-call(bf16[2,128,768]{2,1,0:T(8,128)(2,1)} %get-tuple-element., ...), custom_call_target="tpu_custom_call" | custom-call | tf_op jit(solution)/shard_map/pallas_call | solution.py:1612
Async XLA Ops:
  0.6 0.7 copy-start.6
  0.7 0.7 copy-start.2
  0.7 0.7 copy-start.3
  0.7 0.7 copy-start.4
  0.7 0.7 copy-start.5
  0.7 0.7 copy-start
  0.7 0.7 copy-start.1

commit v5 on v4

--- a/solution.py
+++ b/solution.py
@@ -929,11 +929,15 @@
 
 
 def loop(low_end, high_end, act):
-    def one(k, carry):
-        act(k)
+    count = high_end - low_end
+    width = next(w for w in (4, 3, 2, 1) if count % w == 0)
+
+    def several(k, carry):
+        for i in range(width):
+            act(low_end + width * k + i)
         return carry
 
-    lax.fori_loop(low_end, high_end, one, 0)
+    lax.fori_loop(0, count // width, several, 0)
 
 
 def iota(shape, dim):
@@ -985,10 +989,10 @@
         "tok_sem": two, "end_sem": two, "seg_sem": two, "segend_sem": two, "given_sem": dma((2, 16)),
         "wz_full": v((768, DI), bf16), "wout_full": v((DI, 768), bf16), "wz_sem": gather_sems(planes), "wout_sem": gather_sems(planes),
         "cot_own": v((ROWS, 768), bf16), "cot_sem": two, "act_sem": two, "back_sem": two,
-        "segcol": v((384, 128), f32), "same": v((KC, ROWS + HALO, 128), f32),
+        "segcol": v((384, 128), f32), "same": v((KC - 1, ROWS, 128), f32),
         "pre": v((ROWS, CH), f32), "inner": v((ROWS, DI), f32), "bproj": v((ROWS, N), bf16), "cproj": v((ROWS, N), bf16),
         "cumt": v((H, 8, ROWS), f32), "bar": v((ROWS, ROWS), f32), "scores": v((ROWS, ROWS), f32),
-        "step": v((ROWS, 128), f32), "cum": v((ROWS, 128), f32), "ein": v((ROWS, 128), f32), "eout": v((ROWS, 128), f32),
+        "step": v((ROWS, 128), f32), "ein": v((ROWS, 128), f32), "eout": v((ROWS, 128), f32),
         "stepx": v((ROWS, DI), f32), "einx": v((ROWS, DI), f32), "eoutx": v((ROWS, DI), f32), "cumx": v((ROWS, DI), f32),
         "xs": v((ROWS, DI), bf16), "xso": v((ROWS, DI), bf16),
         "part": v((N, DI), f32), "factors": v((2, 8, DI), f32), "factor_sem": dma((2,)), "skipx": v((8, DI), f32),
@@ -1064,9 +1068,8 @@
     for k in range(3):
         r.segcol[128 * k : 128 * k + 128, :] = jnp.transpose(jnp.broadcast_to(r.seg[k, 0:1, :], (128, 128)))
     seg = r.segcol[128:384, :]
-    for k in range(KC):
-        r.same[k] = jnp.zeros((ROWS + HALO, 128), f32)
-        r.same[k, 8 : 8 + ROWS, :] = jnp.where(r.segcol[125 + k : 125 + k + ROWS, :] == seg, 1.0, 0.0)
+    for k in range(KC - 1):
+        r.same[k] = jnp.where(r.segcol[125 + k : 125 + k + ROWS, :] == seg, 1.0, 0.0)
     gather_a.sides(3)
     gather_z.begin_sides()
     gather_a.diagonal(2)
@@ -1087,7 +1090,8 @@
         at = at_tile(j)
         total = jnp.broadcast_to(r.conv[4:5, at], (ROWS, TILE))
         for k in range(KC):
-            total = total + r.conv[k : k + 1, at] * r.proj[13 + k : 13 + k + ROWS, at] * r.same[k, 8 : 8 + ROWS, :]
+            term = r.conv[k : k + 1, at] * r.proj[13 + k : 13 + k + ROWS, at]
+            total = total + (term if k == KC - 1 else term * r.same[k])
         r.pre[:, at] = total
         return total * sigmoid(total)
 
@@ -1100,7 +1104,6 @@
     lower = jnp.where(iota((ROWS, ROWS), 0) >= iota((ROWS, ROWS), 1), 1.0, 0.0)
     cum = jnp.dot(lower, step * rate, precision=HIGHEST, preferred_element_type=f32)
     r.step[...] = step
-    r.cum[...] = cum
     across = jnp.transpose(cum)
     for h in range(H):
         r.cumt[h] = jnp.broadcast_to(across[h : h + 1, :], (8, ROWS))
@@ -1255,12 +1258,12 @@
     r.gskip[...] = jnp.zeros((8, DI), f32)
 
     def gate_back(k):
-        rows = at_rows(k, 16)
+        rows = at_rows(k, 32)
         gate_in, sig, mixed, v = gated_values(rows)
         scale = r.scale[rows, 0:1]
         dgated = r.dxs[rows, :]
         weighed = dgated * (v * scale)
-        r.ggain[...] = r.ggain[...] + weighed[0:8, :] + weighed[8:16, :]
+        r.ggain[...] = r.ggain[...] + weighed[0:8, :] + weighed[8:16, :] + weighed[16:24, :] + weighed[24:32, :]
         a = r.gain[6:7, :] * dgated
         dv = scale * (a - v * (scale * scale) * jnp.mean(v * a, axis=-1, keepdims=True))
         dmixed = dv * (gate_in * sig)
@@ -1269,9 +1272,9 @@
         r.dyin[rows, :] = low(dmixed * r.einx[rows, :])
         r.dz[rows, :] = low(dv * mixed * (sig * (1.0 + gate_in * (1.0 - sig))))
         skip = dmixed * r.inner[rows, :]
-        r.gskip[...] = r.gskip[...] + skip[0:8, :] + skip[8:16, :]
-
-    loop(0, ROWS // 16, gate_back)
+        r.gskip[...] = r.gskip[...] + skip[0:8, :] + skip[8:16, :] + skip[16:24, :] + skip[24:32, :]
+
+    loop(0, ROWS // 32, gate_back)
 
     def incoming(j):
         at = at_tile(j)
@@ -1389,7 +1392,7 @@
         grad = grad * (sig * (1.0 + pre * (1.0 - sig)))
         taps = []
         for k in range(KC):
-            kept = grad if k == KC - 1 else grad * r.same[k, 8 : 8 + ROWS, :]
+            kept = grad if k == KC - 1 else grad * r.same[k]
             r.dpre[k, 8 : 8 + ROWS, :] = kept
             taps.append(jnp.sum(kept * r.proj[13 + k : 13 + k + ROWS, at], axis=0, keepdims=True))
         taps += [jnp.sum(grad, axis=0, keepdims=True), jnp.zeros((3, TILE), f32)]

time: 134 us -> 126 us (0.940); the launches traced: 133 us -> 126 us
  Pallas kernels: 131 us -> 124 us
    pallas_call x1, Pallas kernels: 128 us -> 121 us  [block(): pl.pallas_call(functools.partial(block_kernel, planes, list(named)), out_...]
where the time goes in v5:
time: 126 us
  Pallas kernels  124 us (98%)
    pallas_call x1, Pallas kernels, block(): pl.pallas_call(functools.partial(block_kernel, planes, list(named)), out_...  121 us
    pallas_call x1, Pallas kernels, deliver(): pl.pallas_call(deliver_kernel, out_shape=[jax.ShapeDtypeStruct(*s) for s...  2.67 us

profile of v5, /device:TPU:0, one launch (start us, length us, event | category | flops | bytes accessed | tf_op | source)
XLA Modules:
  0.0 126.1 jit_solution(1462566895616643800)
XLA Ops:
  0.6 0.0 copy-start.6
  0.7 0.0 copy-start.2
  0.7 0.0 copy-start.3
  0.7 0.0 copy-start.4
  0.7 0.0 copy-start.5
  0.7 0.0 copy-start
  0.7 0.0 copy-start.1
  0.7 0.6 copy-done.6
  1.3 0.0 copy-done.2
  1.3 0.0 copy-done.3
  1.3 0.0 copy-done.4
  1.3 0.0 copy-done.5
  1.4 0.0 copy-done
  1.4 0.0 copy-done.1
  1.4 0.6 pad_add_fusion.refs_3_
  2.0 121.3 %shard_map.203 = (bf16[2,128,768]{2,1,0:T(8,128)(2,1)}, bf16[2,128,768]{2,1,0:T(8,128)(2,1)}, f32[2,48,1024]{2,1,0:T(8,128)}, f32[48,1536]{1,0:T(8,128)}, f32[96,768]{1,0:T(8,128)}, /*index=5*/f32[8,128]{1,0:T(8,128)}) custom-call(bf16[2,128,768]{2,1,0:T(8,128)(2,1)} %bitcast.21, bf16[2,128,768]{2,1,0:T(8,128)(2,1)} %bitcast.22, s32[2,128]{1,0:T(2,128)} %bitcast.23, ...), custom_call_target="tpu_custom_call" | custom-call | tf_op jit(solution)/shard_map/pallas_call | solution.py:1580
  123.3 2.7 %shard_map.204 = (bf16[2,128,768]{2,1,0:T(8,128)(2,1)}, bf16[2,128,768]{2,1,0:T(8,128)(2,1)}, f32[1,48]{1,0:T(1,128)}, f32[48,3352]{1,0:T(8,128)}, f32[4,112]{1,...) custom-call(bf16[2,128,768]{2,1,0:T(8,128)(2,1)} %get-tuple-element., ...), custom_call_target="tpu_custom_call" | custom-call | tf_op jit(solution)/shard_map/pallas_call | solution.py:1615
Async XLA Ops:
  0.6 0.7 copy-start.6
  0.7 0.7 copy-start.2
  0.7 0.7 copy-start.3
  0.7 0.7 copy-start.4
  0.7 0.7 copy-start.5
  0.7 0.7 copy-start
  0.7 0.7 copy-start.1

commit v6 on v5

--- a/solution.py
+++ b/solution.py
@@ -930,7 +930,7 @@
 
 def loop(low_end, high_end, act):
     count = high_end - low_end
-    width = next(w for w in (4, 3, 2, 1) if count % w == 0)
+    width = next(w for w in (6, 4, 3, 2, 1) if count % w == 0)
 
     def several(k, carry):
         for i in range(width):

time: 126 us -> 126 us (level)
  no operation moved by 1% of the time
where the time goes in v6:
time: 126 us; the launch traced here: 125 us
  Pallas kernels  123 us (98%)
    pallas_call x1, Pallas kernels, block(): pl.pallas_call(functools.partial(block_kernel, planes, list(named)), out_...  121 us
    pallas_call x1, Pallas kernels, deliver(): pl.pallas_call(deliver_kernel, out_shape=[jax.ShapeDtypeStruct(*s) for s...  2.67 us

profile of v6, /device:TPU:0, one launch (start us, length us, event | category | flops | bytes accessed | tf_op | source)
XLA Modules:
  0.0 125.5 jit_solution(2417224230348424875)
XLA Ops:
  0.6 0.0 copy-start.6
  0.7 0.0 copy-start.2
  0.7 0.0 copy-start.3
  0.7 0.0 copy-start.4
  0.7 0.0 copy-start.5
  0.7 0.0 copy-start
  0.7 0.0 copy-start.1
  0.7 0.6 copy-done.6
  1.3 0.0 copy-done.2
  1.3 0.0 copy-done.3
  1.3 0.0 copy-done.4
  1.3 0.0 copy-done.5
  1.4 0.0 copy-done
  1.4 0.0 copy-done.1
  1.4 0.6 pad_add_fusion.refs_3_
  2.0 120.7 %shard_map.203 = (bf16[2,128,768]{2,1,0:T(8,128)(2,1)}, bf16[2,128,768]{2,1,0:T(8,128)(2,1)}, f32[2,48,1024]{2,1,0:T(8,128)}, f32[48,1536]{1,0:T(8,128)}, f32[96,768]{1,0:T(8,128)}, /*index=5*/f32[8,128]{1,0:T(8,128)}) custom-call(bf16[2,128,768]{2,1,0:T(8,128)(2,1)} %bitcast.21, bf16[2,128,768]{2,1,0:T(8,128)(2,1)} %bitcast.22, s32[2,128]{1,0:T(2,128)} %bitcast.23, ...), custom_call_target="tpu_custom_call" | custom-call | tf_op jit(solution)/shard_map/pallas_call | solution.py:1580
  122.7 2.7 %shard_map.204 = (bf16[2,128,768]{2,1,0:T(8,128)(2,1)}, bf16[2,128,768]{2,1,0:T(8,128)(2,1)}, f32[1,48]{1,0:T(1,128)}, f32[48,3352]{1,0:T(8,128)}, f32[4,112]{1,...) custom-call(bf16[2,128,768]{2,1,0:T(8,128)(2,1)} %get-tuple-element., ...), custom_call_target="tpu_custom_call" | custom-call | tf_op jit(solution)/shard_map/pallas_call | solution.py:1615
Async XLA Ops:
  0.6 0.7 copy-start.6
  0.7 0.7 copy-start.2
  0.7 0.7 copy-start.3
  0.7 0.7 copy-start.4
  0.7 0.7 copy-start.5
  0.7 0.7 copy-start
  0.7 0.7 copy-start.1
